TPU v7x, 32 devices: a whole 2x2x4 slice. The times are simulated.
32 devices in a mesh: pano: 2 (over y), seq: 4 (over z), win: 4 (over x, core).
Axes of the slice: x: 2, y: 2, z: 4, core: 2. Of those that a mesh axis runs over, the one named last changes fastest.
Arguments:
- query: bfloat16 [8, 768, 1536], P(('pano', 'win'), 'seq'), parts along dimension 0, may hold values from -8 to 8
- key_image: bfloat16 [8, 768, 1536], P(('pano', 'win'), 'seq'), parts along dimension 0, may hold values from -8 to 8
- value_image: bfloat16 [8, 768, 1536], P(('pano', 'win'), 'seq'), parts along dimension 0, may hold values from -6 to 6
- key_text: bfloat16 [8, 64, 1536], P(('pano', 'win'), 'seq'), parts along dimension 0, may hold values from -6 to 6
- value_text: bfloat16 [8, 64, 1536], P(('pano', 'win'), 'seq'), parts along dimension 0, may hold values from -6 to 6
- prompt_ids: int32 [8, 64], P(('pano', 'win')), parts along dimension 0, may hold values from 0 to 32127, as said below
- blend: int32 [8, 768], P(('pano', 'win'), 'seq'), parts along dimension 0, may hold values from 1 to 15, as said below
- w_out: bfloat16 [1536, 3072], replicated, may hold values from -0.15625 to 0.15625
Outputs:
- joined: bfloat16 [8, 768, 3072], P(('pano', 'win'), 'seq'), parts along dimension 0
There are 2 independent parts, one for each index of `pano`. A program takes and returns all parts, laid end to end along the dimension named above; an argument that names none is the same for every part. Nothing has to cross between parts.
Inputs may be any that keep to these rules, and one draw needn't show every extreme that they name: `prompt_ids`: in each window the nonzero ids form a leading run of 16 or more positions and the rest are 0. At row r and column c < 32, blend[w] plus blend[w - 1] at row r, column c + 32 equals 16, window numbers taken modulo 4.
All inputs are finite; a program needn't handle non-finite values.
Results may differ from a plain program's by a relative error of at most 0.0085.
Values may be sent and summed in bfloat16 or wider, within the bound.
No kernel may reach another device: no remote copies, remote signals or barrier semaphores. Data moves between devices by JAX's collectives and lax.ppermute only.
A program may use at most 64 MiB of HBM per device.

v0:
```python
import jax
import jax.numpy as jnp
from jax import lax
from jax.sharding import PartitionSpec as P

HEADS = 12
HEAD_DIM = 128
WCOLS = 64
ROWS_DEV = 3
STRIDE = 32


blend_total = 16.0


def swapped(block, axis, stride):
    count = lax.axis_size(axis)
    route = []
    for low in range(count):
        high = low | 1 << stride
        if high != low and high < count:
            route += [(low, high), (high, low)]
    return lax.ppermute(block, axis, route)


def shifted(block, axis, distance):
    devices = range(lax.axis_size(axis))
    route = [((i - distance) % len(devices), i) for i in devices]
    return lax.ppermute(block, axis, route)


def regroup(stacked, bit_count):
    row_count = stacked.shape[0]
    carried = stacked.reshape(row_count, 1 << bit_count, -1)
    position = lax.axis_index("seq")
    for bit_index in range(bit_count):
        own_bit = position >> bit_index & 1
        paired = carried.reshape(carried.shape[0], carried.shape[1] // 2, 2, carried.shape[2])
        kept_half = lax.dynamic_index_in_dim(paired, own_bit, 2, keepdims=False)
        sent_half = lax.dynamic_index_in_dim(paired, 1 - own_bit, 2, keepdims=False)
        received = swapped(sent_half, "seq", bit_index)
        lower_half = jnp.where(own_bit == 0, kept_half, received)
        upper_half = jnp.where(own_bit == 0, received, kept_half)
        carried = jnp.concatenate([lower_half, upper_half], axis=0)
    return carried.reshape(carried.shape[0], -1)


def ungroup(attended, bit_count):
    carried = attended.reshape(attended.shape[0], 1, attended.shape[1])
    position = lax.axis_index("seq")
    for bit_index in reversed(range(bit_count)):
        own_bit = position >> bit_index & 1
        halves = carried.reshape(2, carried.shape[0] // 2, carried.shape[1], carried.shape[2])
        kept_half = lax.dynamic_index_in_dim(halves, own_bit, 0, keepdims=False)
        sent_half = lax.dynamic_index_in_dim(halves, 1 - own_bit, 0, keepdims=False)
        received = swapped(sent_half, "seq", bit_index)
        lower_half = jnp.where(own_bit == 0, kept_half, received)
        upper_half = jnp.where(own_bit == 0, received, kept_half)
        stacked = jnp.stack([lower_half, upper_half], axis=2)
        carried = stacked.reshape(kept_half.shape[0], -1, kept_half.shape[2])
    return carried.reshape(carried.shape[0], -1)


def absorb(carried, key_value, valid_keys, queries, head_count):
    running, denominator, numerator = carried
    keys_block = key_value[0].reshape(key_value.shape[1], head_count, HEAD_DIM)
    values_block = key_value[1].reshape(key_value.shape[1], head_count, HEAD_DIM)
    scores = jnp.einsum(
        "qhd,khd->qhk", queries, keys_block, preferred_element_type=jnp.float32
    ) * HEAD_DIM ** (-0.5)
    scores = jnp.where(valid_keys[None, None, :], scores, -jnp.inf)
    updated = jnp.maximum(running, jnp.max(scores, axis=2))
    rescale = jnp.exp(running - updated)
    weights = jnp.exp(scores - updated[:, :, None])
    denominator = denominator * rescale + jnp.sum(weights, axis=2)
    product = jnp.einsum(
        "qhk,khd->qhd",
        weights.astype(jnp.bfloat16),
        values_block,
        preferred_element_type=jnp.float32,
    )
    numerator = numerator * rescale[:, :, None] + product
    return (updated, denominator, numerator)


def pass_strips(window_rows):
    from_prev = shifted(window_rows[:, STRIDE:], "win", 1)
    from_next = shifted(window_rows[:, :STRIDE], "win", -1)
    return (from_prev, from_next)


def project_rows(features, w_out):
    flat_rows = features.reshape(-1, features.shape[-1])
    result = jnp.dot(flat_rows, w_out, preferred_element_type=jnp.float32).astype(jnp.bfloat16)
    return result.reshape(ROWS_DEV, -1, w_out.shape[1])


def on_device(query, key_image, value_image, key_text, value_text, prompt_ids, blend, w_out):
    bit_count = 2
    group_size = 1 << bit_count
    image_rows = query.shape[1]
    text_rows = key_text.shape[1]
    key_rows = image_rows + text_rows
    head_count = HEADS // group_size
    stacked = jnp.concatenate(
        [query[0], key_image[0], key_text[0], value_image[0], value_text[0]], axis=0
    )
    grouped = regroup(stacked, bit_count).reshape(group_size, image_rows + 2 * key_rows, -1)
    queries = grouped[:, :image_rows].reshape(group_size * image_rows, head_count, HEAD_DIM)
    keys_grouped = grouped[:, image_rows : image_rows + key_rows].reshape(group_size * key_rows, -1)
    values_grouped = grouped[:, image_rows + key_rows :].reshape(group_size * key_rows, -1)
    key_value = jnp.stack([keys_grouped, values_grouped])
    seq_count = lax.axis_size("seq")
    text_valid = prompt_ids[0].reshape(seq_count, text_rows) != 0
    key_valid = jnp.concatenate([jnp.ones((seq_count, image_rows), jnp.bool_), text_valid], axis=1)
    group_count = seq_count // group_size
    own_group = lax.axis_index("seq") // group_size

    def valid_for(source):
        return lax.dynamic_slice_in_dim(key_valid, source * group_size, group_size, 0).reshape(-1)

    query_count = group_size * image_rows
    initial = (
        jnp.full((query_count, head_count), -jnp.inf, jnp.float32),
        jnp.zeros((query_count, head_count), jnp.float32),
        jnp.zeros((query_count, head_count, HEAD_DIM), jnp.float32),
    )
    carried = absorb(initial, key_value, valid_for(own_group), queries, head_count)

    def one_turn(turn_index, loop_state):
        current, moving = loop_state
        moving = shifted(moving, "seq", group_size)
        source = (own_group - turn_index) % group_count
        return (absorb(current, moving, valid_for(source), queries, head_count), moving)

    carried, key_value = lax.fori_loop(1, group_count, one_turn, (carried, key_value))
    running, denominator, numerator = carried
    attended = (numerator / denominator[:, :, None]).astype(jnp.bfloat16).reshape(query_count, -1)
    attended = ungroup(attended, bit_count)
    got_prev, got_next = pass_strips(attended.reshape(ROWS_DEV, WCOLS, -1))
    projected = project_rows(attended, w_out)
    from_prev = project_rows(got_prev, w_out)
    from_next = project_rows(got_next, w_out)
    weight_own = blend[0].reshape(ROWS_DEV, WCOLS, 1).astype(jnp.float32)
    partner = jnp.concatenate([from_prev, from_next], axis=1).astype(jnp.float32)
    joined = (
        weight_own * projected.astype(jnp.float32) + (blend_total - weight_own) * partner
    ) / blend_total
    return joined.astype(jnp.bfloat16).reshape(1, -1, joined.shape[-1])


def solution(mesh):
    placed = (
        P(("pano", "win"), "seq", None),
        P(("pano", "win"), "seq", None),
        P(("pano", "win"), "seq", None),
        P(("pano", "win"), "seq", None),
        P(("pano", "win"), "seq", None),
        P(("pano", "win"), None),
        P(("pano", "win"), "seq"),
        P(),
    )
    return jax.shard_map(
        on_device,
        mesh=mesh,
        in_specs=placed,
        out_specs=P(("pano", "win"), "seq", None),
        check_vma=False,
    )
```

profile of v0, /device:TPU:1, one launch (start us, length us, event | category | flops | bytes accessed | tf_op | source)
XLA Modules:
  0.0 136.2 jit_solution(3077362369434255031)
XLA Ops:
  0.0 1.9 %concatenate.28 = bf16[192,2,2,384]{3,2,1,0:T(2,128)(2,1)S(1)} reshape(bf16[1,192,1536]{2,1,0:T(8,128)(2,1)} %param.8) | data formatting | bytes 1179648 | tf_op jit(solution)/shard_map/concatenate | solution.py:105
  2.0 0.4 constant_dynamic-update-slice_fusion.4
  2.4 1.9 %concatenate.29 = bf16[192,2,2,384]{3,2,1,0:T(2,128)(2,1)S(1)} reshape(bf16[1,192,1536]{2,1,0:T(8,128)(2,1)} %param.9) | data formatting | bytes 1179648 | tf_op jit(solution)/shard_map/concatenate | solution.py:105
  4.4 1.9 %concatenate.31 = bf16[192,2,2,384]{3,2,1,0:T(2,128)(2,1)S(1)} reshape(bf16[1,192,1536]{2,1,0:T(8,128)(2,1)} %param.10) | data formatting | bytes 1179648 | tf_op jit(solution)/shard_map/concatenate | solution.py:105
  6.4 0.5 constant_dynamic-update-slice_fusion.3
  7.0 0.5 constant_dynamic-update-slice_fusion.1
  7.6 5.1 %constant_dynamic-slice_fusion.3 = (bf16[608,2,1,384]{3,2,1,0:T(2,128)(2,1)}, bf16[608,2,1,384]{3,2,1,0:T(2,128)(2,1)S(1)}) fusion(bf16[608,2,2,384]{3,2,1,0:T(2,128)(2,1)S(1)} %constant_dynamic-update-slice_fusion, s32[]{:T(128)S(6)} %select_n.83, s32[]{:T(128)S(6)} %select_n.84), kind=kLoop, calls=%fused_computation.60 | loop fusion | bytes 3735560 | tf_op jit(solution)/shard_map/jit(dynamic_index_in_dim)/dynamic_slice | solution.py:39
  12.7 0.1 copy.52
  12.8 2.2 %collective-permute-start = (bf16[608,2,384]{2,0,1:T(8,128)(2,1)S(1)}, bf16[608,2,384]{2,0,1:T(8,128)(2,1)S(1)}, u32[]{:S(2)}, u32[]{:S(2)}) collective-permute-start(bf16[608,2,384]{2,0,1:T(8,128)(2,1)S(1)} %bitcast.75), channel_id=1, source_target_pairs={{0,4},{4,0},{8,12},{12,8},{1,5},{5,1},{9,13},{13,9},{2,6},{6,2},{1... | collective-permute-start | bytes 2801672 | tf_op jit(solution)/shard_map/ppermute | solution.py:23
  15.0 20.4 %collective-permute-done = bf16[608,2,384]{2,0,1:T(8,128)(2,1)S(1)} collective-permute-done((bf16[608,2,384]{2,0,1:T(8,128)(2,1)S(1)}, bf16[608,2,384]{2,0,1:T(8,128)(2,1)S(1)}, u32[]{:S(2)}, u32[]{:S(2)}) %collective-permute-start) | collective-permute-done | bytes 933920 | tf_op jit(solution)/shard_map/ppermute | solution.py:23
  35.5 1.8 %bitcast_select_fusion = (bf16[608,2,384]{2,0,1:T(8,128)(2,1)S(1)}, bf16[608,2,384]{2,0,1:T(8,128)(2,1)S(1)}) fusion(bf16[608,2,384]{2,0,1:T(8,128)(2,1)S(1)} %collective-permute-done, pred[]{:T(512)S(6)} %eq.4, bf16[608,2,1,384]{3,2,1,0:T(2,128)(2,1)} %get-tuple-element.11), kind=kLoop, calls=%fused_computation.29 | loop fusion | flops 933888 | bytes 3735553 | tf_op jit(solution)/shard_map/jit(_where)/select_n | solution.py:43
  37.2 1.0 fusion.18
  38.3 2.2 %collective-permute-start.1 = (bf16[1216,1,384]{2,0,1:T(8,128)(2,1)}, bf16[1216,1,384]{2,0,1:T(8,128)(2,1)S(1)}, u32[]{:S(2)}, u32[]{:S(2)}) collective-permute-start(bf16[1216,1,384]{2,0,1:T(8,128)(2,1)} %fusion.18), channel_id=1, source_target_pairs={{0,8},{8,0},{4,12},{12,4},{1,9},{9,1},{5,13},{13,5},{2,10},{10,2},... | collective-permute-start | bytes 2801672 | tf_op jit(solution)/shard_map/ppermute | solution.py:23
  40.5 0.1 ne.15
  40.5 0.1 concatenate.27
  40.6 0.1 broadcast_in_dim.26
  40.7 40.4 %collective-permute-done.1 = bf16[1216,1,384]{2,0,1:T(8,128)(2,1)S(1)} collective-permute-done((bf16[1216,1,384]{2,0,1:T(8,128)(2,1)}, bf16[1216,1,384]{2,0,1:T(8,128)(2,1)S(1)}, u32[]{:S(2)}, u32[]{:S(2)}) %collective-permute-start.1) | collective-permute-done | bytes 933920 | tf_op jit(solution)/shard_map/ppermute | solution.py:23
  81.1 0.4 broadcast_select_fusion.1
  81.5 0.2 pad_maximum_fusion
  81.7 0.1 fusion.33
  81.8 0.1 slice.21
  81.9 0.2 reshape.85
  82.1 0.2 reshape.79
  82.3 1.3 bitcast_reduce_fusion
  83.7 2.2 %fusion.1 = f32[768,3]{0,1:T(4,128)S(1)} fusion(f32[3,832,768]{2,1,0:T(8,128)S(1)} %get-tuple-element.24, f32[768,3]{0,1:T(4,128)S(1)} %get-tuple-element.23, pred[832]{0:T(1024)(128)(4,1)S(1)} %broadcast_in_dim.26), kind=kLoop, calls=%fused_computation.4 | loop fusion | flops 7665408 | bytes 7686976 | tf_op jit(solution)/shard_map/reduce_sum | solution.py:75
  85.9 0.8 copy-done
  86.7 0.2 reshape.86
  86.9 5.1 %divide_convert_fusion = bf16[768,3,128]{0,2,1:T(8,128)(2,1)S(1)} fusion(f32[3,832,768]{2,1,0:T(8,128)} %copy-done, f32[768,3]{0,1:T(4,128)S(1)} %get-tuple-element.23, pred[832]{0:T(1024)(128)(4,1)S(1)} %broadcast_in_dim.26, bf16[832,3,128]{2,1,0:T(4,128)(2,1)S(1)} %reshape.86, f32[768,3]{0,1:T(4,128)S(1)} %get-tuple-element.22, ...), kind=kOutput, calls=%fused_computation.26 | convolution fusion | flops 499286016 | bytes 8924992 | tf_op jit(solution)/shard_map/qhk,khd->qhd/dot_general | solution.py:76
  92.1 0.1 reshape_reshape_reshape.6
  92.2 1.2 constant_dynamic-slice_fusion.1
  93.4 0.9 copy.38
  94.3 0.1 collective-permute-start.2
  94.4 0.9 copy.37
  95.2 13.6 %collective-permute-done.2 = bf16[384,1,384]{2,0,1:T(8,128)(2,1)S(1)} collective-permute-done((bf16[384,1,384]{2,0,1:T(8,128)(2,1)S(1)}, bf16[384,1,384]{2,0,1:T(8,128)(2,1)S(1)}, u32[]{:S(2)}, u32[]{:S(2)}) %collective-permute-start.2) | collective-permute-done | bytes 294944 | tf_op jit(solution)/shard_map/ppermute | solution.py:23
  108.9 0.1 collective-permute-start.3
  109.0 6.3 %collective-permute-done.3 = bf16[192,2,384]{2,0,1:T(8,128)(2,1)S(1)} collective-permute-done((bf16[192,2,384]{2,0,1:T(8,128)(2,1)S(1)}, bf16[192,2,384]{2,0,1:T(8,128)(2,1)S(1)}, u32[]{:S(2)}, u32[]{:S(2)}) %collective-permute-start.3) | collective-permute-done | bytes 294944 | tf_op jit(solution)/shard_map/ppermute | solution.py:23
  115.3 0.1 select_bitcast_fusion.1
  115.3 0.1 pad_maximum_fusion.2
  115.4 0.6 copy.27
  116.0 0.4 reshape_reshape_reshape.7
  116.5 3.7 %collective-permute-start.4 = (bf16[3,32,1536]{2,1,0:T(8,128)(2,1)S(1)}, bf16[3,32,1536]{2,1,0:T(8,128)(2,1)S(1)}, u32[]{:S(2)}, u32[]{:S(2)}) collective-permute-start(bf16[3,32,1536]{2,1,0:T(8,128)(2,1)S(1)} %get-tuple-element.15), channel_id=1, source_target_pairs={{3,0},{0,1},{1,2},{2,3},{7,4},{4,5},{5,6},{6,7},{11,8},{8,9},{9,10... | collective-permute-start | bytes 884744 | tf_op jit(solution)/shard_map/ppermute | solution.py:29
  120.2 0.4 reshape_reshape.9
  120.6 4.4 %collective-permute-done.4 = bf16[3,32,1536]{2,1,0:T(8,128)(2,1)S(1)} collective-permute-done((bf16[3,32,1536]{2,1,0:T(8,128)(2,1)S(1)}, bf16[3,32,1536]{2,1,0:T(8,128)(2,1)S(1)}, u32[]{:S(2)}, u32[]{:S(2)}) %collective-permute-start.4) | collective-permute-done | bytes 294944 | tf_op jit(solution)/shard_map/ppermute | solution.py:29
  125.1 5.4 %convolution_convert_fusion.2 = bf16[96,3072]{1,0:T(8,128)(2,1)S(1)} fusion(bf16[96,1536]{1,0:T(8,128)(2,1)S(1)} %bitcast.76, bf16[1536,3072]{1,0:T(8,128)(2,1)} %param.15), kind=kOutput, calls=%fused_computation.16 | convolution fusion | flops 906264576 | bytes 10321920 | tf_op jit(solution)/shard_map/dot_general | solution.py:94
  130.5 0.7 slice-done.2
  131.2 1.7 %convolution_convert_fusion.1 = bf16[96,3072]{1,0:T(8,128)(2,1)S(1)} fusion(bf16[96,1536]{1,0:T(8,128)(2,1)S(1)} %bitcast.77, bf16[1536,3072]{1,0:T(8,128)(2,1)S(1)} %bitcast.65), kind=kOutput, calls=%fused_computation.15 | convolution fusion | flops 906264576 | bytes 10321920 | tf_op jit(solution)/shard_map/dot_general | solution.py:94
  132.9 0.1 pad_maximum_fusion.1
  133.0 3.2 %fusion.11 = bf16[1,192,3072]{2,1,0:T(8,128)(2,1)} fusion(bf16[192,1536]{1,0:T(8,128)(2,1)S(1)} %reshape_reshape.9, bf16[1536,3072]{1,0:T(8,128)(2,1)S(1)} %bitcast.65, bf16[192,3072]{1,0:T(8,128)(2,1)S(1)} %bitcast.74, f32[192]{0:T(256)S(1)} %broadcast_subtract_fusion, f32[192]{0:T(256)S(1)} %bitcast.80), kind=kOutput, calls=%fused_computation.14 | convolution fusion | flops 1816657920 | bytes 12387840 | tf_op jit(solution)/shard_map/dot_general | solution.py:94
  (28 shorter events, 0.4 us)
Async XLA Ops:
  0.0 4.3 %copy-start.1 = (bf16[1,16,1536]{2,1,0:T(8,128)(2,1)S(1)}, bf16[1,16,1536]{2,1,0:T(8,128)(2,1)}, u32[]{:S(2)}) copy-start(bf16[1,16,1536]{2,1,0:T(8,128)(2,1)} %param.11) | copy-start | bytes 147460
  2.0 4.4 %copy-start.2 = (bf16[1,16,1536]{2,1,0:T(8,128)(2,1)S(1)}, bf16[1,16,1536]{2,1,0:T(8,128)(2,1)}, u32[]{:S(2)}) copy-start(bf16[1,16,1536]{2,1,0:T(8,128)(2,1)} %param.12) | copy-start | bytes 147460
  12.8 22.6 %collective-permute-start = (bf16[608,2,384]{2,0,1:T(8,128)(2,1)S(1)}, bf16[608,2,384]{2,0,1:T(8,128)(2,1)S(1)}, u32[]{:S(2)}, u32[]{:S(2)}) collective-permute-start(bf16[608,2,384]{2,0,1:T(8,128)(2,1)S(1)} %bitcast.75), channel_id=1, source_target_pairs={{0,4},{4,0},{8,12},{12,8},{1,5},{5,1},{9,13},{13,9},{2,6},{6,2},{1... | collective-permute-start | bytes 2801672 | tf_op jit(solution)/shard_map/ppermute | solution.py:23
  37.2 3.2 %copy-start.4 = (s32[1,64]{1,0:T(1,128)S(1)}, s32[1,64]{1,0:T(1,128)}, u32[]{:S(2)}) copy-start(s32[1,64]{1,0:T(1,128)} %param.13) | copy-start | bytes 772
  38.3 42.8 %collective-permute-start.1 = (bf16[1216,1,384]{2,0,1:T(8,128)(2,1)}, bf16[1216,1,384]{2,0,1:T(8,128)(2,1)S(1)}, u32[]{:S(2)}, u32[]{:S(2)}) collective-permute-start(bf16[1216,1,384]{2,0,1:T(8,128)(2,1)} %fusion.18), channel_id=1, source_target_pairs={{0,8},{8,0},{4,12},{12,4},{1,9},{9,1},{5,13},{13,5},{2,10},{10,2},... | collective-permute-start | bytes 2801672 | tf_op jit(solution)/shard_map/ppermute | solution.py:23
  83.7 3.0 %copy-start = (f32[3,832,768]{2,1,0:T(8,128)}, f32[3,832,768]{2,1,0:T(8,128)S(1)}, u32[]{:S(2)}) copy-start(f32[3,832,768]{2,1,0:T(8,128)S(1)} %get-tuple-element.24) | copy-start | bytes 23003140
  94.3 14.5 %collective-permute-start.2 = (bf16[384,1,384]{2,0,1:T(8,128)(2,1)S(1)}, bf16[384,1,384]{2,0,1:T(8,128)(2,1)S(1)}, u32[]{:S(2)}, u32[]{:S(2)}) collective-permute-start(bf16[384,1,384]{2,0,1:T(8,128)(2,1)S(1)} %bitcast.78), channel_id=1, source_target_pairs={{0,8},{8,0},{4,12},{12,4},{1,9},{9,1},{5,13},{13,5},{2,10},{10,2},... | collective-permute-start | bytes 884744 | tf_op jit(solution)/shard_map/ppermute | solution.py:23
  108.9 6.4 %collective-permute-start.3 = (bf16[192,2,384]{2,0,1:T(8,128)(2,1)S(1)}, bf16[192,2,384]{2,0,1:T(8,128)(2,1)S(1)}, u32[]{:S(2)}, u32[]{:S(2)}) collective-permute-start(bf16[192,2,384]{2,0,1:T(8,128)(2,1)S(1)} %fusion.27), channel_id=1, source_target_pairs={{0,4},{4,0},{8,12},{12,8},{1,5},{5,1},{9,13},{13,9},{2,6},{6,2},{1... | collective-permute-start | bytes 884744 | tf_op jit(solution)/shard_map/ppermute | solution.py:23
  115.4 4.8 %copy-start.3 = (s32[1,192]{1,0:T(1,128)S(1)}, s32[1,192]{1,0:T(1,128)}, u32[]{:S(2)}) copy-start(s32[1,192]{1,0:T(1,128)} %param.14) | copy-start | bytes 2308
  116.5 8.6 %collective-permute-start.4 = (bf16[3,32,1536]{2,1,0:T(8,128)(2,1)S(1)}, bf16[3,32,1536]{2,1,0:T(8,128)(2,1)S(1)}, u32[]{:S(2)}, u32[]{:S(2)}) collective-permute-start(bf16[3,32,1536]{2,1,0:T(8,128)(2,1)S(1)} %get-tuple-element.15), channel_id=1, source_target_pairs={{3,0},{0,1},{1,2},{2,3},{7,4},{4,5},{5,6},{6,7},{11,8},{8,9},{9,10... | collective-permute-start | bytes 884744 | tf_op jit(solution)/shard_map/ppermute | solution.py:29
  120.2 10.3 %slice-start = ((s8[9437184]{0:T(1024)(128)(4,1)}), s8[1048576]{0:T(1024)(128)(4,1)S(1)}, s32[]{:S(2)}) async-start(s8[9437184]{0:T(1024)(128)(4,1)} %bitcast.64), calls=%async_computation | async-start | bytes 2097152
  120.6 9.9 %collective-permute-start.5 = (bf16[3,32,1536]{2,1,0:T(8,128)(2,1)S(1)}, bf16[3,32,1536]{2,1,0:T(8,128)(2,1)S(1)}, u32[]{:S(2)}, u32[]{:S(2)}) collective-permute-start(bf16[3,32,1536]{2,1,0:T(8,128)(2,1)S(1)} %get-tuple-element.16), channel_id=1, source_target_pairs={{1,0},{2,1},{3,2},{0,3},{5,4},{6,5},{7,6},{4,7},{9,8},{10,9},{11,1... | collective-permute-start | bytes 884744 | tf_op jit(solution)/shard_map/ppermute | solution.py:29
  125.1 5.5 %slice-start.1 = ((s8[9437184]{0:T(1024)(128)(4,1)}), s8[4194304]{0:T(1024)(128)(4,1)S(1)}, s32[]{:S(2)}) async-start(s8[9437184]{0:T(1024)(128)(4,1)} %bitcast.64), calls=%async_computation.1 | async-start | bytes 8388608
  125.1 6.1 %slice-start.2 = ((s8[9437184]{0:T(1024)(128)(4,1)}), s8[4194304]{0:T(1024)(128)(4,1)S(1)}, s32[]{:S(2)}) async-start(s8[9437184]{0:T(1024)(128)(4,1)} %bitcast.64), calls=%async_computation.2 | async-start | bytes 8388608
where the time goes:
time: 139 us; the launch traced here: 136 us
  waiting for transfers between devices  85.1 us (61%)
  local copies, waits for them, and re-layouts  19.8 us (14%)
  matrix products  16.8 us (12%)
  starting transfers between devices  8.24 us (6%)
  other arithmetic  5.97 us (4%)
    ppermute x4, waiting for transfers between devices, swapped(): return lax.ppermute(block, axis, route)  80.6 us
    dot_general x3, matrix products, project_rows(): jnp.dot(flat_rows, w_out, preferred_element_type=jnp.float32)  10.3 us
    concatenate x6, local copies, waits for them, and re-layouts, on_device(): jnp.concatenate([query[0], key_image[0], key_text[0], value_image[0], val...  5.93 us
    dot_general x1, matrix products, absorb(): jnp.einsum('qhk,khd->qhd', weights.astype(jnp.bfloat16), values_block, pr...  5.15 us
    dynamic_slice x1, local copies, waits for them, and re-layouts, regroup(): kept_half = lax.dynamic_index_in_dim(paired, own_bit, 2, keepdims=False)  5.11 us
    unnamed x22, local copies, waits for them, and re-layouts  4.71 us
    ppermute x4, starting transfers between devices, swapped(): return lax.ppermute(block, axis, route)  4.49 us
    ppermute x2, waiting for transfers between devices, shifted(): return lax.ppermute(block, axis, route)  4.43 us
  transfers between devices with their start and end apart: 6, of which 5 were waited for; matrix products, arithmetic and copies ran while one was open for 5% of the time, Pallas kernels for 0%

commit v1 on v0

v1 whole, which is shorter than its diff:
```python
import functools
import math

import jax
import jax.numpy as jnp
from jax import lax
from jax.experimental import pallas as pl
from jax.experimental.pallas import tpu as pltpu
from jax.sharding import PartitionSpec as P

HEADS = 12
HEAD_DIM = 128
WCOLS = 64
STRIDE = 32
BLEND_TOTAL = 16.0
SCALE = HEAD_DIM ** (-0.5)
EXP2_SCALE = SCALE * math.log2(math.e)
VMEM_LIMIT = 24 * 1024 * 1024

ANY = pl.BlockSpec(memory_space=pl.ANY)
VMEM = pl.BlockSpec(memory_space=pltpu.VMEM)


def shifted(block, axis, distance, group):
    count = lax.axis_size(axis)
    route = []
    for i in range(count):
        base = i // group * group
        route.append((i, base + (i % group + distance) % group))
    return lax.ppermute(block, axis, route)


def pack_kernel(chunk, group, head_count, *refs):
    sources, packed, sems = refs[:5], refs[5 : 5 + group], refs[5 + group]
    position = lax.rem(lax.axis_index("seq"), group)
    copies = []
    for distance in range(group):
        head = lax.rem(position + distance, group) * head_count + chunk
        columns = pl.ds(pl.multiple_of(head * HEAD_DIM, HEAD_DIM), HEAD_DIM)
        row = 0
        for source in sources:
            rows = source.shape[0]
            copy = pltpu.make_async_copy(
                source.at[:, columns], packed[distance].at[pl.ds(row, rows)], sems.at[len(copies)]
            )
            copy.start()
            copies.append(copy)
            row += rows
    for copy in copies:
        copy.wait()


def pack(sources, chunk, group, head_count):
    rows = sum(source.shape[0] for source in sources)
    return pl.pallas_call(
        functools.partial(pack_kernel, chunk, group, head_count),
        out_shape=[jax.ShapeDtypeStruct((rows, HEAD_DIM), sources[0].dtype)] * group,
        in_specs=[ANY] * len(sources),
        out_specs=[ANY] * group,
        scratch_shapes=[pltpu.SemaphoreType.DMA((group * len(sources),))],
        name="pack",
    )(*sources)


def attend_kernel(group, image_rows, text_rows, ids, *refs):
    blocks, (left, right, keys, values) = refs[:group], refs[group:]
    position = lax.rem(lax.axis_index("seq"), group)
    key_rows = image_rows + text_rows
    for distance in range(group):
        block = blocks[distance]
        source = lax.rem(position - distance + group, group)
        image = pl.ds(distance * image_rows, image_rows)
        text = pl.ds(pl.multiple_of(group * image_rows + source * text_rows, text_rows), text_rows)
        key_at, value_at = image_rows, image_rows + key_rows
        keys[image] = block[key_at : key_at + image_rows]
        keys[text] = block[key_at + image_rows : key_at + key_rows]
        values[image] = block[value_at : value_at + image_rows]
        values[text] = block[value_at + image_rows : value_at + key_rows]
    image_keys = group * image_rows
    valid = ids[...] != 0
    half = left.shape[0] // group
    for distance in range(group):
        scores = lax.dot_general(
            blocks[distance][:image_rows],
            keys[...],
            (((1,), (1,)), ((), ())),
            preferred_element_type=jnp.float32,
        )
        scores = jnp.concatenate(
            [scores[:, :image_keys], jnp.where(valid, scores[:, image_keys:], -jnp.inf)], axis=1
        )
        peak = jnp.max(scores, axis=1, keepdims=True)
        weights = jnp.exp2((scores - peak) * EXP2_SCALE)
        total = jnp.sum(weights, axis=1, keepdims=True)
        result = jnp.dot(
            weights.astype(jnp.bfloat16), values[...], preferred_element_type=jnp.float32
        )
        result = (result / total).astype(jnp.bfloat16)
        for row in range(image_rows // WCOLS):
            at = distance * half + row * STRIDE
            left[at : at + STRIDE] = result[row * WCOLS : row * WCOLS + STRIDE]
            right[at : at + STRIDE] = result[row * WCOLS + STRIDE : (row + 1) * WCOLS]


def attend(blocks, ids, image_rows, text_rows):
    group = len(blocks)
    strip = jax.ShapeDtypeStruct((group * image_rows // 2, HEAD_DIM), jnp.bfloat16)
    keys = pltpu.VMEM((group * (image_rows + text_rows), HEAD_DIM), jnp.bfloat16)
    key_count, query_count = group * (image_rows + text_rows), group * image_rows
    return pl.pallas_call(
        functools.partial(attend_kernel, group, image_rows, text_rows),
        out_shape=[strip, strip],
        in_specs=[VMEM] * (1 + group),
        out_specs=[VMEM, VMEM],
        scratch_shapes=[keys, keys],
        compiler_params=pltpu.CompilerParams(vmem_limit_bytes=VMEM_LIMIT),
        cost_estimate=pl.CostEstimate(
            flops=4 * query_count * key_count * HEAD_DIM,
            bytes_accessed=4 * key_count * HEAD_DIM * 2,
            transcendentals=query_count * key_count,
        ),
        name="attend",
    )(ids, *blocks)


def blend_kernel(group, left, right, from_prev, from_next, weight_left, weight_right, *outs):
    half = left.shape[0] // group
    for own, partner, weight_ref, at in (
        (left, from_prev, weight_left, 0),
        (right, from_next, weight_right, half),
    ):
        for distance in range(group):
            rows = pl.ds(distance * half, half)
            weight = weight_ref[rows]
            mixed = weight * own[rows].astype(jnp.float32) + (BLEND_TOTAL - weight) * partner[
                rows
            ].astype(jnp.float32)
            outs[distance][pl.ds(at, half)] = (mixed * (1.0 / BLEND_TOTAL)).astype(jnp.bfloat16)


def blend_strips(left, right, from_prev, from_next, weight_left, weight_right, group):
    out = jax.ShapeDtypeStruct((2 * left.shape[0] // group, HEAD_DIM), jnp.bfloat16)
    return pl.pallas_call(
        functools.partial(blend_kernel, group),
        out_shape=[out] * group,
        in_specs=[VMEM] * 6,
        out_specs=[VMEM] * group,
        name="blend",
    )(left, right, from_prev, from_next, weight_left, weight_right)


def project_kernel(group, head_count, *refs):
    blocks, (w_out, out, features) = refs[: group * head_count], refs[group * head_count :]
    image_rows = out.shape[0]

    @pl.when(pl.program_id(0) == 0)
    def _():
        position = lax.rem(lax.axis_index("seq"), group)
        for chunk in range(head_count):
            for distance in range(group):
                head = lax.rem(position + distance, group) * head_count + chunk
                columns = pl.ds(pl.multiple_of(head * HEAD_DIM, HEAD_DIM), HEAD_DIM)
                block = blocks[chunk * group + distance]
                for row in range(image_rows // WCOLS):
                    for side in range(2):
                        start = side * image_rows // 2 + row * STRIDE
                        features[pl.ds(row * WCOLS + side * STRIDE, STRIDE), columns] = block[
                            start : start + STRIDE
                        ]

    out[...] = jnp.dot(features[...], w_out[...], preferred_element_type=jnp.float32).astype(
        jnp.bfloat16
    )


def project(blocks, w_out, group, head_count):
    image_rows = blocks[0].shape[0]
    depth, width = w_out.shape
    tile = width // 6
    return pl.pallas_call(
        functools.partial(project_kernel, group, head_count),
        grid=(width // tile,),
        out_shape=jax.ShapeDtypeStruct((image_rows, width), jnp.bfloat16),
        in_specs=[pl.BlockSpec((image_rows, HEAD_DIM), lambda n: (0, 0))] * len(blocks)
        + [pl.BlockSpec((depth, tile), lambda n: (0, n))],
        out_specs=pl.BlockSpec((image_rows, tile), lambda n: (0, n)),
        scratch_shapes=[pltpu.VMEM((image_rows, depth), jnp.bfloat16)],
        compiler_params=pltpu.CompilerParams(vmem_limit_bytes=VMEM_LIMIT),
        cost_estimate=pl.CostEstimate(
            flops=2 * image_rows * depth * width,
            bytes_accessed=2 * (depth * width + image_rows * (depth + width)),
            transcendentals=0,
        ),
        name="project",
    )(*blocks, w_out)


def absorb(carried, keys, values, valid_keys, queries):
    running, denominator, numerator = carried
    scores = jnp.einsum("qhd,khd->qhk", queries, keys, preferred_element_type=jnp.float32) * SCALE
    scores = jnp.where(valid_keys[None, None, :], scores, -jnp.inf)
    updated = jnp.maximum(running, jnp.max(scores, axis=2))
    rescale = jnp.exp(running - updated)
    weights = jnp.exp(scores - updated[:, :, None])
    denominator = denominator * rescale + jnp.sum(weights, axis=2)
    product = jnp.einsum(
        "qhk,khd->qhd", weights.astype(jnp.bfloat16), values, preferred_element_type=jnp.float32
    )
    numerator = numerator * rescale[:, :, None] + product
    return (updated, denominator, numerator)


def attend_ring(blocks, prompt_ids, image_rows, text_rows):
    head_count, group = len(blocks), len(blocks[0])
    key_rows = image_rows + text_rows
    stacked = jnp.stack([jnp.stack(chunk) for chunk in blocks], axis=2)
    queries = stacked[:, :image_rows].reshape(group * image_rows, head_count, HEAD_DIM)
    keys = stacked[:, image_rows : image_rows + key_rows].reshape(-1, head_count, HEAD_DIM)
    values = stacked[:, image_rows + key_rows :].reshape(-1, head_count, HEAD_DIM)
    seq_count = lax.axis_size("seq")
    group_count = seq_count // group
    own_group = lax.axis_index("seq") // group
    order = (lax.axis_index("seq") % group - jnp.arange(group)) % group
    text_valid = prompt_ids.reshape(seq_count, text_rows) != 0

    def valid_for(source):
        text = lax.dynamic_slice_in_dim(text_valid, source * group, group, 0)[order]
        return jnp.concatenate([jnp.ones((group, image_rows), jnp.bool_), text], axis=1).reshape(-1)

    def next_group(block):
        route = [(i, (i + group) % seq_count) for i in range(seq_count)]
        return lax.ppermute(block, "seq", route)

    query_count = group * image_rows
    initial = (
        jnp.full((query_count, head_count), -jnp.inf, jnp.float32),
        jnp.zeros((query_count, head_count), jnp.float32),
        jnp.zeros((query_count, head_count, HEAD_DIM), jnp.float32),
    )
    carried = absorb(initial, keys, values, valid_for(own_group), queries)

    def one_turn(turn, state):
        current, keys, values = state
        keys, values = next_group(keys), next_group(values)
        source = (own_group - turn) % group_count
        return (absorb(current, keys, values, valid_for(source), queries), keys, values)

    carried, _, _ = lax.fori_loop(1, group_count, one_turn, (carried, keys, values))
    _, denominator, numerator = carried
    attended = (numerator / denominator[:, :, None]).astype(jnp.bfloat16)
    sides = attended.reshape(-1, 2, STRIDE, head_count, HEAD_DIM)
    return [
        (sides[:, 0, :, c].reshape(-1, HEAD_DIM), sides[:, 1, :, c].reshape(-1, HEAD_DIM))
        for c in range(head_count)
    ]


def on_device(query, key_image, value_image, key_text, value_text, prompt_ids, blend, w_out):
    seq_count = lax.axis_size("seq")
    win_count = lax.axis_size("win")
    group = math.gcd(HEADS, seq_count)
    head_count = HEADS // group
    image_rows, text_rows = query.shape[1], key_text.shape[1]
    sources = [query[0], key_image[0], key_text[0], value_image[0], value_text[0]]

    blocks = []
    for chunk in range(head_count):
        packed = pack(sources, chunk, group, head_count)
        blocks.append(
            [packed[0]] + [shifted(packed[d], "seq", d, group) for d in range(1, group)]
        )

    weights = jnp.concatenate(
        [blend] + [shifted(blend, "seq", d, group) for d in range(1, group)], axis=0
    )
    weights = weights.astype(jnp.float32).reshape(-1, 2, STRIDE)
    weight_left, weight_right = (weights[:, side].reshape(-1, 1) for side in range(2))

    if seq_count == group:
        strips = [attend(chunk, prompt_ids, image_rows, text_rows) for chunk in blocks]
    else:
        strips = attend_ring(blocks, prompt_ids[0], image_rows, text_rows)

    features = []
    for left, right in strips:
        from_prev = shifted(right, "win", 1, win_count)
        from_next = shifted(left, "win", -1, win_count)
        mixed = blend_strips(left, right, from_prev, from_next, weight_left, weight_right, group)
        features.append(mixed[0])
        features += [shifted(mixed[d], "seq", -d, group) for d in range(1, group)]
    return project(features, w_out, group, head_count)[None]


def solution(mesh):
    tokens = P(("pano", "win"), "seq", None)
    return jax.shard_map(
        on_device,
        mesh=mesh,
        in_specs=(tokens,) * 5 + (P(("pano", "win"), None), P(("pano", "win"), "seq"), P()),
        out_specs=tokens,
        check_vma=False,
    )
```

time: 139 us -> 142 us (1.022); the launches traced: 136 us -> 141 us
  Pallas kernels: 0 us -> 76.6 us
  waiting for transfers between devices: 85.1 us -> 13 us
  starting transfers between devices: 8.24 us -> 36.2 us
  matrix products: 16.8 us -> 0 us
  local copies, waits for them, and re-layouts: 19.8 us -> 13.9 us
  other arithmetic: 5.97 us -> 0.69 us
    ppermute x4 -> x0, waiting for transfers between devices: 80.6 us -> none  [swapped(): return lax.ppermute(block, axis, route)]
    pallas_call x0 -> x10, Pallas kernels: none -> 76.6 us  [the longest x3 60.4 us: pack(): pl.pallas_call(functools.partial(pack_kernel, chunk, group, head_count),...]
    ppermute x2 -> x27, starting transfers between devices: 3.75 us -> 36.2 us  [shifted(): return lax.ppermute(block, axis, route)]
    dot_general x5 -> x0, matrix products: 16.8 us -> none  [the longest x3 10.3 us: project_rows(): jnp.dot(flat_rows, w_out, preferred_element_type=jnp.float32)]
    ppermute x2 -> x27, waiting for transfers between devices: 4.43 us -> 13 us  [shifted(): return lax.ppermute(block, axis, route)]
    unnamed x22 -> x44, local copies, waits for them, and re-layouts: 4.71 us -> 12 us
    dynamic_slice x3 -> x0, local copies, waits for them, and re-layouts: 6.48 us -> none  [the longest x1 5.11 us: regroup(): kept_half = lax.dynamic_index_in_dim(paired, own_bit, 2, keepdims=False)]
    concatenate x7 -> x0, local copies, waits for them, and re-layouts: 6.01 us -> none  [the longest x6 5.93 us: on_device(): jnp.concatenate([query[0], key_image[0], key_text[0], value_image[0], val...]
  transfers between devices with their start and end apart: 6 -> 27, of which waited for: 5 -> 5; matrix products, arithmetic and copies ran while one was open for 5% -> 2% of each run, Pallas kernels for 0% -> 37%
where the time goes in v1:
time: 142 us; the launch traced here: 141 us
  Pallas kernels  76.6 us (54%)
  starting transfers between devices  36.2 us (25%)
  local copies, waits for them, and re-layouts  13.9 us (10%)
  waiting for transfers between devices  13 us (9%)
    pallas_call x3, Pallas kernels, pack(): pl.pallas_call(functools.partial(pack_kernel, chunk, group, head_count),...  60.4 us
    ppermute x27, starting transfers between devices, shifted(): return lax.ppermute(block, axis, route)  36.2 us
    ppermute x27, waiting for transfers between devices, shifted(): return lax.ppermute(block, axis, route)  13 us
    unnamed x44, local copies, waits for them, and re-layouts  12 us
    pallas_call x3, Pallas kernels, blend_strips(): pl.pallas_call(functools.partial(blend_kernel, group), out_shape=[out] *...  6.31 us
    pallas_call x3, Pallas kernels, attend(): pl.pallas_call(functools.partial(attend_kernel, group, image_rows, text_r...  5.33 us
    pallas_call x1, Pallas kernels, project(): pl.pallas_call(functools.partial(project_kernel, group, head_count), grid...  4.59 us
  transfers between devices with their start and end apart: 27, of which 5 were waited for; matrix products, arithmetic and copies ran while one was open for 2% of the time, Pallas kernels for 37%

profile of v1, /device:TPU:1, one launch (start us, length us, event | category | flops | bytes accessed | tf_op | source)
XLA Modules:
  0.0 140.8 jit_solution(8077607832403928833)
XLA Ops:
  0.0 20.1 %pack.5 = (bf16[608,128]{1,0:T(8,128)(2,1)}, bf16[608,128]{1,0:T(8,128)(2,1)}, bf16[608,128]{1,0:T(8,128)(2,1)}, bf16[608,128]{1,0:T(8,128)(2,1)}) custom-call(bf16[192,1536]{1,0:T(8,128)(2,1)} %bitcast.6, bf16[192,1536]{1,0:T(8,128)(2,1)} %bitcast.9, bf16[16,1536]{1,0:T(8,128)(2,1)} %bitcast.15, bf16[192,1536]{1,0:T(8,128)(2,1)} %bitcast.12, ...), custom_call_target="tpu_custom_call" | custom-call | tf_op jit(solution)/shard_map/pack/pallas_call | solution.py:55
  20.1 2.2 %collective-permute-start.19 = (bf16[608,128]{1,0:T(8,128)(2,1)}, bf16[608,128]{1,0:T(8,128)(2,1)S(1)}, u32[]{:S(2)}, u32[]{:S(2)}) collective-permute-start(bf16[608,128]{1,0:T(8,128)(2,1)} %get-tuple-element.56), channel_id=1, source_target_pairs={{0,4},{4,8},{8,12},{12,0},{1,5},{5,9},{9,13},{13,1},{2,6},{6,10},{... | collective-permute-start | bytes 466952 | tf_op jit(solution)/shard_map/ppermute | solution.py:30
  22.3 2.3 %collective-permute-start.20 = (bf16[608,128]{1,0:T(8,128)(2,1)}, bf16[608,128]{1,0:T(8,128)(2,1)S(1)}, u32[]{:S(2)}, u32[]{:S(2)}) collective-permute-start(bf16[608,128]{1,0:T(8,128)(2,1)} %get-tuple-element.57), channel_id=1, source_target_pairs={{0,8},{4,12},{8,0},{12,4},{1,9},{5,13},{9,1},{13,5},{2,10},{6,14},... | collective-permute-start | bytes 466952 | tf_op jit(solution)/shard_map/ppermute | solution.py:30
  24.6 1.1 collective-permute-start.21
  25.7 20.1 %pack.4 = (bf16[608,128]{1,0:T(8,128)(2,1)}, bf16[608,128]{1,0:T(8,128)(2,1)}, bf16[608,128]{1,0:T(8,128)(2,1)}, bf16[608,128]{1,0:T(8,128)(2,1)}) custom-call(bf16[192,1536]{1,0:T(8,128)(2,1)} %bitcast.7, bf16[192,1536]{1,0:T(8,128)(2,1)} %bitcast.10, bf16[16,1536]{1,0:T(8,128)(2,1)} %bitcast.16, bf16[192,1536]{1,0:T(8,128)(2,1)} %bitcast.13, ...), custom_call_target="tpu_custom_call" | custom-call | tf_op jit(solution)/shard_map/pack/pallas_call | solution.py:55
  45.9 0.5 collective-permute-start.11
  46.4 3.5 %collective-permute-done.6 = s32[1,192]{1,0:T(1,128)S(1)} collective-permute-done((s32[1,192]{1,0:T(1,128)}, s32[1,192]{1,0:T(1,128)S(1)}, u32[]{:S(2)}, u32[]{:S(2)}) %collective-permute-start.6) | collective-permute-done | bytes 800 | tf_op jit(solution)/shard_map/ppermute | solution.py:30
  49.8 2.5 %collective-permute-start.5 = (s32[1,192]{1,0:T(1,128)}, s32[1,192]{1,0:T(1,128)S(1)}, u32[]{:S(2)}, u32[]{:S(2)}) collective-permute-start(s32[1,192]{1,0:T(1,128)} %param.14), channel_id=1, source_target_pairs={{0,4},{4,8},{8,12},{12,0},{1,5},{5,9},{9,13},{13,1},{2,6},{6,10},{... | collective-permute-start | bytes 2312 | tf_op jit(solution)/shard_map/ppermute | solution.py:30
  52.3 2.0 %collective-permute-done.5 = s32[1,192]{1,0:T(1,128)S(1)} collective-permute-done((s32[1,192]{1,0:T(1,128)}, s32[1,192]{1,0:T(1,128)S(1)}, u32[]{:S(2)}, u32[]{:S(2)}) %collective-permute-start.5) | collective-permute-done | bytes 800 | tf_op jit(solution)/shard_map/ppermute | solution.py:30
  54.3 1.1 collective-permute-start.7
  55.4 1.8 %collective-permute-done.7 = s32[1,192]{1,0:T(1,128)S(1)} collective-permute-done((s32[1,192]{1,0:T(1,128)}, s32[1,192]{1,0:T(1,128)S(1)}, u32[]{:S(2)}, u32[]{:S(2)}) %collective-permute-start.7) | collective-permute-done | bytes 800 | tf_op jit(solution)/shard_map/ppermute | solution.py:30
  57.3 2.6 %collective-permute-start.13 = (bf16[608,128]{1,0:T(8,128)(2,1)}, bf16[608,128]{1,0:T(8,128)(2,1)S(1)}, u32[]{:S(2)}, u32[]{:S(2)}) collective-permute-start(bf16[608,128]{1,0:T(8,128)(2,1)} %get-tuple-element.48), channel_id=1, source_target_pairs={{0,12},{4,0},{8,4},{12,8},{1,13},{5,1},{9,5},{13,9},{2,14},{6,2},{... | collective-permute-start | bytes 466952 | tf_op jit(solution)/shard_map/ppermute | solution.py:30
  59.8 20.1 %pack.3 = (bf16[608,128]{1,0:T(8,128)(2,1)}, bf16[608,128]{1,0:T(8,128)(2,1)}, bf16[608,128]{1,0:T(8,128)(2,1)}, bf16[608,128]{1,0:T(8,128)(2,1)}) custom-call(bf16[192,1536]{1,0:T(8,128)(2,1)} %bitcast.8, bf16[192,1536]{1,0:T(8,128)(2,1)} %bitcast.11, bf16[16,1536]{1,0:T(8,128)(2,1)} %bitcast.17, bf16[192,1536]{1,0:T(8,128)(2,1)} %bitcast.14, ...), custom_call_target="tpu_custom_call" | custom-call | tf_op jit(solution)/shard_map/pack/pallas_call | solution.py:55
  80.3 1.3 collective-permute-start.1
  81.6 2.3 %collective-permute-start.2 = (bf16[608,128]{1,0:T(8,128)(2,1)}, bf16[608,128]{1,0:T(8,128)(2,1)S(1)}, u32[]{:S(2)}, u32[]{:S(2)}) collective-permute-start(bf16[608,128]{1,0:T(8,128)(2,1)} %get-tuple-element.38), channel_id=1, source_target_pairs={{0,12},{4,0},{8,4},{12,8},{1,13},{5,1},{9,5},{13,9},{2,14},{6,2},{... | collective-permute-start | bytes 466952 | tf_op jit(solution)/shard_map/ppermute | solution.py:30
  83.9 0.9 copy-done.12
  84.8 0.7 copy-done.13
  85.4 1.8 %attend.5 = (bf16[384,128]{1,0:T(8,128)(2,1)S(1)}, bf16[384,128]{1,0:T(8,128)(2,1)S(1)}) custom-call(s32[1,64]{1,0:T(1,128)S(1)} %copy-done.13, bf16[608,128]{1,0:T(8,128)(2,1)S(1)} %copy-done.12, bf16[608,128]{1,0:T(8,128)(2,1)S(1)} %collective-permute-done.19.refs_1_, bf16[608,128]{1,0:T(8,128)(2,1)S(1)} %collective-permute-done.20.refs_2_, ...), custom_call_target="tpu_custom_call" | custom-call | flops 327155712 | bytes 851968 | tf_op jit(solution)/shard_map/attend/pallas_call | solution.py:110
  87.2 6.7 %collective-permute-start.23 = (bf16[384,128]{1,0:T(8,128)(2,1)S(1)}, bf16[384,128]{1,0:T(8,128)(2,1)S(1)}, u32[]{:S(2)}, u32[]{:S(2)}) collective-permute-start(bf16[384,128]{1,0:T(8,128)(2,1)S(1)} %get-tuple-element.59.left), channel_id=1, source_target_pairs={{0,3},{1,0},{2,1},{3,2},{4,7},{5,4},{6,5},{7,6},{8,11},{9,8},{10,9... | collective-permute-start | bytes 294920 | tf_op jit(solution)/shard_map/ppermute | solution.py:30
  94.0 0.7 add_convert_fusion
  94.8 1.2 collective-permute-start.22
  95.9 0.9 copy-done.10
  96.9 0.7 copy-done.14
  97.5 1.8 %attend.4 = (bf16[384,128]{1,0:T(8,128)(2,1)S(1)}, bf16[384,128]{1,0:T(8,128)(2,1)S(1)}) custom-call(s32[1,64]{1,0:T(1,128)S(1)} %copy-done.14, bf16[608,128]{1,0:T(8,128)(2,1)S(1)} %copy-done.10, bf16[608,128]{1,0:T(8,128)(2,1)S(1)} %collective-permute-done.11.refs_1_, bf16[608,128]{1,0:T(8,128)(2,1)S(1)} %collective-permute-done.12.refs_2_, ...), custom_call_target="tpu_custom_call" | custom-call | flops 327155712 | bytes 851968 | tf_op jit(solution)/shard_map/attend/pallas_call | solution.py:110
  99.4 1.7 %collective-permute-start.14 = (bf16[384,128]{1,0:T(8,128)(2,1)S(1)}, bf16[384,128]{1,0:T(8,128)(2,1)S(1)}, u32[]{:S(2)}, u32[]{:S(2)}) collective-permute-start(bf16[384,128]{1,0:T(8,128)(2,1)S(1)} %get-tuple-element.50.right), channel_id=1, source_target_pairs={{0,1},{1,2},{2,3},{3,0},{4,5},{5,6},{6,7},{7,4},{8,9},{9,10},{10,1... | collective-permute-start | bytes 294920 | tf_op jit(solution)/shard_map/ppermute | solution.py:30
  101.1 0.9 copy-done.11
  102.0 0.7 copy-done.15
  102.7 1.8 %attend.3 = (bf16[384,128]{1,0:T(8,128)(2,1)S(1)}, bf16[384,128]{1,0:T(8,128)(2,1)S(1)}) custom-call(s32[1,64]{1,0:T(1,128)S(1)} %copy-done.15, bf16[608,128]{1,0:T(8,128)(2,1)S(1)} %copy-done.11, bf16[608,128]{1,0:T(8,128)(2,1)S(1)} %collective-permute-done.refs_1_, bf16[608,128]{1,0:T(8,128)(2,1)S(1)} %collective-permute-done.1.refs_2_, ...), custom_call_target="tpu_custom_call" | custom-call | flops 327155712 | bytes 851968 | tf_op jit(solution)/shard_map/attend/pallas_call | solution.py:110
  104.6 1.7 %collective-permute-start.3 = (bf16[384,128]{1,0:T(8,128)(2,1)S(1)}, bf16[384,128]{1,0:T(8,128)(2,1)S(1)}, u32[]{:S(2)}, u32[]{:S(2)}) collective-permute-start(bf16[384,128]{1,0:T(8,128)(2,1)S(1)} %get-tuple-element.40.right), channel_id=1, source_target_pairs={{0,1},{1,2},{2,3},{3,0},{4,5},{5,6},{6,7},{7,4},{8,9},{9,10},{10,1... | collective-permute-start | bytes 294920 | tf_op jit(solution)/shard_map/ppermute | solution.py:30
  106.3 0.9 reshape.6.weight_right
  107.2 0.9 reshape.5.weight_left
  108.1 0.6 copy-done.21
  108.7 2.1 %blend.5 = (bf16[192,128]{1,0:T(8,128)(2,1)}, bf16[192,128]{1,0:T(8,128)(2,1)}, bf16[192,128]{1,0:T(8,128)(2,1)}, bf16[192,128]{1,0:T(8,128)(2,1)}) custom-call(bf16[384,128]{1,0:T(8,128)(2,1)} %copy-done.1, bf16[384,128]{1,0:T(8,128)(2,1)} %copy-done.2, bf16[384,128]{1,0:T(8,128)(2,1)} %copy-done.21, bf16[384,128]{1,0:T(8,128)(2,1)} %copy-done.16, ...), custom_call_target="tpu_custom_call" | custom-call | tf_op jit(solution)/shard_map/blend/pallas_call | solution.py:143
  111.0 1.5 %collective-permute-start.25 = (bf16[192,128]{1,0:T(8,128)(2,1)}, bf16[192,128]{1,0:T(8,128)(2,1)S(1)}, u32[]{:S(2)}, u32[]{:S(2)}) collective-permute-start(bf16[192,128]{1,0:T(8,128)(2,1)} %get-tuple-element.63), channel_id=1, source_target_pairs={{0,8},{4,12},{8,0},{12,4},{1,9},{5,13},{9,1},{13,5},{2,10},{6,14},... | collective-permute-start | bytes 147464 | tf_op jit(solution)/shard_map/ppermute | solution.py:30
  112.5 1.4 collective-permute-start.26
  113.9 2.1 %blend.4 = (bf16[192,128]{1,0:T(8,128)(2,1)}, bf16[192,128]{1,0:T(8,128)(2,1)}, bf16[192,128]{1,0:T(8,128)(2,1)}, bf16[192,128]{1,0:T(8,128)(2,1)}) custom-call(bf16[384,128]{1,0:T(8,128)(2,1)} %copy-done.3, bf16[384,128]{1,0:T(8,128)(2,1)} %copy-done.4, bf16[384,128]{1,0:T(8,128)(2,1)} %copy-done.19, bf16[384,128]{1,0:T(8,128)(2,1)} %copy-done.17, ...), custom_call_target="tpu_custom_call" | custom-call | tf_op jit(solution)/shard_map/blend/pallas_call | solution.py:143
  116.0 1.9 %collective-permute-start.16 = (bf16[192,128]{1,0:T(8,128)(2,1)}, bf16[192,128]{1,0:T(8,128)(2,1)S(1)}, u32[]{:S(2)}, u32[]{:S(2)}) collective-permute-start(bf16[192,128]{1,0:T(8,128)(2,1)} %get-tuple-element.52), channel_id=1, source_target_pairs={{0,12},{4,0},{8,4},{12,8},{1,13},{5,1},{9,5},{13,9},{2,14},{6,2},{... | collective-permute-start | bytes 147464 | tf_op jit(solution)/shard_map/ppermute | solution.py:30
  118.0 0.6 copy-done.20
  118.6 2.1 %blend.3 = (bf16[192,128]{1,0:T(8,128)(2,1)}, bf16[192,128]{1,0:T(8,128)(2,1)}, bf16[192,128]{1,0:T(8,128)(2,1)}, bf16[192,128]{1,0:T(8,128)(2,1)}) custom-call(bf16[384,128]{1,0:T(8,128)(2,1)} %copy-done.5, bf16[384,128]{1,0:T(8,128)(2,1)} %copy-done.6, bf16[384,128]{1,0:T(8,128)(2,1)} %copy-done.20, bf16[384,128]{1,0:T(8,128)(2,1)} %copy-done.18, ...), custom_call_target="tpu_custom_call" | custom-call | tf_op jit(solution)/shard_map/blend/pallas_call | solution.py:143
  120.7 3.2 %collective-permute-start.8 = (bf16[192,128]{1,0:T(8,128)(2,1)}, bf16[192,128]{1,0:T(8,128)(2,1)S(1)}, u32[]{:S(2)}, u32[]{:S(2)}) collective-permute-start(bf16[192,128]{1,0:T(8,128)(2,1)} %get-tuple-element.42), channel_id=1, source_target_pairs={{0,12},{4,0},{8,4},{12,8},{1,13},{5,1},{9,5},{13,9},{2,14},{6,2},{... | collective-permute-start | bytes 147464 | tf_op jit(solution)/shard_map/ppermute | solution.py:30
  124.0 0.4 collective-permute-start.10
  124.4 1.9 %collective-permute-done.18.refs_7_ = bf16[192,128]{1,0:T(8,128)(2,1)S(1)} collective-permute-done((bf16[192,128]{1,0:T(8,128)(2,1)}, bf16[192,128]{1,0:T(8,128)(2,1)S(1)}, u32[]{:S(2)}, u32[]{:S(2)}) %collective-permute-start.18) | collective-permute-done | bytes 49184 | tf_op jit(solution)/shard_map/ppermute | solution.py:30
  126.2 3.9 %collective-permute-done.9.refs_2_ = bf16[192,128]{1,0:T(8,128)(2,1)S(1)} collective-permute-done((bf16[192,128]{1,0:T(8,128)(2,1)}, bf16[192,128]{1,0:T(8,128)(2,1)S(1)}, u32[]{:S(2)}, u32[]{:S(2)}) %collective-permute-start.9) | collective-permute-done | bytes 49184 | tf_op jit(solution)/shard_map/ppermute | solution.py:30
  130.1 3.7 %copy-done = bf16[1536,3072]{1,0:T(8,128)(2,1)S(1)} copy-done((bf16[1536,3072]{1,0:T(8,128)(2,1)S(1)}, bf16[1536,3072]{1,0:T(8,128)(2,1)}, u32[]{:S(2)}) %copy-start) | copy-done | bytes 9437208
  133.8 0.8 copy-done.7
  134.6 0.8 copy-done.8
  135.4 0.8 copy-done.9
  136.2 4.6 %project.1 = bf16[192,3072]{1,0:T(8,128)(2,1)} custom-call(bf16[192,128]{1,0:T(8,128)(2,1)S(1)} %copy-done.9, bf16[192,128]{1,0:T(8,128)(2,1)S(1)} %collective-permute-done.8.refs_1_, bf16[192,128]{1,0:T(8,128)(2,1)S(1)} %collective-permute-done.9.refs_2_, bf16[192,128]{1,0:T(8,128)(2,1)S(1)} %collective-permute-done.10.refs_3_, ...), custom_call_target="tpu_custom_call" | custom-call | flops 1811939328 | bytes 11206656 | tf_op jit(solution)/shard_map/project/pallas_call | solution.py:180
  (65 shorter events, 1.1 us)
Async XLA Ops:
  20.1 37.1 %collective-permute-start.19 = (bf16[608,128]{1,0:T(8,128)(2,1)}, bf16[608,128]{1,0:T(8,128)(2,1)S(1)}, u32[]{:S(2)}, u32[]{:S(2)}) collective-permute-start(bf16[608,128]{1,0:T(8,128)(2,1)} %get-tuple-element.56), channel_id=1, source_target_pairs={{0,4},{4,8},{8,12},{12,0},{1,5},{5,9},{9,13},{13,1},{2,6},{6,10},{... | collective-permute-start | bytes 466952 | tf_op jit(solution)/shard_map/ppermute | solution.py:30
  22.3 57.6 %collective-permute-start.20 = (bf16[608,128]{1,0:T(8,128)(2,1)}, bf16[608,128]{1,0:T(8,128)(2,1)S(1)}, u32[]{:S(2)}, u32[]{:S(2)}) collective-permute-start(bf16[608,128]{1,0:T(8,128)(2,1)} %get-tuple-element.57), channel_id=1, source_target_pairs={{0,8},{4,12},{8,0},{12,4},{1,9},{5,13},{9,1},{13,5},{2,10},{6,14},... | collective-permute-start | bytes 466952 | tf_op jit(solution)/shard_map/ppermute | solution.py:30
  24.6 55.7 %collective-permute-start.21 = (bf16[608,128]{1,0:T(8,128)(2,1)}, bf16[608,128]{1,0:T(8,128)(2,1)S(1)}, u32[]{:S(2)}, u32[]{:S(2)}) collective-permute-start(bf16[608,128]{1,0:T(8,128)(2,1)} %get-tuple-element.58), channel_id=1, source_target_pairs={{0,12},{4,0},{8,4},{12,8},{1,13},{5,1},{9,5},{13,9},{2,14},{6,2},{... | collective-permute-start | bytes 466952 | tf_op jit(solution)/shard_map/ppermute | solution.py:30
  45.9 35.7 %collective-permute-start.11 = (bf16[608,128]{1,0:T(8,128)(2,1)}, bf16[608,128]{1,0:T(8,128)(2,1)S(1)}, u32[]{:S(2)}, u32[]{:S(2)}) collective-permute-start(bf16[608,128]{1,0:T(8,128)(2,1)} %get-tuple-element.46), channel_id=1, source_target_pairs={{0,4},{4,8},{8,12},{12,0},{1,5},{5,9},{9,13},{13,1},{2,6},{6,10},{... | collective-permute-start | bytes 466952 | tf_op jit(solution)/shard_map/ppermute | solution.py:30
  46.3 3.5 %collective-permute-start.6 = (s32[1,192]{1,0:T(1,128)}, s32[1,192]{1,0:T(1,128)S(1)}, u32[]{:S(2)}, u32[]{:S(2)}) collective-permute-start(s32[1,192]{1,0:T(1,128)} %param.14), channel_id=1, source_target_pairs={{0,8},{4,12},{8,0},{12,4},{1,9},{5,13},{9,1},{13,5},{2,10},{6,14},... | collective-permute-start | bytes 2312 | tf_op jit(solution)/shard_map/ppermute | solution.py:30
  49.8 4.4 %collective-permute-start.5 = (s32[1,192]{1,0:T(1,128)}, s32[1,192]{1,0:T(1,128)S(1)}, u32[]{:S(2)}, u32[]{:S(2)}) collective-permute-start(s32[1,192]{1,0:T(1,128)} %param.14), channel_id=1, source_target_pairs={{0,4},{4,8},{8,12},{12,0},{1,5},{5,9},{9,13},{13,1},{2,6},{6,10},{... | collective-permute-start | bytes 2312 | tf_op jit(solution)/shard_map/ppermute | solution.py:30
  54.3 2.9 %collective-permute-start.7 = (s32[1,192]{1,0:T(1,128)}, s32[1,192]{1,0:T(1,128)S(1)}, u32[]{:S(2)}, u32[]{:S(2)}) collective-permute-start(s32[1,192]{1,0:T(1,128)} %param.14), channel_id=1, source_target_pairs={{0,12},{4,0},{8,4},{12,8},{1,13},{5,1},{9,5},{13,9},{2,14},{6,2},{... | collective-permute-start | bytes 2312 | tf_op jit(solution)/shard_map/ppermute | solution.py:30
  57.2 30.1 %collective-permute-start.12 = (bf16[608,128]{1,0:T(8,128)(2,1)}, bf16[608,128]{1,0:T(8,128)(2,1)S(1)}, u32[]{:S(2)}, u32[]{:S(2)}) collective-permute-start(bf16[608,128]{1,0:T(8,128)(2,1)} %get-tuple-element.47), channel_id=1, source_target_pairs={{0,8},{4,12},{8,0},{12,4},{1,9},{5,13},{9,1},{13,5},{2,10},{6,14},... | collective-permute-start | bytes 466952 | tf_op jit(solution)/shard_map/ppermute | solution.py:30
  57.3 37.5 %collective-permute-start.13 = (bf16[608,128]{1,0:T(8,128)(2,1)}, bf16[608,128]{1,0:T(8,128)(2,1)S(1)}, u32[]{:S(2)}, u32[]{:S(2)}) collective-permute-start(bf16[608,128]{1,0:T(8,128)(2,1)} %get-tuple-element.48), channel_id=1, source_target_pairs={{0,12},{4,0},{8,4},{12,8},{1,13},{5,1},{9,5},{13,9},{2,14},{6,2},{... | collective-permute-start | bytes 466952 | tf_op jit(solution)/shard_map/ppermute | solution.py:30
  80.0 19.3 %collective-permute-start = (bf16[608,128]{1,0:T(8,128)(2,1)}, bf16[608,128]{1,0:T(8,128)(2,1)S(1)}, u32[]{:S(2)}, u32[]{:S(2)}) collective-permute-start(bf16[608,128]{1,0:T(8,128)(2,1)} %get-tuple-element.36), channel_id=1, source_target_pairs={{0,4},{4,8},{8,12},{12,0},{1,5},{5,9},{9,13},{13,1},{2,6},{6,10},{... | collective-permute-start | bytes 466952 | tf_op jit(solution)/shard_map/ppermute | solution.py:30
  80.3 19.1 %collective-permute-start.1 = (bf16[608,128]{1,0:T(8,128)(2,1)}, bf16[608,128]{1,0:T(8,128)(2,1)S(1)}, u32[]{:S(2)}, u32[]{:S(2)}) collective-permute-start(bf16[608,128]{1,0:T(8,128)(2,1)} %get-tuple-element.37), channel_id=1, source_target_pairs={{0,8},{4,12},{8,0},{12,4},{1,9},{5,13},{9,1},{13,5},{2,10},{6,14},... | collective-permute-start | bytes 466952 | tf_op jit(solution)/shard_map/ppermute | solution.py:30
  81.6 19.5 %collective-permute-start.2 = (bf16[608,128]{1,0:T(8,128)(2,1)}, bf16[608,128]{1,0:T(8,128)(2,1)S(1)}, u32[]{:S(2)}, u32[]{:S(2)}) collective-permute-start(bf16[608,128]{1,0:T(8,128)(2,1)} %get-tuple-element.38), channel_id=1, source_target_pairs={{0,12},{4,0},{8,4},{12,8},{1,13},{5,1},{9,5},{13,9},{2,14},{6,2},{... | collective-permute-start | bytes 466952 | tf_op jit(solution)/shard_map/ppermute | solution.py:30
  83.9 0.9 copy-start.12
  84.8 0.7 copy-start.13
  87.2 20.9 %copy-start.1 = (bf16[384,128]{1,0:T(8,128)(2,1)}, bf16[384,128]{1,0:T(8,128)(2,1)S(1)}, u32[]{:S(2)}) copy-start(bf16[384,128]{1,0:T(8,128)(2,1)S(1)} %get-tuple-element.59.left) | copy-start | bytes 294916
  87.2 20.9 %copy-start.2 = (bf16[384,128]{1,0:T(8,128)(2,1)}, bf16[384,128]{1,0:T(8,128)(2,1)S(1)}, u32[]{:S(2)}) copy-start(bf16[384,128]{1,0:T(8,128)(2,1)S(1)} %get-tuple-element.60.right) | copy-start | bytes 294916
  87.2 17.3 %collective-permute-start.23 = (bf16[384,128]{1,0:T(8,128)(2,1)S(1)}, bf16[384,128]{1,0:T(8,128)(2,1)S(1)}, u32[]{:S(2)}, u32[]{:S(2)}) collective-permute-start(bf16[384,128]{1,0:T(8,128)(2,1)S(1)} %get-tuple-element.59.left), channel_id=1, source_target_pairs={{0,3},{1,0},{2,1},{3,2},{4,7},{5,4},{6,5},{7,6},{8,11},{9,8},{10,9... | collective-permute-start | bytes 294920 | tf_op jit(solution)/shard_map/ppermute | solution.py:30
  94.8 13.3 %collective-permute-start.22 = (bf16[384,128]{1,0:T(8,128)(2,1)S(1)}, bf16[384,128]{1,0:T(8,128)(2,1)S(1)}, u32[]{:S(2)}, u32[]{:S(2)}) collective-permute-start(bf16[384,128]{1,0:T(8,128)(2,1)S(1)} %get-tuple-element.60.right), channel_id=1, source_target_pairs={{0,1},{1,2},{2,3},{3,0},{4,5},{5,6},{6,7},{7,4},{8,9},{9,10},{10,1... | collective-permute-start | bytes 294920 | tf_op jit(solution)/shard_map/ppermute | solution.py:30
  95.9 0.9 copy-start.10
  96.9 0.7 copy-start.14
  99.3 14.6 %copy-start.3 = (bf16[384,128]{1,0:T(8,128)(2,1)}, bf16[384,128]{1,0:T(8,128)(2,1)S(1)}, u32[]{:S(2)}) copy-start(bf16[384,128]{1,0:T(8,128)(2,1)S(1)} %get-tuple-element.49.left) | copy-start | bytes 294916
  99.3 14.6 %copy-start.4 = (bf16[384,128]{1,0:T(8,128)(2,1)}, bf16[384,128]{1,0:T(8,128)(2,1)S(1)}, u32[]{:S(2)}) copy-start(bf16[384,128]{1,0:T(8,128)(2,1)S(1)} %get-tuple-element.50.right) | copy-start | bytes 294916
  99.3 11.7 %collective-permute-start.15 = (bf16[384,128]{1,0:T(8,128)(2,1)S(1)}, bf16[384,128]{1,0:T(8,128)(2,1)S(1)}, u32[]{:S(2)}, u32[]{:S(2)}) collective-permute-start(bf16[384,128]{1,0:T(8,128)(2,1)S(1)} %get-tuple-element.49.left), channel_id=1, source_target_pairs={{0,3},{1,0},{2,1},{3,2},{4,7},{5,4},{6,5},{7,6},{8,11},{9,8},{10,9... | collective-permute-start | bytes 294920 | tf_op jit(solution)/shard_map/ppermute | solution.py:30
  99.4 13.1 %collective-permute-start.14 = (bf16[384,128]{1,0:T(8,128)(2,1)S(1)}, bf16[384,128]{1,0:T(8,128)(2,1)S(1)}, u32[]{:S(2)}, u32[]{:S(2)}) collective-permute-start(bf16[384,128]{1,0:T(8,128)(2,1)S(1)} %get-tuple-element.50.right), channel_id=1, source_target_pairs={{0,1},{1,2},{2,3},{3,0},{4,5},{5,6},{6,7},{7,4},{8,9},{9,10},{10,1... | collective-permute-start | bytes 294920 | tf_op jit(solution)/shard_map/ppermute | solution.py:30
  101.1 0.9 copy-start.11
  102.0 0.7 copy-start.15
  104.5 13.5 %copy-start.5 = (bf16[384,128]{1,0:T(8,128)(2,1)}, bf16[384,128]{1,0:T(8,128)(2,1)S(1)}, u32[]{:S(2)}) copy-start(bf16[384,128]{1,0:T(8,128)(2,1)S(1)} %get-tuple-element.39.left) | copy-start | bytes 294916
  104.5 13.5 %copy-start.6 = (bf16[384,128]{1,0:T(8,128)(2,1)}, bf16[384,128]{1,0:T(8,128)(2,1)S(1)}, u32[]{:S(2)}) copy-start(bf16[384,128]{1,0:T(8,128)(2,1)S(1)} %get-tuple-element.40.right) | copy-start | bytes 294916
  104.5 11.5 %collective-permute-start.4 = (bf16[384,128]{1,0:T(8,128)(2,1)S(1)}, bf16[384,128]{1,0:T(8,128)(2,1)S(1)}, u32[]{:S(2)}, u32[]{:S(2)}) collective-permute-start(bf16[384,128]{1,0:T(8,128)(2,1)S(1)} %get-tuple-element.39.left), channel_id=1, source_target_pairs={{0,3},{1,0},{2,1},{3,2},{4,7},{5,4},{6,5},{7,6},{8,11},{9,8},{10,9... | collective-permute-start | bytes 294920 | tf_op jit(solution)/shard_map/ppermute | solution.py:30
  104.6 3.5 %copy-start.16 = (bf16[384,128]{1,0:T(8,128)(2,1)}, bf16[384,128]{1,0:T(8,128)(2,1)S(1)}, u32[]{:S(2)}) copy-start(bf16[384,128]{1,0:T(8,128)(2,1)S(1)} %collective-permute-done.23.from_next) | copy-start | bytes 294916
  104.6 13.4 %collective-permute-start.3 = (bf16[384,128]{1,0:T(8,128)(2,1)S(1)}, bf16[384,128]{1,0:T(8,128)(2,1)S(1)}, u32[]{:S(2)}, u32[]{:S(2)}) collective-permute-start(bf16[384,128]{1,0:T(8,128)(2,1)S(1)} %get-tuple-element.40.right), channel_id=1, source_target_pairs={{0,1},{1,2},{2,3},{3,0},{4,5},{5,6},{6,7},{7,4},{8,9},{9,10},{10,1... | collective-permute-start | bytes 294920 | tf_op jit(solution)/shard_map/ppermute | solution.py:30
  110.8 9.9 %collective-permute-start.24 = (bf16[192,128]{1,0:T(8,128)(2,1)}, bf16[192,128]{1,0:T(8,128)(2,1)S(1)}, u32[]{:S(2)}, u32[]{:S(2)}) collective-permute-start(bf16[192,128]{1,0:T(8,128)(2,1)} %get-tuple-element.62), channel_id=1, source_target_pairs={{0,12},{4,0},{8,4},{12,8},{1,13},{5,1},{9,5},{13,9},{2,14},{6,2},{... | collective-permute-start | bytes 147464 | tf_op jit(solution)/shard_map/ppermute | solution.py:30
  111.0 2.9 %copy-start.17 = (bf16[384,128]{1,0:T(8,128)(2,1)}, bf16[384,128]{1,0:T(8,128)(2,1)S(1)}, u32[]{:S(2)}) copy-start(bf16[384,128]{1,0:T(8,128)(2,1)S(1)} %collective-permute-done.15.from_next) | copy-start | bytes 294916
  111.0 9.7 %collective-permute-start.25 = (bf16[192,128]{1,0:T(8,128)(2,1)}, bf16[192,128]{1,0:T(8,128)(2,1)S(1)}, u32[]{:S(2)}, u32[]{:S(2)}) collective-permute-start(bf16[192,128]{1,0:T(8,128)(2,1)} %get-tuple-element.63), channel_id=1, source_target_pairs={{0,8},{4,12},{8,0},{12,4},{1,9},{5,13},{9,1},{13,5},{2,10},{6,14},... | collective-permute-start | bytes 147464 | tf_op jit(solution)/shard_map/ppermute | solution.py:30
  112.5 1.4 copy-start.19
  112.5 11.5 %collective-permute-start.26 = (bf16[192,128]{1,0:T(8,128)(2,1)}, bf16[192,128]{1,0:T(8,128)(2,1)S(1)}, u32[]{:S(2)}, u32[]{:S(2)}) collective-permute-start(bf16[192,128]{1,0:T(8,128)(2,1)} %get-tuple-element.64), channel_id=1, source_target_pairs={{0,4},{4,8},{8,12},{12,0},{1,5},{5,9},{9,13},{13,1},{2,6},{6,10},{... | collective-permute-start | bytes 147464 | tf_op jit(solution)/shard_map/ppermute | solution.py:30
  116.0 2.0 %copy-start.18 = (bf16[384,128]{1,0:T(8,128)(2,1)}, bf16[384,128]{1,0:T(8,128)(2,1)S(1)}, u32[]{:S(2)}) copy-start(bf16[384,128]{1,0:T(8,128)(2,1)S(1)} %collective-permute-done.4.from_next) | copy-start | bytes 294916
  116.0 8.0 %collective-permute-start.16 = (bf16[192,128]{1,0:T(8,128)(2,1)}, bf16[192,128]{1,0:T(8,128)(2,1)S(1)}, u32[]{:S(2)}, u32[]{:S(2)}) collective-permute-start(bf16[192,128]{1,0:T(8,128)(2,1)} %get-tuple-element.52), channel_id=1, source_target_pairs={{0,12},{4,0},{8,4},{12,8},{1,13},{5,1},{9,5},{13,9},{2,14},{6,2},{... | collective-permute-start | bytes 147464 | tf_op jit(solution)/shard_map/ppermute | solution.py:30
  118.0 0.6 copy-start.20
  118.0 6.4 %collective-permute-start.17 = (bf16[192,128]{1,0:T(8,128)(2,1)}, bf16[192,128]{1,0:T(8,128)(2,1)S(1)}, u32[]{:S(2)}, u32[]{:S(2)}) collective-permute-start(bf16[192,128]{1,0:T(8,128)(2,1)} %get-tuple-element.53), channel_id=1, source_target_pairs={{0,8},{4,12},{8,0},{12,4},{1,9},{5,13},{9,1},{13,5},{2,10},{6,14},... | collective-permute-start | bytes 147464 | tf_op jit(solution)/shard_map/ppermute | solution.py:30
  120.7 5.6 %collective-permute-start.18 = (bf16[192,128]{1,0:T(8,128)(2,1)}, bf16[192,128]{1,0:T(8,128)(2,1)S(1)}, u32[]{:S(2)}, u32[]{:S(2)}) collective-permute-start(bf16[192,128]{1,0:T(8,128)(2,1)} %get-tuple-element.54), channel_id=1, source_target_pairs={{0,4},{4,8},{8,12},{12,0},{1,5},{5,9},{9,13},{13,1},{2,6},{6,10},{... | collective-permute-start | bytes 147464 | tf_op jit(solution)/shard_map/ppermute | solution.py:30
  120.7 5.5 %collective-permute-start.8 = (bf16[192,128]{1,0:T(8,128)(2,1)}, bf16[192,128]{1,0:T(8,128)(2,1)S(1)}, u32[]{:S(2)}, u32[]{:S(2)}) collective-permute-start(bf16[192,128]{1,0:T(8,128)(2,1)} %get-tuple-element.42), channel_id=1, source_target_pairs={{0,12},{4,0},{8,4},{12,8},{1,13},{5,1},{9,5},{13,9},{2,14},{6,2},{... | collective-permute-start | bytes 147464 | tf_op jit(solution)/shard_map/ppermute | solution.py:30
  124.0 6.1 %collective-permute-start.9 = (bf16[192,128]{1,0:T(8,128)(2,1)}, bf16[192,128]{1,0:T(8,128)(2,1)S(1)}, u32[]{:S(2)}, u32[]{:S(2)}) collective-permute-start(bf16[192,128]{1,0:T(8,128)(2,1)} %get-tuple-element.43), channel_id=1, source_target_pairs={{0,8},{4,12},{8,0},{12,4},{1,9},{5,13},{9,1},{13,5},{2,10},{6,14},... | collective-permute-start | bytes 147464 | tf_op jit(solution)/shard_map/ppermute | solution.py:30
  124.0 6.1 %collective-permute-start.10 = (bf16[192,128]{1,0:T(8,128)(2,1)}, bf16[192,128]{1,0:T(8,128)(2,1)S(1)}, u32[]{:S(2)}, u32[]{:S(2)}) collective-permute-start(bf16[192,128]{1,0:T(8,128)(2,1)} %get-tuple-element.44), channel_id=1, source_target_pairs={{0,4},{4,8},{8,12},{12,0},{1,5},{5,9},{9,13},{13,1},{2,6},{6,10},{... | collective-permute-start | bytes 147464 | tf_op jit(solution)/shard_map/ppermute | solution.py:30
  130.1 3.7 %copy-start = (bf16[1536,3072]{1,0:T(8,128)(2,1)S(1)}, bf16[1536,3072]{1,0:T(8,128)(2,1)}, u32[]{:S(2)}) copy-start(bf16[1536,3072]{1,0:T(8,128)(2,1)} %refs_12_.1) | copy-start | bytes 28311556
  133.8 0.8 copy-start.7
  134.6 0.8 copy-start.8
  135.4 0.8 copy-start.9
  (1 other events, 0.6 us)

commit v2 on v1

--- a/solution.py
+++ b/solution.py
@@ -15,9 +15,10 @@
 BLEND_TOTAL = 16.0
 SCALE = HEAD_DIM ** (-0.5)
 EXP2_SCALE = SCALE * math.log2(math.e)
-VMEM_LIMIT = 24 * 1024 * 1024
+SMALL = pltpu.CompilerParams(vmem_limit_bytes=16 * 1024 * 1024)
 
 ANY = pl.BlockSpec(memory_space=pl.ANY)
+HBM = pl.BlockSpec(memory_space=pltpu.HBM)
 VMEM = pl.BlockSpec(memory_space=pltpu.VMEM)
 
 
@@ -30,8 +31,8 @@
     return lax.ppermute(block, axis, route)
 
 
-def pack_kernel(chunk, group, head_count, *refs):
-    sources, packed, sems = refs[:5], refs[5 : 5 + group], refs[5 + group]
+def pack_kernel(chunk, group, head_count, count, *refs):
+    sources, packed, sems = refs[:count], refs[count : count + group], refs[count + group]
     position = lax.rem(lax.axis_index("seq"), group)
     copies = []
     for distance in range(group):
@@ -40,8 +41,11 @@
         row = 0
         for source in sources:
             rows = source.shape[0]
+            narrow = source.shape[1] == HEAD_DIM
             copy = pltpu.make_async_copy(
-                source.at[:, columns], packed[distance].at[pl.ds(row, rows)], sems.at[len(copies)]
+                source if narrow else source.at[:, columns],
+                packed[distance].at[pl.ds(row, rows)],
+                sems.at[len(copies)],
             )
             copy.start()
             copies.append(copy)
@@ -53,11 +57,12 @@
 def pack(sources, chunk, group, head_count):
     rows = sum(source.shape[0] for source in sources)
     return pl.pallas_call(
-        functools.partial(pack_kernel, chunk, group, head_count),
+        functools.partial(pack_kernel, chunk, group, head_count, len(sources)),
         out_shape=[jax.ShapeDtypeStruct((rows, HEAD_DIM), sources[0].dtype)] * group,
-        in_specs=[ANY] * len(sources),
-        out_specs=[ANY] * group,
+        in_specs=[HBM] * len(sources),
+        out_specs=[VMEM] * group,
         scratch_shapes=[pltpu.SemaphoreType.DMA((group * len(sources),))],
+        compiler_params=SMALL,
         name="pack",
     )(*sources)
 
@@ -113,7 +118,7 @@
         in_specs=[VMEM] * (1 + group),
         out_specs=[VMEM, VMEM],
         scratch_shapes=[keys, keys],
-        compiler_params=pltpu.CompilerParams(vmem_limit_bytes=VMEM_LIMIT),
+        compiler_params=SMALL,
         cost_estimate=pl.CostEstimate(
             flops=4 * query_count * key_count * HEAD_DIM,
             bytes_accessed=4 * key_count * HEAD_DIM * 2,
@@ -121,6 +126,34 @@
         ),
         name="attend",
     )(ids, *blocks)
+
+
+def weigh_kernel(group, weight_row, image_rows, *refs):
+    blocks, (weight_left, weight_right) = refs[:group], refs[group:]
+    half = image_rows // 2
+    for distance in range(group):
+        columns = blocks[distance][weight_row : weight_row + 16].astype(jnp.float32).T
+        for row in range(image_rows // WCOLS):
+            column, start = row * WCOLS // 128, row * WCOLS % 128
+            at = distance * half + row * STRIDE
+            for side, out in ((0, weight_left), (1, weight_right)):
+                first = start + side * STRIDE
+                out[at : at + STRIDE] = jnp.broadcast_to(
+                    columns[first : first + STRIDE, column : column + 1], (STRIDE, HEAD_DIM)
+                )
+
+
+def weigh(blocks, weight_row, image_rows):
+    group = len(blocks)
+    out = jax.ShapeDtypeStruct((group * image_rows // 2, HEAD_DIM), jnp.float32)
+    return pl.pallas_call(
+        functools.partial(weigh_kernel, group, weight_row, image_rows),
+        out_shape=[out, out],
+        in_specs=[VMEM] * group,
+        out_specs=[VMEM, VMEM],
+        compiler_params=SMALL,
+        name="weigh",
+    )(*blocks)
 
 
 def blend_kernel(group, left, right, from_prev, from_next, weight_left, weight_right, *outs):
@@ -145,54 +178,121 @@
         out_shape=[out] * group,
         in_specs=[VMEM] * 6,
         out_specs=[VMEM] * group,
+        compiler_params=SMALL,
         name="blend",
     )(left, right, from_prev, from_next, weight_left, weight_right)
 
 
-def project_kernel(group, head_count, *refs):
-    blocks, (w_out, out, features) = refs[: group * head_count], refs[group * head_count :]
-    image_rows = out.shape[0]
-
-    @pl.when(pl.program_id(0) == 0)
-    def _():
-        position = lax.rem(lax.axis_index("seq"), group)
-        for chunk in range(head_count):
-            for distance in range(group):
-                head = lax.rem(position + distance, group) * head_count + chunk
-                columns = pl.ds(pl.multiple_of(head * HEAD_DIM, HEAD_DIM), HEAD_DIM)
-                block = blocks[chunk * group + distance]
-                for row in range(image_rows // WCOLS):
-                    for side in range(2):
-                        start = side * image_rows // 2 + row * STRIDE
-                        features[pl.ds(row * WCOLS + side * STRIDE, STRIDE), columns] = block[
-                            start : start + STRIDE
-                        ]
-
-    out[...] = jnp.dot(features[...], w_out[...], preferred_element_type=jnp.float32).astype(
-        jnp.bfloat16
-    )
-
-
-def project(blocks, w_out, group, head_count):
-    image_rows = blocks[0].shape[0]
-    depth, width = w_out.shape
-    tile = width // 6
-    return pl.pallas_call(
-        functools.partial(project_kernel, group, head_count),
-        grid=(width // tile,),
+def load_kernel(group, head_count, w_out, *refs):
+    outs, sems = refs[:head_count], refs[head_count]
+    copies = []
+    for chunk in range(head_count):
+        for source in range(group):
+            head = source * head_count + chunk
+            copy = pltpu.make_async_copy(
+                w_out.at[pl.ds(head * HEAD_DIM, HEAD_DIM)],
+                outs[chunk].at[pl.ds(source * HEAD_DIM, HEAD_DIM)],
+                sems.at[len(copies)],
+            )
+            copy.start()
+            copies.append(copy)
+    for copy in copies:
+        copy.wait()
+
+
+def load_weights(w_out, group, head_count):
+    out = jax.ShapeDtypeStruct((group * HEAD_DIM, w_out.shape[1]), w_out.dtype)
+    return pl.pallas_call(
+        functools.partial(load_kernel, group, head_count),
+        out_shape=[out] * head_count,
+        in_specs=[ANY],
+        out_specs=[VMEM] * head_count,
+        scratch_shapes=[pltpu.SemaphoreType.DMA((group * head_count,))],
+        compiler_params=SMALL,
+        name="load_weights",
+    )(w_out)
+
+
+def gather_features(blocks, features):
+    group, image_rows = len(blocks), features.shape[0]
+    position = lax.rem(lax.axis_index("seq"), group)
+    for distance, block in enumerate(blocks):
+        source = lax.rem(position + distance, group)
+        columns = pl.ds(pl.multiple_of(source * HEAD_DIM, HEAD_DIM), HEAD_DIM)
+        for row in range(image_rows // WCOLS):
+            for side in range(2):
+                start = side * image_rows // 2 + row * STRIDE
+                at = row * WCOLS + side * STRIDE
+                features[pl.ds(at, STRIDE), columns] = block[start : start + STRIDE]
+
+
+def begin_kernel(group, count, *refs):
+    blocks, weights = refs[: group * count], refs[group * count : (group + 1) * count]
+    total = refs[(group + 1) * count]
+    features = refs[(group + 1) * count + 1 :]
+    for chunk in range(count):
+        gather_features(blocks[chunk * group : (chunk + 1) * group], features[chunk])
+    tile = total.shape[1] // 6
+    for at in range(0, total.shape[1], tile):
+        total[:, at : at + tile] = sum(
+            jnp.dot(
+                features[chunk][...],
+                weights[chunk][:, at : at + tile],
+                preferred_element_type=jnp.float32,
+            )
+            for chunk in range(count)
+        )
+
+
+def project_begin(blocks, weights, group):
+    image_rows, width = blocks[0].shape[0], weights[0].shape[1]
+    count = len(weights)
+    return pl.pallas_call(
+        functools.partial(begin_kernel, group, count),
+        out_shape=jax.ShapeDtypeStruct((image_rows, width), jnp.float32),
+        in_specs=[VMEM] * (len(blocks) + count),
+        out_specs=VMEM,
+        scratch_shapes=[pltpu.VMEM((image_rows, group * HEAD_DIM), jnp.bfloat16)] * count,
+        compiler_params=SMALL,
+        name="project_begin",
+    )(*blocks, *weights)
+
+
+def end_kernel(group, *refs):
+    blocks, (weights, total, out, features, result, sems) = refs[:group], refs[group:]
+    gather_features(blocks, features)
+    tile = result.shape[1] // 6
+    copies = []
+    for at in range(0, result.shape[1], tile):
+        columns = pl.ds(at, tile)
+        product = jnp.dot(
+            features[...], weights[:, columns], preferred_element_type=jnp.float32
+        )
+        result[:, columns] = (total[:, columns] + product).astype(jnp.bfloat16)
+        copy = pltpu.make_async_copy(
+            result.at[:, columns], out.at[:, columns], sems.at[len(copies)]
+        )
+        copy.start()
+        copies.append(copy)
+    for copy in copies:
+        copy.wait()
+
+
+def project_end(blocks, weights, total, group):
+    image_rows, width = total.shape
+    return pl.pallas_call(
+        functools.partial(end_kernel, group),
         out_shape=jax.ShapeDtypeStruct((image_rows, width), jnp.bfloat16),
-        in_specs=[pl.BlockSpec((image_rows, HEAD_DIM), lambda n: (0, 0))] * len(blocks)
-        + [pl.BlockSpec((depth, tile), lambda n: (0, n))],
-        out_specs=pl.BlockSpec((image_rows, tile), lambda n: (0, n)),
-        scratch_shapes=[pltpu.VMEM((image_rows, depth), jnp.bfloat16)],
-        compiler_params=pltpu.CompilerParams(vmem_limit_bytes=VMEM_LIMIT),
-        cost_estimate=pl.CostEstimate(
-            flops=2 * image_rows * depth * width,
-            bytes_accessed=2 * (depth * width + image_rows * (depth + width)),
-            transcendentals=0,
-        ),
-        name="project",
-    )(*blocks, w_out)
+        in_specs=[VMEM] * (len(blocks) + 2),
+        out_specs=ANY,
+        scratch_shapes=[
+            pltpu.VMEM((image_rows, group * HEAD_DIM), jnp.bfloat16),
+            pltpu.VMEM((image_rows, width), jnp.bfloat16),
+            pltpu.SemaphoreType.DMA((6,)),
+        ],
+        compiler_params=SMALL,
+        name="project_end",
+    )(*blocks, weights, total)
 
 
 def absorb(carried, keys, values, valid_keys, queries):
@@ -263,32 +363,39 @@
     image_rows, text_rows = query.shape[1], key_text.shape[1]
     sources = [query[0], key_image[0], key_text[0], value_image[0], value_text[0]]
 
+    weight_rows = -(-image_rows // (16 * 128)) * 16
+    weight_block = jnp.pad(
+        blend[0].astype(jnp.bfloat16), (0, weight_rows * 128 - image_rows)
+    ).reshape(weight_rows, 128)
+    weight_chunk = min(1, head_count - 1)
+    message_rows = 3 * image_rows + 2 * text_rows
+
     blocks = []
     for chunk in range(head_count):
-        packed = pack(sources, chunk, group, head_count)
+        extra = [weight_block] if chunk == weight_chunk else []
+        packed = pack(sources + extra, chunk, group, head_count)
         blocks.append(
             [packed[0]] + [shifted(packed[d], "seq", d, group) for d in range(1, group)]
         )
-
-    weights = jnp.concatenate(
-        [blend] + [shifted(blend, "seq", d, group) for d in range(1, group)], axis=0
-    )
-    weights = weights.astype(jnp.float32).reshape(-1, 2, STRIDE)
-    weight_left, weight_right = (weights[:, side].reshape(-1, 1) for side in range(2))
+    w_chunks = load_weights(w_out, group, head_count)
+    weight_left, weight_right = weigh(blocks[weight_chunk], message_rows, image_rows)
 
     if seq_count == group:
         strips = [attend(chunk, prompt_ids, image_rows, text_rows) for chunk in blocks]
     else:
-        strips = attend_ring(blocks, prompt_ids[0], image_rows, text_rows)
+        trimmed = [[block[:message_rows] for block in chunk] for chunk in blocks]
+        strips = attend_ring(trimmed, prompt_ids[0], image_rows, text_rows)
 
     features = []
     for left, right in strips:
         from_prev = shifted(right, "win", 1, win_count)
         from_next = shifted(left, "win", -1, win_count)
         mixed = blend_strips(left, right, from_prev, from_next, weight_left, weight_right, group)
-        features.append(mixed[0])
-        features += [shifted(mixed[d], "seq", -d, group) for d in range(1, group)]
-    return project(features, w_out, group, head_count)[None]
+        features.append(
+            [mixed[0]] + [shifted(mixed[d], "seq", -d, group) for d in range(1, group)]
+        )
+    total = project_begin(sum(features[:-1], []), w_chunks[:-1], group)
+    return project_end(features[-1], w_chunks[-1], total, group)[None]
 
 
 def solution(mesh):

time: 142 us -> 74 us (0.52)
  Pallas kernels: 76.6 us -> 10.7 us
  local copies, waits for them, and re-layouts: 13.9 us -> 4.82 us
  waiting for transfers between devices: 13 us -> 18.4 us
  starting transfers between devices: 36.2 us -> 37.7 us
    pallas_call x4 -> x7, Pallas kernels: 65 us -> 5.05 us  [the longest x1 1.54 us: project_end(): pl.pallas_call(functools.partial(end_kernel, group), out_shape=jax.ShapeD...]
    unnamed x44 -> x14, local copies, waits for them, and re-layouts: 12 us -> 4.81 us
    pallas_call x3, Pallas kernels: 6.31 us -> 0.3 us  [blend_strips(): pl.pallas_call(functools.partial(blend_kernel, group), out_shape=[out] *...]
    ppermute x27 -> x24, waiting for transfers between devices: 13 us -> 18.4 us  [shifted(): return lax.ppermute(block, axis, route)]
    another operation x2 -> x0, local copies, waits for them, and re-layouts: 1.74 us -> none  [on_device(): weights[:, side].reshape(-1, 1)]
    ppermute x27 -> x24, starting transfers between devices: 36.2 us -> 37.7 us  [shifted(): return lax.ppermute(block, axis, route)]
  transfers between devices with their start and end apart: 27 -> 24, of which waited for: 5 -> 6; matrix products, arithmetic and copies ran while one was open for 2% -> 1% of each run, Pallas kernels for 37% -> 12%
where the time goes in v2:
time: 74 us; the launch traced here: 72.5 us
  starting transfers between devices  37.7 us (51%)
  waiting for transfers between devices  18.4 us (25%)
  Pallas kernels  10.7 us (14%)
  local copies, waits for them, and re-layouts  4.82 us (7%)
    ppermute x24, starting transfers between devices, shifted(): return lax.ppermute(block, axis, route)  37.7 us
    ppermute x24, waiting for transfers between devices, shifted(): return lax.ppermute(block, axis, route)  18.4 us
    pallas_call x3, Pallas kernels, attend(): pl.pallas_call(functools.partial(attend_kernel, group, image_rows, text_r...  5.34 us
    unnamed x14, local copies, waits for them, and re-layouts  4.81 us
    pallas_call x1, Pallas kernels, project_end(): pl.pallas_call(functools.partial(end_kernel, group), out_shape=jax.ShapeD...  1.54 us
  transfers between devices with their start and end apart: 24, of which 6 were waited for; matrix products, arithmetic and copies ran while one was open for 1% of the time, Pallas kernels for 12%

profile of v2, /device:TPU:1, one launch (start us, length us, event | category | flops | bytes accessed | tf_op | source)
XLA Modules:
  0.0 72.5 jit_solution(6206071289419630144)
XLA Ops:
  0.0 1.1 %copy-done.1 = bf16[1,192,1536]{2,1,0:T(8,128)(2,1)S(1)} copy-done((bf16[1,192,1536]{2,1,0:T(8,128)(2,1)S(1)}, bf16[1,192,1536]{2,1,0:T(8,128)(2,1)}, u32[]{:S(2)}) %copy-start.1) | copy-done | bytes 589848
  1.1 1.1 %copy-done.2 = bf16[1,192,1536]{2,1,0:T(8,128)(2,1)S(1)} copy-done((bf16[1,192,1536]{2,1,0:T(8,128)(2,1)S(1)}, bf16[1,192,1536]{2,1,0:T(8,128)(2,1)}, u32[]{:S(2)}) %copy-start.2) | copy-done | bytes 589848
  2.1 1.1 %copy-done.3 = bf16[1,192,1536]{2,1,0:T(8,128)(2,1)S(1)} copy-done((bf16[1,192,1536]{2,1,0:T(8,128)(2,1)S(1)}, bf16[1,192,1536]{2,1,0:T(8,128)(2,1)}, u32[]{:S(2)}) %copy-start.3) | copy-done | bytes 589848
  3.2 0.8 %copy-done.4 = bf16[1,16,1536]{2,1,0:T(8,128)(2,1)S(1)} copy-done((bf16[1,16,1536]{2,1,0:T(8,128)(2,1)S(1)}, bf16[1,16,1536]{2,1,0:T(8,128)(2,1)}, u32[]{:S(2)}) %copy-start.4) | copy-done | bytes 49176
  4.0 0.8 %copy-done.5 = bf16[1,16,1536]{2,1,0:T(8,128)(2,1)S(1)} copy-done((bf16[1,16,1536]{2,1,0:T(8,128)(2,1)S(1)}, bf16[1,16,1536]{2,1,0:T(8,128)(2,1)}, u32[]{:S(2)}) %copy-start.5) | copy-done | bytes 49176
  4.8 0.3 pack.5
  5.2 2.2 %collective-permute-start.11 = (bf16[608,128]{1,0:T(8,128)(2,1)S(1)}, bf16[608,128]{1,0:T(8,128)(2,1)S(1)}, u32[]{:S(2)}, u32[]{:S(2)}) collective-permute-start(bf16[608,128]{1,0:T(8,128)(2,1)S(1)} %get-tuple-element.58), channel_id=1, source_target_pairs={{0,4},{4,8},{8,12},{12,0},{1,5},{5,9},{9,13},{13,1},{2,6},{6,10},{... | collective-permute-start | bytes 466952 | tf_op jit(solution)/shard_map/ppermute | solution.py:31
  7.3 0.7 convert_reduce_fusion
  8.1 0.0 copy-start
  8.1 0.4 pack.4
  8.5 1.3 %collective-permute-start.5 = (bf16[624,128]{1,0:T(8,128)(2,1)S(1)}, bf16[624,128]{1,0:T(8,128)(2,1)S(1)}, u32[]{:S(2)}, u32[]{:S(2)}) collective-permute-start(bf16[624,128]{1,0:T(8,128)(2,1)S(1)} %get-tuple-element.47), channel_id=1, source_target_pairs={{0,4},{4,8},{8,12},{12,0},{1,5},{5,9},{9,13},{13,1},{2,6},{6,10},{... | collective-permute-start | bytes 479240 | tf_op jit(solution)/shard_map/ppermute | solution.py:31
  9.9 1.1 %collective-permute-start.12 = (bf16[608,128]{1,0:T(8,128)(2,1)S(1)}, bf16[608,128]{1,0:T(8,128)(2,1)S(1)}, u32[]{:S(2)}, u32[]{:S(2)}) collective-permute-start(bf16[608,128]{1,0:T(8,128)(2,1)S(1)} %get-tuple-element.59), channel_id=1, source_target_pairs={{0,8},{4,12},{8,0},{12,4},{1,9},{5,13},{9,1},{13,5},{2,10},{6,14},... | collective-permute-start | bytes 466952 | tf_op jit(solution)/shard_map/ppermute | solution.py:31
  11.0 2.3 %collective-permute-start.13 = (bf16[608,128]{1,0:T(8,128)(2,1)S(1)}, bf16[608,128]{1,0:T(8,128)(2,1)S(1)}, u32[]{:S(2)}, u32[]{:S(2)}) collective-permute-start(bf16[608,128]{1,0:T(8,128)(2,1)S(1)} %get-tuple-element.60), channel_id=1, source_target_pairs={{0,12},{4,0},{8,4},{12,8},{1,13},{5,1},{9,5},{13,9},{2,14},{6,2},{... | collective-permute-start | bytes 466952 | tf_op jit(solution)/shard_map/ppermute | solution.py:31
  13.2 0.1 collective-permute-start.6
  13.3 1.2 %collective-permute-start.7 = (bf16[624,128]{1,0:T(8,128)(2,1)S(1)}, bf16[624,128]{1,0:T(8,128)(2,1)S(1)}, u32[]{:S(2)}, u32[]{:S(2)}) collective-permute-start(bf16[624,128]{1,0:T(8,128)(2,1)S(1)} %get-tuple-element.49), channel_id=1, source_target_pairs={{0,12},{4,0},{8,4},{12,8},{1,13},{5,1},{9,5},{13,9},{2,14},{6,2},{... | collective-permute-start | bytes 479240 | tf_op jit(solution)/shard_map/ppermute | solution.py:31
  14.5 0.3 pack.3
  14.9 9.9 %collective-permute-done.12.refs_2_ = bf16[608,128]{1,0:T(8,128)(2,1)S(1)} collective-permute-done((bf16[608,128]{1,0:T(8,128)(2,1)S(1)}, bf16[608,128]{1,0:T(8,128)(2,1)S(1)}, u32[]{:S(2)}, u32[]{:S(2)}) %collective-permute-start.12) | collective-permute-done | bytes 155680 | tf_op jit(solution)/shard_map/ppermute | solution.py:31
  24.8 7.2 %collective-permute-start = (bf16[608,128]{1,0:T(8,128)(2,1)S(1)}, bf16[608,128]{1,0:T(8,128)(2,1)S(1)}, u32[]{:S(2)}, u32[]{:S(2)}) collective-permute-start(bf16[608,128]{1,0:T(8,128)(2,1)S(1)} %get-tuple-element.41), channel_id=1, source_target_pairs={{0,4},{4,8},{8,12},{12,0},{1,5},{5,9},{9,13},{13,1},{2,6},{6,10},{... | collective-permute-start | bytes 466952 | tf_op jit(solution)/shard_map/ppermute | solution.py:31
  32.0 3.1 %collective-permute-start.1 = (bf16[608,128]{1,0:T(8,128)(2,1)S(1)}, bf16[608,128]{1,0:T(8,128)(2,1)S(1)}, u32[]{:S(2)}, u32[]{:S(2)}) collective-permute-start(bf16[608,128]{1,0:T(8,128)(2,1)S(1)} %get-tuple-element.42), channel_id=1, source_target_pairs={{0,8},{4,12},{8,0},{12,4},{1,9},{5,13},{9,1},{13,5},{2,10},{6,14},... | collective-permute-start | bytes 466952 | tf_op jit(solution)/shard_map/ppermute | solution.py:31
  35.1 1.8 %attend.4 = (bf16[384,128]{1,0:T(8,128)(2,1)S(1)}, bf16[384,128]{1,0:T(8,128)(2,1)S(1)}) custom-call(s32[1,64]{1,0:T(1,128)S(1)} %copy-done.6, bf16[608,128]{1,0:T(8,128)(2,1)S(1)} %get-tuple-element.57.refs_0_, bf16[608,128]{1,0:T(8,128)(2,1)S(1)} %collective-permute-done.11.refs_1_, bf16[608,128]{1,0:T(8,128)(2,1)S(1)} %collective-permute-done.12.refs_2_, ...), custom_call_target="tpu_custom_call" | custom-call | flops 327155712 | bytes 851968 | tf_op jit(solution)/shard_map/attend/pallas_call | solution.py:115
  36.9 2.5 %collective-permute-start.15 = (bf16[384,128]{1,0:T(8,128)(2,1)S(1)}, bf16[384,128]{1,0:T(8,128)(2,1)S(1)}, u32[]{:S(2)}, u32[]{:S(2)}) collective-permute-start(bf16[384,128]{1,0:T(8,128)(2,1)S(1)} %get-tuple-element.61.left), channel_id=1, source_target_pairs={{0,3},{1,0},{2,1},{3,2},{4,7},{5,4},{6,5},{7,6},{8,11},{9,8},{10,9... | collective-permute-start | bytes 294920 | tf_op jit(solution)/shard_map/ppermute | solution.py:31
  39.4 1.2 %collective-permute-start.14 = (bf16[384,128]{1,0:T(8,128)(2,1)S(1)}, bf16[384,128]{1,0:T(8,128)(2,1)S(1)}, u32[]{:S(2)}, u32[]{:S(2)}) collective-permute-start(bf16[384,128]{1,0:T(8,128)(2,1)S(1)} %get-tuple-element.62.right), channel_id=1, source_target_pairs={{0,1},{1,2},{2,3},{3,0},{4,5},{5,6},{6,7},{7,4},{8,9},{9,10},{10,1... | collective-permute-start | bytes 294920 | tf_op jit(solution)/shard_map/ppermute | solution.py:31
  40.6 1.8 %attend.5 = (bf16[384,128]{1,0:T(8,128)(2,1)S(1)}, bf16[384,128]{1,0:T(8,128)(2,1)S(1)}) custom-call(s32[1,64]{1,0:T(1,128)S(1)} %copy-done.6, bf16[624,128]{1,0:T(8,128)(2,1)S(1)} %get-tuple-element.46.refs_0_, bf16[624,128]{1,0:T(8,128)(2,1)S(1)} %collective-permute-done.5.refs_1_, bf16[624,128]{1,0:T(8,128)(2,1)S(1)} %collective-permute-done.6.refs_2_, ...), custom_call_target="tpu_custom_call" | custom-call | flops 327155712 | bytes 851968 | tf_op jit(solution)/shard_map/attend/pallas_call | solution.py:115
  42.4 0.1 collective-permute-start.20
  42.5 5.2 %collective-permute-done.1.refs_2_ = bf16[608,128]{1,0:T(8,128)(2,1)S(1)} collective-permute-done((bf16[608,128]{1,0:T(8,128)(2,1)S(1)}, bf16[608,128]{1,0:T(8,128)(2,1)S(1)}, u32[]{:S(2)}, u32[]{:S(2)}) %collective-permute-start.1) | collective-permute-done | bytes 155680 | tf_op jit(solution)/shard_map/ppermute | solution.py:31
  47.6 1.7 %collective-permute-start.19 = (bf16[384,128]{1,0:T(8,128)(2,1)S(1)}, bf16[384,128]{1,0:T(8,128)(2,1)S(1)}, u32[]{:S(2)}, u32[]{:S(2)}) collective-permute-start(bf16[384,128]{1,0:T(8,128)(2,1)S(1)} %get-tuple-element.68.right), channel_id=1, source_target_pairs={{0,1},{1,2},{2,3},{3,0},{4,5},{5,6},{6,7},{7,4},{8,9},{9,10},{10,1... | collective-permute-start | bytes 294920 | tf_op jit(solution)/shard_map/ppermute | solution.py:31
  49.3 1.8 %attend.3 = (bf16[384,128]{1,0:T(8,128)(2,1)S(1)}, bf16[384,128]{1,0:T(8,128)(2,1)S(1)}) custom-call(s32[1,64]{1,0:T(1,128)S(1)} %copy-done.6, bf16[608,128]{1,0:T(8,128)(2,1)S(1)} %get-tuple-element.40.refs_0_, bf16[608,128]{1,0:T(8,128)(2,1)S(1)} %collective-permute-done.refs_1_, bf16[608,128]{1,0:T(8,128)(2,1)S(1)} %collective-permute-done.1.refs_2_, ...), custom_call_target="tpu_custom_call" | custom-call | flops 327155712 | bytes 851968 | tf_op jit(solution)/shard_map/attend/pallas_call | solution.py:115
  51.1 0.1 collective-permute-start.4
  51.2 1.7 %collective-permute-start.3 = (bf16[384,128]{1,0:T(8,128)(2,1)S(1)}, bf16[384,128]{1,0:T(8,128)(2,1)S(1)}, u32[]{:S(2)}, u32[]{:S(2)}) collective-permute-start(bf16[384,128]{1,0:T(8,128)(2,1)S(1)} %get-tuple-element.45.right), channel_id=1, source_target_pairs={{0,1},{1,2},{2,3},{3,0},{4,5},{5,6},{6,7},{7,4},{8,9},{9,10},{10,1... | collective-permute-start | bytes 294920 | tf_op jit(solution)/shard_map/ppermute | solution.py:31
  52.9 0.2 weigh.1
  53.1 0.1 blend.4
  53.2 4.6 %collective-permute-start.16 = (bf16[192,128]{1,0:T(8,128)(2,1)S(1)}, bf16[192,128]{1,0:T(8,128)(2,1)S(1)}, u32[]{:S(2)}, u32[]{:S(2)}) collective-permute-start(bf16[192,128]{1,0:T(8,128)(2,1)S(1)} %get-tuple-element.64), channel_id=1, source_target_pairs={{0,12},{4,0},{8,4},{12,8},{1,13},{5,1},{9,5},{13,9},{2,14},{6,2},{... | collective-permute-start | bytes 147464 | tf_op jit(solution)/shard_map/ppermute | solution.py:31
  57.8 0.4 collective-permute-start.18
  58.2 0.1 blend.5
  58.3 3.0 %collective-permute-start.21 = (bf16[192,128]{1,0:T(8,128)(2,1)S(1)}, bf16[192,128]{1,0:T(8,128)(2,1)S(1)}, u32[]{:S(2)}, u32[]{:S(2)}) collective-permute-start(bf16[192,128]{1,0:T(8,128)(2,1)S(1)} %get-tuple-element.70), channel_id=1, source_target_pairs={{0,12},{4,0},{8,4},{12,8},{1,13},{5,1},{9,5},{13,9},{2,14},{6,2},{... | collective-permute-start | bytes 147464 | tf_op jit(solution)/shard_map/ppermute | solution.py:31
  61.3 0.1 blend.3
  61.4 0.6 collective-permute-start.22
  62.0 0.0 collective-permute-start.23
  62.0 0.1 collective-permute-done.17.refs_2_
  62.1 3.1 %collective-permute-start.8 = (bf16[192,128]{1,0:T(8,128)(2,1)S(1)}, bf16[192,128]{1,0:T(8,128)(2,1)S(1)}, u32[]{:S(2)}, u32[]{:S(2)}) collective-permute-start(bf16[192,128]{1,0:T(8,128)(2,1)S(1)} %get-tuple-element.53), channel_id=1, source_target_pairs={{0,12},{4,0},{8,4},{12,8},{1,13},{5,1},{9,5},{13,9},{2,14},{6,2},{... | collective-permute-start | bytes 147464 | tf_op jit(solution)/shard_map/ppermute | solution.py:31
  65.3 0.1 collective-permute-start.9
  65.3 0.3 collective-permute-start.10
  65.6 0.8 %load_weights.1 = (bf16[512,3072]{1,0:T(8,128)(2,1)S(1)}, bf16[512,3072]{1,0:T(8,128)(2,1)S(1)}, bf16[512,3072]{1,0:T(8,128)(2,1)S(1)}) custom-call(bf16[1536,3072]{1,0:T(8,128)(2,1)S(1)} %copy-done), custom_call_target="tpu_custom_call" | custom-call | tf_op jit(solution)/shard_map/load_weights/pallas_call | solution.py:205
  66.4 0.4 collective-permute-done.23.refs_7_
  66.8 1.4 %project_begin.1.refs_5_ = f32[192,3072]{1,0:T(8,128)S(1)} custom-call(bf16[192,128]{1,0:T(8,128)(2,1)S(1)} %get-tuple-element.63.refs_0_, bf16[192,128]{1,0:T(8,128)(2,1)S(1)} %collective-permute-done.16.refs_1_, bf16[192,128]{1,0:T(8,128)(2,1)S(1)} %collective-permute-done.17.refs_2_, bf16[192,128]{1,0:T(8,128)(2,1)S(1)} %collective-permute-done.18.refs_3_, ...), custom_call_target="tpu_custom_call" | custom-call | tf_op jit(solution)/shard_map/project_begin/pallas_call | solution.py:250
  68.2 0.2 collective-permute-done.8.refs_1_
  68.4 2.6 %collective-permute-done.9.refs_2_ = bf16[192,128]{1,0:T(8,128)(2,1)S(1)} collective-permute-done((bf16[192,128]{1,0:T(8,128)(2,1)S(1)}, bf16[192,128]{1,0:T(8,128)(2,1)S(1)}, u32[]{:S(2)}, u32[]{:S(2)}) %collective-permute-start.9) | collective-permute-done | bytes 49184 | tf_op jit(solution)/shard_map/ppermute | solution.py:31
  71.0 1.5 %project_end.1 = bf16[192,3072]{1,0:T(8,128)(2,1)} custom-call(bf16[192,128]{1,0:T(8,128)(2,1)S(1)} %get-tuple-element.52.refs_0_, bf16[192,128]{1,0:T(8,128)(2,1)S(1)} %collective-permute-done.8.refs_1_, bf16[192,128]{1,0:T(8,128)(2,1)S(1)} %collective-permute-done.9.refs_2_, bf16[192,128]{1,0:T(8,128)(2,1)S(1)} %collective-permute-done.10.refs_3_, ...), custom_call_target="tpu_custom_call" | custom-call | tf_op jit(solution)/shard_map/project_end/pallas_call | solution.py:283
  (29 shorter events, 0.1 us)
Async XLA Ops:
  0.0 35.1 %copy-start.6 = (s32[1,64]{1,0:T(1,128)S(1)}, s32[1,64]{1,0:T(1,128)}, u32[]{:S(2)}) copy-start(s32[1,64]{1,0:T(1,128)} %ids.5) | copy-start | bytes 772
  0.0 1.1 %copy-start.1 = (bf16[1,192,1536]{2,1,0:T(8,128)(2,1)S(1)}, bf16[1,192,1536]{2,1,0:T(8,128)(2,1)}, u32[]{:S(2)}) copy-start(bf16[1,192,1536]{2,1,0:T(8,128)(2,1)} %param.8) | copy-start | bytes 1769476
  1.1 1.1 %copy-start.2 = (bf16[1,192,1536]{2,1,0:T(8,128)(2,1)S(1)}, bf16[1,192,1536]{2,1,0:T(8,128)(2,1)}, u32[]{:S(2)}) copy-start(bf16[1,192,1536]{2,1,0:T(8,128)(2,1)} %param.9) | copy-start | bytes 1769476
  2.1 1.1 %copy-start.3 = (bf16[1,192,1536]{2,1,0:T(8,128)(2,1)S(1)}, bf16[1,192,1536]{2,1,0:T(8,128)(2,1)}, u32[]{:S(2)}) copy-start(bf16[1,192,1536]{2,1,0:T(8,128)(2,1)} %param.10) | copy-start | bytes 1769476
  3.2 0.8 %copy-start.4 = (bf16[1,16,1536]{2,1,0:T(8,128)(2,1)S(1)}, bf16[1,16,1536]{2,1,0:T(8,128)(2,1)}, u32[]{:S(2)}) copy-start(bf16[1,16,1536]{2,1,0:T(8,128)(2,1)} %param.11) | copy-start | bytes 147460
  4.0 0.8 %copy-start.5 = (bf16[1,16,1536]{2,1,0:T(8,128)(2,1)S(1)}, bf16[1,16,1536]{2,1,0:T(8,128)(2,1)}, u32[]{:S(2)}) copy-start(bf16[1,16,1536]{2,1,0:T(8,128)(2,1)} %param.12) | copy-start | bytes 147460
  5.2 8.1 %collective-permute-start.11 = (bf16[608,128]{1,0:T(8,128)(2,1)S(1)}, bf16[608,128]{1,0:T(8,128)(2,1)S(1)}, u32[]{:S(2)}, u32[]{:S(2)}) collective-permute-start(bf16[608,128]{1,0:T(8,128)(2,1)S(1)} %get-tuple-element.58), channel_id=1, source_target_pairs={{0,4},{4,8},{8,12},{12,0},{1,5},{5,9},{9,13},{13,1},{2,6},{6,10},{... | collective-permute-start | bytes 466952 | tf_op jit(solution)/shard_map/ppermute | solution.py:31
  8.1 57.6 %copy-start = (bf16[1536,3072]{1,0:T(8,128)(2,1)S(1)}, bf16[1536,3072]{1,0:T(8,128)(2,1)}, u32[]{:S(2)}) copy-start(bf16[1536,3072]{1,0:T(8,128)(2,1)} %w_out.1) | copy-start | bytes 28311556
  8.5 26.6 %collective-permute-start.5 = (bf16[624,128]{1,0:T(8,128)(2,1)S(1)}, bf16[624,128]{1,0:T(8,128)(2,1)S(1)}, u32[]{:S(2)}, u32[]{:S(2)}) collective-permute-start(bf16[624,128]{1,0:T(8,128)(2,1)S(1)} %get-tuple-element.47), channel_id=1, source_target_pairs={{0,4},{4,8},{8,12},{12,0},{1,5},{5,9},{9,13},{13,1},{2,6},{6,10},{... | collective-permute-start | bytes 479240 | tf_op jit(solution)/shard_map/ppermute | solution.py:31
  9.9 14.9 %collective-permute-start.12 = (bf16[608,128]{1,0:T(8,128)(2,1)S(1)}, bf16[608,128]{1,0:T(8,128)(2,1)S(1)}, u32[]{:S(2)}, u32[]{:S(2)}) collective-permute-start(bf16[608,128]{1,0:T(8,128)(2,1)S(1)} %get-tuple-element.59), channel_id=1, source_target_pairs={{0,8},{4,12},{8,0},{12,4},{1,9},{5,13},{9,1},{13,5},{2,10},{6,14},... | collective-permute-start | bytes 466952 | tf_op jit(solution)/shard_map/ppermute | solution.py:31
  11.0 21.0 %collective-permute-start.13 = (bf16[608,128]{1,0:T(8,128)(2,1)S(1)}, bf16[608,128]{1,0:T(8,128)(2,1)S(1)}, u32[]{:S(2)}, u32[]{:S(2)}) collective-permute-start(bf16[608,128]{1,0:T(8,128)(2,1)S(1)} %get-tuple-element.60), channel_id=1, source_target_pairs={{0,12},{4,0},{8,4},{12,8},{1,13},{5,1},{9,5},{13,9},{2,14},{6,2},{... | collective-permute-start | bytes 466952 | tf_op jit(solution)/shard_map/ppermute | solution.py:31
  13.2 23.6 %collective-permute-start.6 = (bf16[624,128]{1,0:T(8,128)(2,1)S(1)}, bf16[624,128]{1,0:T(8,128)(2,1)S(1)}, u32[]{:S(2)}, u32[]{:S(2)}) collective-permute-start(bf16[624,128]{1,0:T(8,128)(2,1)S(1)} %get-tuple-element.48), channel_id=1, source_target_pairs={{0,8},{4,12},{8,0},{12,4},{1,9},{5,13},{9,1},{13,5},{2,10},{6,14},... | collective-permute-start | bytes 479240 | tf_op jit(solution)/shard_map/ppermute | solution.py:31
  13.3 26.1 %collective-permute-start.7 = (bf16[624,128]{1,0:T(8,128)(2,1)S(1)}, bf16[624,128]{1,0:T(8,128)(2,1)S(1)}, u32[]{:S(2)}, u32[]{:S(2)}) collective-permute-start(bf16[624,128]{1,0:T(8,128)(2,1)S(1)} %get-tuple-element.49), channel_id=1, source_target_pairs={{0,12},{4,0},{8,4},{12,8},{1,13},{5,1},{9,5},{13,9},{2,14},{6,2},{... | collective-permute-start | bytes 479240 | tf_op jit(solution)/shard_map/ppermute | solution.py:31
  24.8 17.6 %collective-permute-start = (bf16[608,128]{1,0:T(8,128)(2,1)S(1)}, bf16[608,128]{1,0:T(8,128)(2,1)S(1)}, u32[]{:S(2)}, u32[]{:S(2)}) collective-permute-start(bf16[608,128]{1,0:T(8,128)(2,1)S(1)} %get-tuple-element.41), channel_id=1, source_target_pairs={{0,4},{4,8},{8,12},{12,0},{1,5},{5,9},{9,13},{13,1},{2,6},{6,10},{... | collective-permute-start | bytes 466952 | tf_op jit(solution)/shard_map/ppermute | solution.py:31
  32.0 15.7 %collective-permute-start.1 = (bf16[608,128]{1,0:T(8,128)(2,1)S(1)}, bf16[608,128]{1,0:T(8,128)(2,1)S(1)}, u32[]{:S(2)}, u32[]{:S(2)}) collective-permute-start(bf16[608,128]{1,0:T(8,128)(2,1)S(1)} %get-tuple-element.42), channel_id=1, source_target_pairs={{0,8},{4,12},{8,0},{12,4},{1,9},{5,13},{9,1},{13,5},{2,10},{6,14},... | collective-permute-start | bytes 466952 | tf_op jit(solution)/shard_map/ppermute | solution.py:31
  35.1 14.2 %collective-permute-start.2 = (bf16[608,128]{1,0:T(8,128)(2,1)S(1)}, bf16[608,128]{1,0:T(8,128)(2,1)S(1)}, u32[]{:S(2)}, u32[]{:S(2)}) collective-permute-start(bf16[608,128]{1,0:T(8,128)(2,1)S(1)} %get-tuple-element.43), channel_id=1, source_target_pairs={{0,12},{4,0},{8,4},{12,8},{1,13},{5,1},{9,5},{13,9},{2,14},{6,2},{... | collective-permute-start | bytes 466952 | tf_op jit(solution)/shard_map/ppermute | solution.py:31
  36.9 14.3 %collective-permute-start.15 = (bf16[384,128]{1,0:T(8,128)(2,1)S(1)}, bf16[384,128]{1,0:T(8,128)(2,1)S(1)}, u32[]{:S(2)}, u32[]{:S(2)}) collective-permute-start(bf16[384,128]{1,0:T(8,128)(2,1)S(1)} %get-tuple-element.61.left), channel_id=1, source_target_pairs={{0,3},{1,0},{2,1},{3,2},{4,7},{5,4},{6,5},{7,6},{8,11},{9,8},{10,9... | collective-permute-start | bytes 294920 | tf_op jit(solution)/shard_map/ppermute | solution.py:31
  39.4 13.7 %collective-permute-start.14 = (bf16[384,128]{1,0:T(8,128)(2,1)S(1)}, bf16[384,128]{1,0:T(8,128)(2,1)S(1)}, u32[]{:S(2)}, u32[]{:S(2)}) collective-permute-start(bf16[384,128]{1,0:T(8,128)(2,1)S(1)} %get-tuple-element.62.right), channel_id=1, source_target_pairs={{0,1},{1,2},{2,3},{3,0},{4,5},{5,6},{6,7},{7,4},{8,9},{9,10},{10,1... | collective-permute-start | bytes 294920 | tf_op jit(solution)/shard_map/ppermute | solution.py:31
  42.4 15.4 %collective-permute-start.20 = (bf16[384,128]{1,0:T(8,128)(2,1)S(1)}, bf16[384,128]{1,0:T(8,128)(2,1)S(1)}, u32[]{:S(2)}, u32[]{:S(2)}) collective-permute-start(bf16[384,128]{1,0:T(8,128)(2,1)S(1)} %get-tuple-element.67.left), channel_id=1, source_target_pairs={{0,3},{1,0},{2,1},{3,2},{4,7},{5,4},{6,5},{7,6},{8,11},{9,8},{10,9... | collective-permute-start | bytes 294920 | tf_op jit(solution)/shard_map/ppermute | solution.py:31
  47.6 10.2 %collective-permute-start.19 = (bf16[384,128]{1,0:T(8,128)(2,1)S(1)}, bf16[384,128]{1,0:T(8,128)(2,1)S(1)}, u32[]{:S(2)}, u32[]{:S(2)}) collective-permute-start(bf16[384,128]{1,0:T(8,128)(2,1)S(1)} %get-tuple-element.68.right), channel_id=1, source_target_pairs={{0,1},{1,2},{2,3},{3,0},{4,5},{5,6},{6,7},{7,4},{8,9},{9,10},{10,1... | collective-permute-start | bytes 294920 | tf_op jit(solution)/shard_map/ppermute | solution.py:31
  51.1 7.2 %collective-permute-start.4 = (bf16[384,128]{1,0:T(8,128)(2,1)S(1)}, bf16[384,128]{1,0:T(8,128)(2,1)S(1)}, u32[]{:S(2)}, u32[]{:S(2)}) collective-permute-start(bf16[384,128]{1,0:T(8,128)(2,1)S(1)} %get-tuple-element.44.left), channel_id=1, source_target_pairs={{0,3},{1,0},{2,1},{3,2},{4,7},{5,4},{6,5},{7,6},{8,11},{9,8},{10,9... | collective-permute-start | bytes 294920 | tf_op jit(solution)/shard_map/ppermute | solution.py:31
  51.2 10.1 %collective-permute-start.3 = (bf16[384,128]{1,0:T(8,128)(2,1)S(1)}, bf16[384,128]{1,0:T(8,128)(2,1)S(1)}, u32[]{:S(2)}, u32[]{:S(2)}) collective-permute-start(bf16[384,128]{1,0:T(8,128)(2,1)S(1)} %get-tuple-element.45.right), channel_id=1, source_target_pairs={{0,1},{1,2},{2,3},{3,0},{4,5},{5,6},{6,7},{7,4},{8,9},{9,10},{10,1... | collective-permute-start | bytes 294920 | tf_op jit(solution)/shard_map/ppermute | solution.py:31
  53.2 8.7 %collective-permute-start.16 = (bf16[192,128]{1,0:T(8,128)(2,1)S(1)}, bf16[192,128]{1,0:T(8,128)(2,1)S(1)}, u32[]{:S(2)}, u32[]{:S(2)}) collective-permute-start(bf16[192,128]{1,0:T(8,128)(2,1)S(1)} %get-tuple-element.64), channel_id=1, source_target_pairs={{0,12},{4,0},{8,4},{12,8},{1,13},{5,1},{9,5},{13,9},{2,14},{6,2},{... | collective-permute-start | bytes 147464 | tf_op jit(solution)/shard_map/ppermute | solution.py:31
  57.8 4.3 %collective-permute-start.17 = (bf16[192,128]{1,0:T(8,128)(2,1)S(1)}, bf16[192,128]{1,0:T(8,128)(2,1)S(1)}, u32[]{:S(2)}, u32[]{:S(2)}) collective-permute-start(bf16[192,128]{1,0:T(8,128)(2,1)S(1)} %get-tuple-element.65), channel_id=1, source_target_pairs={{0,8},{4,12},{8,0},{12,4},{1,9},{5,13},{9,1},{13,5},{2,10},{6,14},... | collective-permute-start | bytes 147464 | tf_op jit(solution)/shard_map/ppermute | solution.py:31
  57.8 7.4 %collective-permute-start.18 = (bf16[192,128]{1,0:T(8,128)(2,1)S(1)}, bf16[192,128]{1,0:T(8,128)(2,1)S(1)}, u32[]{:S(2)}, u32[]{:S(2)}) collective-permute-start(bf16[192,128]{1,0:T(8,128)(2,1)S(1)} %get-tuple-element.66), channel_id=1, source_target_pairs={{0,4},{4,8},{8,12},{12,0},{1,5},{5,9},{9,13},{13,1},{2,6},{6,10},{... | collective-permute-start | bytes 147464 | tf_op jit(solution)/shard_map/ppermute | solution.py:31
  58.3 7.0 %collective-permute-start.21 = (bf16[192,128]{1,0:T(8,128)(2,1)S(1)}, bf16[192,128]{1,0:T(8,128)(2,1)S(1)}, u32[]{:S(2)}, u32[]{:S(2)}) collective-permute-start(bf16[192,128]{1,0:T(8,128)(2,1)S(1)} %get-tuple-element.70), channel_id=1, source_target_pairs={{0,12},{4,0},{8,4},{12,8},{1,13},{5,1},{9,5},{13,9},{2,14},{6,2},{... | collective-permute-start | bytes 147464 | tf_op jit(solution)/shard_map/ppermute | solution.py:31
  61.4 5.0 %collective-permute-start.22 = (bf16[192,128]{1,0:T(8,128)(2,1)S(1)}, bf16[192,128]{1,0:T(8,128)(2,1)S(1)}, u32[]{:S(2)}, u32[]{:S(2)}) collective-permute-start(bf16[192,128]{1,0:T(8,128)(2,1)S(1)} %get-tuple-element.71), channel_id=1, source_target_pairs={{0,8},{4,12},{8,0},{12,4},{1,9},{5,13},{9,1},{13,5},{2,10},{6,14},... | collective-permute-start | bytes 147464 | tf_op jit(solution)/shard_map/ppermute | solution.py:31
  62.0 4.8 %collective-permute-start.23 = (bf16[192,128]{1,0:T(8,128)(2,1)S(1)}, bf16[192,128]{1,0:T(8,128)(2,1)S(1)}, u32[]{:S(2)}, u32[]{:S(2)}) collective-permute-start(bf16[192,128]{1,0:T(8,128)(2,1)S(1)} %get-tuple-element.72), channel_id=1, source_target_pairs={{0,4},{4,8},{8,12},{12,0},{1,5},{5,9},{9,13},{13,1},{2,6},{6,10},{... | collective-permute-start | bytes 147464 | tf_op jit(solution)/shard_map/ppermute | solution.py:31
  62.1 6.3 %collective-permute-start.8 = (bf16[192,128]{1,0:T(8,128)(2,1)S(1)}, bf16[192,128]{1,0:T(8,128)(2,1)S(1)}, u32[]{:S(2)}, u32[]{:S(2)}) collective-permute-start(bf16[192,128]{1,0:T(8,128)(2,1)S(1)} %get-tuple-element.53), channel_id=1, source_target_pairs={{0,12},{4,0},{8,4},{12,8},{1,13},{5,1},{9,5},{13,9},{2,14},{6,2},{... | collective-permute-start | bytes 147464 | tf_op jit(solution)/shard_map/ppermute | solution.py:31
  65.3 5.7 %collective-permute-start.9 = (bf16[192,128]{1,0:T(8,128)(2,1)S(1)}, bf16[192,128]{1,0:T(8,128)(2,1)S(1)}, u32[]{:S(2)}, u32[]{:S(2)}) collective-permute-start(bf16[192,128]{1,0:T(8,128)(2,1)S(1)} %get-tuple-element.54), channel_id=1, source_target_pairs={{0,8},{4,12},{8,0},{12,4},{1,9},{5,13},{9,1},{13,5},{2,10},{6,14},... | collective-permute-start | bytes 147464 | tf_op jit(solution)/shard_map/ppermute | solution.py:31
  65.3 5.7 %collective-permute-start.10 = (bf16[192,128]{1,0:T(8,128)(2,1)S(1)}, bf16[192,128]{1,0:T(8,128)(2,1)S(1)}, u32[]{:S(2)}, u32[]{:S(2)}) collective-permute-start(bf16[192,128]{1,0:T(8,128)(2,1)S(1)} %get-tuple-element.55), channel_id=1, source_target_pairs={{0,4},{4,8},{8,12},{12,0},{1,5},{5,9},{9,13},{13,1},{2,6},{6,10},{... | collective-permute-start | bytes 147464 | tf_op jit(solution)/shard_map/ppermute | solution.py:31

commit v3 on v0

v3 whole, which is shorter than its diff:
```python
import functools
import math

import jax
import jax.numpy as jnp
from jax import lax
from jax.experimental import pallas as pl
from jax.experimental.pallas import tpu as pltpu
from jax.sharding import PartitionSpec as P

HEADS = 12
HEAD_DIM = 128
WCOLS = 64
STRIDE = 32
BLEND_TOTAL = 16.0
SCALE = HEAD_DIM ** (-0.5)
EXP2_SCALE = SCALE * math.log2(math.e)
MIB = 1024 * 1024
SMALL = pltpu.CompilerParams(vmem_limit_bytes=16 * MIB)
NO_COST = pl.CostEstimate(flops=0, bytes_accessed=0, transcendentals=0)
LARGE = pltpu.CompilerParams(vmem_limit_bytes=60 * MIB)

ANY = pl.BlockSpec(memory_space=pl.ANY)
VMEM = pl.BlockSpec(memory_space=pltpu.VMEM)


def shifted(block, axis, distance):
    count = lax.axis_size(axis)
    return lax.ppermute(block, axis, [(i, (i + distance) % count) for i in range(count)])


def swapped(block, distance):
    return lax.ppermute(block, "seq", [(i, i ^ distance) for i in range(lax.axis_size("seq"))])


def crossed(block, step, distance):
    wins, seqs = lax.axis_size("win"), lax.axis_size("seq")
    route = [
        (s * wins + w, (s ^ distance) * wins + (w + step) % wins)
        for s in range(seqs)
        for w in range(wins)
    ]
    return lax.ppermute(block, ("seq", "win"), route)


def partner(distance, group):
    position = lax.rem(lax.axis_index("seq"), group)
    result, bit = 0, 1
    while bit < group:
        own = lax.rem(lax.div(position, bit), 2)
        result = result + (1 - own if distance & bit else own) * bit
        bit *= 2
    return result


def start_block(sources, packed, start, sems):
    columns = pl.ds(pl.multiple_of(start * HEAD_DIM, HEAD_DIM), packed.shape[1])
    copies, row = [], 0
    for source in sources:
        rows = source.shape[0]
        copy = pltpu.make_async_copy(
            source.at[:, columns], packed.at[pl.ds(row, rows)], sems.at[len(copies)]
        )
        copy.start()
        copies.append(copy)
        row += rows
    return copies


def store_weights(blend, wide, packed, row):
    wide[...] = jnp.zeros_like(wide)
    wide[:, : blend.shape[1]] = blend[...].astype(jnp.float32)
    rows, width = packed.shape[0] - row, packed.shape[1]
    index = lax.broadcasted_iota(jnp.int32, (rows, 128), 0)
    value = jnp.zeros((rows, 128), jnp.float32)
    for at in range(0, wide.shape[1], 128):
        value = jnp.where(index == at // 128, wide[:, at : at + 128], value)
    packed[row:, :128] = value.astype(packed.dtype)
    if width > 128:
        packed[row:, 128:] = jnp.zeros((rows, width - 128), packed.dtype)


def pack_kernel(heads, group, distances, count, *refs):
    sources, blend = refs[:count], refs[count]
    packed = refs[count + 1 : count + 1 + len(distances)]
    sems, blend_rows, wide = refs[count + 1 + len(distances) :]
    copies = []
    load = pltpu.make_async_copy(blend, blend_rows, sems.at[len(distances), 0])
    load.start()
    for index, distance in enumerate(distances):
        start = partner(distance, group) * heads
        copies += start_block(sources, packed[index], start, sems.at[index])
    load.wait()
    message_rows = sum(source.shape[0] for source in sources)
    for ref in packed:
        store_weights(blend_rows, wide, ref, message_rows)
    for copy in copies:
        copy.wait()


def weight_rows(blend):
    return -(-blend.shape[1] // (16 * 128)) * 16


def wide_shape(blend):
    return (1, -(-blend.shape[1] // 128) * 128)


def pack(sources, blend, heads, group, distances):
    rows = sum(source.shape[0] for source in sources) + weight_rows(blend)
    out = jax.ShapeDtypeStruct((rows, heads * HEAD_DIM), sources[0].dtype)
    return pl.pallas_call(
        functools.partial(pack_kernel, heads, group, distances, len(sources)),
        out_shape=[out] * len(distances),
        in_specs=[ANY] * (len(sources) + 1),
        out_specs=[VMEM] * len(distances),
        scratch_shapes=[
            pltpu.SemaphoreType.DMA((len(distances) + 1, len(sources))),
            pltpu.VMEM(blend.shape, blend.dtype),
            pltpu.VMEM(wide_shape(blend), jnp.float32),
        ],
        compiler_params=LARGE,
        cost_estimate=NO_COST,
        name="pack",
    )(*sources, blend)


def prepare_kernel(heads, group, count, *refs):
    sources, (blend, ids) = refs[:count], refs[count : count + 2]
    packed, (bias, sems, wide) = refs[-4 - group : -3], refs[-3:]
    message_rows = sum(source.shape[0] for source in sources)
    copies = start_block(sources, packed[0], partner(0, group) * heads, sems.at[0])
    for distance in range(group):
        kept = sources if distance < group // 2 else sources[1:]
        start = group * heads + lax.rem(partner(distance, group), group // 2) * 2
        copies += start_block(kept, packed[1 + distance], start, sems.at[1 + distance])
    bias[...] = jnp.where(ids[...] != 0, 0.0, -jnp.inf)
    store_weights(blend, wide, packed[0], message_rows)
    for copy in copies:
        copy.wait()


def prepare(sources, blend, ids, heads, group, after):
    rows = sum(source.shape[0] for source in sources)
    dtype = sources[0].dtype
    outs = [jax.ShapeDtypeStruct((rows + weight_rows(blend), heads * HEAD_DIM), dtype)]
    for distance in range(group):
        kept = rows if distance < group // 2 else rows - sources[0].shape[0]
        outs.append(jax.ShapeDtypeStruct((kept, 2 * HEAD_DIM), dtype))
    outs.append(jax.ShapeDtypeStruct(ids.shape, jnp.float32))
    return pl.pallas_call(
        functools.partial(prepare_kernel, heads, group, len(sources)),
        out_shape=outs,
        in_specs=[ANY] * len(sources) + [VMEM] * 2 + [ANY] * len(after),
        out_specs=[VMEM] * len(outs),
        scratch_shapes=[
            pltpu.SemaphoreType.DMA((len(outs), len(sources))),
            pltpu.VMEM(wide_shape(blend), jnp.float32),
        ],
        compiler_params=SMALL,
        cost_estimate=NO_COST,
        name="prepare",
    )(*sources, blend, ids, *after)


def attend_kernel(group, image_rows, text_rows, query_blocks, outputs, store, bias, *refs):
    blocks, outs, (keys, values) = refs[:group], refs[-2 - outputs : -2], refs[-2:]
    key_rows = image_rows + text_rows
    for distance in range(group):
        block = blocks[distance]
        source = partner(distance, group)
        image = pl.ds(distance * image_rows, image_rows)
        text = pl.ds(pl.multiple_of(group * image_rows + source * text_rows, text_rows), text_rows)
        key_at = image_rows if distance < query_blocks else 0
        value_at = key_at + key_rows
        keys[image] = block[key_at : key_at + image_rows]
        keys[text] = block[key_at + image_rows : key_at + key_rows]
        values[image] = block[value_at : value_at + image_rows]
        values[text] = block[value_at + image_rows : value_at + key_rows]
    image_keys = group * image_rows
    for at_head in range(0, keys.shape[1], HEAD_DIM):
        head = slice(at_head, at_head + HEAD_DIM)
        for distance in range(query_blocks):
            scores = lax.dot_general(
                blocks[distance][:image_rows, head],
                keys[:, head],
                (((1,), (1,)), ((), ())),
                preferred_element_type=jnp.float32,
            )
            scores = jnp.concatenate(
                [scores[:, :image_keys], scores[:, image_keys:] + bias[...]], axis=1
            )
            peak = jnp.max(scores, axis=1, keepdims=True)
            weights = jnp.exp2((scores - peak) * EXP2_SCALE)
            total = jnp.sum(weights, axis=1, keepdims=True)
            result = jnp.dot(
                weights.astype(jnp.bfloat16), values[:, head], preferred_element_type=jnp.float32
            )
            result = (result / total).astype(jnp.bfloat16)
            store(outs, result, distance, head)


def store_strips(outs, result, distance, head):
    rows = result.shape[0]
    for row in range(rows // WCOLS):
        at = distance * rows // 2 + row * STRIDE
        for side, out in enumerate(outs):
            start = row * WCOLS + side * STRIDE
            out[at : at + STRIDE, head] = result[start : start + STRIDE]


def store_blocks(outs, result, distance, head):
    rows = result.shape[0]
    both = outs[3 * distance]
    for row in range(rows // WCOLS):
        at = row * STRIDE
        for side, out in enumerate(outs[3 * distance + 1 : 3 * distance + 3]):
            start = row * WCOLS + side * STRIDE
            out[at : at + STRIDE, head] = result[start : start + STRIDE]
            at_both = at + side * rows // 2
            both[at_both : at_both + STRIDE, head] = result[start : start + STRIDE]


def attend(blocks, query_blocks, bias, image_rows, text_rows, store, after):
    group, width = len(blocks), blocks[0].shape[1]
    half = image_rows // 2
    if store is store_strips:
        rows = [query_blocks * half] * 2
    else:
        rows = [image_rows, half, half] * query_blocks
    keys = pltpu.VMEM((group * (image_rows + text_rows), width), jnp.bfloat16)
    return pl.pallas_call(
        functools.partial(
            attend_kernel, group, image_rows, text_rows, query_blocks, len(rows), store
        ),
        out_shape=[jax.ShapeDtypeStruct((count, width), jnp.bfloat16) for count in rows],
        in_specs=[VMEM] * (1 + group) + [ANY] * len(after),
        out_specs=[VMEM] * len(rows),
        scratch_shapes=[keys, keys],
        compiler_params=SMALL,
        cost_estimate=NO_COST,
        name="attend",
    )(bias, *blocks, *after)


def weigh_kernel(group, weight_row, image_rows, *refs):
    blocks, (weight_left, weight_right) = refs[:group], refs[group:]
    half = image_rows // 2
    for distance in range(group):
        columns = blocks[distance][weight_row : weight_row + 16, :128].astype(jnp.float32).T
        for row in range(image_rows // WCOLS):
            column, start = row * WCOLS // 128, row * WCOLS % 128
            at = distance * half + row * STRIDE
            for side, out in ((0, weight_left), (1, weight_right)):
                first = start + side * STRIDE
                out[at : at + STRIDE] = jnp.broadcast_to(
                    columns[first : first + STRIDE, column : column + 1], (STRIDE, HEAD_DIM)
                )


def weigh(blocks, weight_row, image_rows):
    group = len(blocks)
    out = jax.ShapeDtypeStruct((group * image_rows // 2, HEAD_DIM), jnp.float32)
    return pl.pallas_call(
        functools.partial(weigh_kernel, group, weight_row, image_rows),
        out_shape=[out, out],
        in_specs=[VMEM] * group,
        out_specs=[VMEM, VMEM],
        compiler_params=SMALL,
        cost_estimate=NO_COST,
        name="weigh",
    )(*blocks)


def mix(weight, own, other):
    mixed = weight * own.astype(jnp.float32) + (BLEND_TOTAL - weight) * other.astype(jnp.float32)
    return (mixed * (1.0 / BLEND_TOTAL)).astype(jnp.bfloat16)


def blend_kernel(own, other, weight, *outs):
    half = outs[0].shape[0]
    for distance, out in enumerate(outs):
        rows = pl.ds(distance * half, half)
        for at_head in range(0, own.shape[1], HEAD_DIM):
            head = pl.ds(at_head, HEAD_DIM)
            out[:, head] = mix(weight[rows], own[rows, head], other[rows, head])


def blend_strips(own, other, weight, blocks):
    rows, width = own.shape
    out = jax.ShapeDtypeStruct((rows // blocks, width), jnp.bfloat16)
    return pl.pallas_call(
        blend_kernel,
        out_shape=[out] * blocks,
        in_specs=[VMEM] * 3,
        out_specs=[VMEM] * blocks,
        compiler_params=SMALL,
        cost_estimate=NO_COST,
        name="blend",
    )(own, other, weight)


def load_kernel(w_out, *refs):
    out, sem = refs[-2:]
    copy = pltpu.make_async_copy(w_out, out, sem)
    copy.start()
    copy.wait()


def load_weights(w_out, after):
    return pl.pallas_call(
        load_kernel,
        out_shape=jax.ShapeDtypeStruct(w_out.shape, w_out.dtype),
        in_specs=[ANY] * (1 + len(after)),
        out_specs=VMEM,
        scratch_shapes=[pltpu.SemaphoreType.DMA],
        compiler_params=SMALL,
        cost_estimate=NO_COST,
        name="load_weights",
    )(w_out, *after)


def collect_kernel(group, *refs):
    blocks, out = refs[:group], refs[-1]
    width = blocks[0].shape[1]
    for distance in range(group):
        start = pl.multiple_of(partner(distance, group) * width, HEAD_DIM)
        out[:, pl.ds(start, width)] = blocks[distance][...]


def collect(blocks, after):
    group = len(blocks)
    rows, width = blocks[0].shape
    return pl.pallas_call(
        functools.partial(collect_kernel, group),
        out_shape=jax.ShapeDtypeStruct((rows, group * width), blocks[0].dtype),
        in_specs=[VMEM] * group + [ANY] * len(after),
        out_specs=VMEM,
        compiler_params=SMALL,
        cost_estimate=NO_COST,
        name="collect",
    )(*blocks, *after)


TILES = 6


def begin_kernel(left, right, weights, total, features):
    depth = features.shape[1]
    for row in range(features.shape[0] // WCOLS):
        strip = slice(row * STRIDE, (row + 1) * STRIDE)
        at = row * WCOLS
        features[at : at + STRIDE] = left[strip]
        features[at + STRIDE : at + WCOLS] = right[strip]
    tile = total.shape[1] // TILES
    for at in range(0, total.shape[1], tile):
        total[:, at : at + tile] = jnp.dot(
            features[...], weights[:depth, at : at + tile], preferred_element_type=jnp.float32
        )


def project_begin(left, right, weights):
    rows, depth = left.shape
    return pl.pallas_call(
        begin_kernel,
        out_shape=jax.ShapeDtypeStruct((2 * rows, weights.shape[1]), jnp.float32),
        in_specs=[VMEM] * 3,
        out_specs=VMEM,
        scratch_shapes=[pltpu.VMEM((2 * rows, depth), jnp.bfloat16)],
        compiler_params=SMALL,
        cost_estimate=NO_COST,
        name="project_begin",
    )(left, right, weights)


def end_kernel(group, *refs):
    blocks, refs = refs[:-8], refs[-8:]
    weight_left, weight_right, weights, total, out, features, result, sems = refs
    width, half = blocks[0].shape[1], features.shape[0] // 2
    for distance in range(len(blocks) // 3):
        own, from_prev, from_next = blocks[3 * distance : 3 * distance + 3]
        place = lax.rem(partner(distance, group), len(blocks) // 3)
        for at_head in range(0, width, HEAD_DIM):
            columns = pl.ds(pl.multiple_of(place * width + at_head, HEAD_DIM), HEAD_DIM)
            head = pl.ds(at_head, HEAD_DIM)
            for row in range(features.shape[0] // WCOLS):
                strip = pl.ds(row * STRIDE, STRIDE)
                for side, other, weight in (
                    (0, from_prev, weight_left),
                    (1, from_next, weight_right),
                ):
                    mine = own[pl.ds(side * half + row * STRIDE, STRIDE), head]
                    features[pl.ds(row * WCOLS + side * STRIDE, STRIDE), columns] = mix(
                        weight[strip], mine, other[strip, head]
                    )
    tile = result.shape[1] // TILES
    first = weights.shape[0] - features.shape[1]
    copies = []
    for at in range(0, result.shape[1], tile):
        columns = pl.ds(at, tile)
        product = jnp.dot(
            features[...], weights[first:, at : at + tile], preferred_element_type=jnp.float32
        )
        result[:, columns] = (total[:, columns] + product).astype(jnp.bfloat16)
        copy = pltpu.make_async_copy(
            result.at[:, columns], out.at[:, columns], sems.at[len(copies)]
        )
        copy.start()
        copies.append(copy)
    for copy in copies:
        copy.wait()


def project_end(blocks, weight_left, weight_right, weights, total, group):
    rows, width = total.shape
    depth = len(blocks) // 3 * blocks[0].shape[1]
    return pl.pallas_call(
        functools.partial(end_kernel, group),
        out_shape=jax.ShapeDtypeStruct((rows, width), jnp.bfloat16),
        in_specs=[VMEM] * (len(blocks) + 4),
        out_specs=ANY,
        scratch_shapes=[
            pltpu.VMEM((rows, depth), jnp.bfloat16),
            pltpu.VMEM((rows, width), jnp.bfloat16),
            pltpu.SemaphoreType.DMA((TILES,)),
        ],
        compiler_params=SMALL,
        cost_estimate=NO_COST,
        name="project_end",
    )(*blocks, weight_left, weight_right, weights, total)


def absorb(carried, keys, values, valid_keys, queries):
    running, denominator, numerator = carried
    scores = jnp.einsum("qhd,khd->qhk", queries, keys, preferred_element_type=jnp.float32) * SCALE
    scores = jnp.where(valid_keys[None, None, :], scores, -jnp.inf)
    updated = jnp.maximum(running, jnp.max(scores, axis=2))
    rescale = jnp.exp(running - updated)
    weights = jnp.exp(scores - updated[:, :, None])
    denominator = denominator * rescale + jnp.sum(weights, axis=2)
    product = jnp.einsum(
        "qhk,khd->qhd", weights.astype(jnp.bfloat16), values, preferred_element_type=jnp.float32
    )
    numerator = numerator * rescale[:, :, None] + product
    return (updated, denominator, numerator)


def attend_ring(blocks, query_blocks, prompt_ids, image_rows, text_rows, store):
    group, width = len(blocks), blocks[0].shape[1]
    head_count = width // HEAD_DIM
    key_rows = image_rows + text_rows
    queries = jnp.concatenate([block[:image_rows] for block in blocks[:query_blocks]], axis=0)
    starts = [image_rows if d < query_blocks else 0 for d in range(group)]
    keys, values = (
        jnp.concatenate(
            [block[at + s : at + s + key_rows] for block, s in zip(blocks, starts)], axis=0
        ).reshape(-1, head_count, HEAD_DIM)
        for at in (0, key_rows)
    )
    queries = queries.reshape(-1, head_count, HEAD_DIM)
    seq_count = lax.axis_size("seq")
    group_count = seq_count // group
    own_group = lax.axis_index("seq") // group
    order = (lax.axis_index("seq") % group) ^ jnp.arange(group)
    text_valid = prompt_ids.reshape(seq_count, text_rows) != 0

    def valid_for(source):
        text = lax.dynamic_slice_in_dim(text_valid, source * group, group, 0)[order]
        return jnp.concatenate([jnp.ones((group, image_rows), jnp.bool_), text], axis=1).reshape(-1)

    query_count = queries.shape[0]
    initial = (
        jnp.full((query_count, head_count), -jnp.inf, jnp.float32),
        jnp.zeros((query_count, head_count), jnp.float32),
        jnp.zeros((query_count, head_count, HEAD_DIM), jnp.float32),
    )
    carried = absorb(initial, keys, values, valid_for(own_group), queries)

    def one_turn(turn, state):
        current, keys, values = state
        keys, values = shifted(keys, "seq", group), shifted(values, "seq", group)
        source = (own_group - turn) % group_count
        return (absorb(current, keys, values, valid_for(source), queries), keys, values)

    carried, _, _ = lax.fori_loop(1, group_count, one_turn, (carried, keys, values))
    _, denominator, numerator = carried
    attended = (numerator / denominator[:, :, None]).astype(jnp.bfloat16)
    strips = [attended.reshape(-1, 2, STRIDE, width)[:, side] for side in range(2)]
    if store is store_strips:
        return [strip.reshape(-1, width) for strip in strips]
    sides = [strip.reshape(query_blocks, -1, width) for strip in strips]
    blocks = []
    for left, right in zip(*sides):
        blocks += [jnp.concatenate([left, right], axis=0), left, right]
    return blocks


def on_device(query, key_image, value_image, key_text, value_text, prompt_ids, blend, w_out):
    seq_count = lax.axis_size("seq")
    group = math.gcd(HEADS & -HEADS, seq_count)
    heads = HEADS // group - 1
    halfway = group // 2
    image_rows, text_rows = query.shape[1], key_text.shape[1]
    message_rows = 3 * image_rows + 2 * text_rows
    sources = [query[0], key_image[0], key_text[0], value_image[0], value_text[0]]

    far, near = tuple(range(halfway, group)), tuple(range(1, halfway))
    first = [None] * group
    for distances in (far, near):
        packed = pack(sources, blend, heads, group, distances)
        for distance, message in zip(distances, packed):
            first[distance] = swapped(message, distance)
    prepared = prepare(sources, blend, prompt_ids, heads, group, [first[halfway]])
    first[0], second, bias = prepared[0], prepared[1:-1], prepared[-1]
    second = [second[0]] + [swapped(second[d], d) for d in range(1, group)]
    weights = load_weights(w_out, [first[halfway]])
    weight_left, weight_right = weigh(first, message_rows, image_rows)

    if seq_count == group:
        def attended(blocks, query_blocks, store, after):
            return attend(blocks, query_blocks, bias, image_rows, text_rows, store, after)
    else:
        def attended(blocks, query_blocks, store, after):
            return attend_ring(
                blocks, query_blocks, prompt_ids[0], image_rows, text_rows, store
            )

    left, right = attended(first, group, store_strips, [])
    mixed = blend_strips(left, shifted(right, "win", 1), weight_left, group)
    begins = [mixed[0]] + [swapped(mixed[d], d) for d in range(1, group)]

    results = attended(second, halfway, store_blocks, [mixed[0], weights])
    blocks = []
    for distance in range(halfway):
        both, left, right = results[3 * distance : 3 * distance + 3]
        blocks += [
            swapped(both, distance) if distance else both,
            crossed(right, 1, distance),
            crossed(left, -1, distance),
        ]
    begins = collect(begins, [results[0]])
    total = project_begin(begins, shifted(begins, "win", -1), weights)
    return project_end(blocks, weight_left, weight_right, weights, total, group)[None]


def solution(mesh):
    tokens = P(("pano", "win"), "seq", None)
    return jax.shard_map(
        on_device,
        mesh=mesh,
        in_specs=(tokens,) * 5 + (P(("pano", "win"), None), P(("pano", "win"), "seq"), P()),
        out_specs=tokens,
        check_vma=False,
    )
```

time: 139 us -> 72.2 us (0.52); the launches traced: 136 us -> 71.7 us
  waiting for transfers between devices: 85.1 us -> 15.7 us
  starting transfers between devices: 8.24 us -> 32.3 us
  matrix products: 16.8 us -> 0 us
  Pallas kernels: 0 us -> 13.7 us
  local copies, waits for them, and re-layouts: 19.8 us -> 9.8 us
  other arithmetic: 5.97 us -> 0 us
    ppermute x6 -> x16, waiting for transfers between devices: 85.1 us -> 15.7 us  [the longest x10 12.3 us: swapped(): lax.ppermute(block, 'seq', [(i, i ^ distance) for i in range(lax.axis_siz...]
    ppermute x6 -> x16, starting transfers between devices: 8.24 us -> 32.3 us  [the longest x10 19.4 us: swapped(): lax.ppermute(block, 'seq', [(i, i ^ distance) for i in range(lax.axis_siz...]
    dot_general x5 -> x0, matrix products: 16.8 us -> none  [the longest x3 10.3 us: project_rows(): jnp.dot(flat_rows, w_out, preferred_element_type=jnp.float32)]
    pallas_call x0 -> x11, Pallas kernels: none -> 13.7 us  [the longest x2 5.22 us: attend(): pl.pallas_call(functools.partial(attend_kernel, group, image_rows, text_r...]
    dynamic_slice x3 -> x0, local copies, waits for them, and re-layouts: 6.48 us -> none  [the longest x1 5.11 us: regroup(): kept_half = lax.dynamic_index_in_dim(paired, own_bit, 2, keepdims=False)]
    concatenate x7 -> x0, local copies, waits for them, and re-layouts: 6.01 us -> none  [the longest x6 5.93 us: on_device(): jnp.concatenate([query[0], key_image[0], key_text[0], value_image[0], val...]
    unnamed x22 -> x16, local copies, waits for them, and re-layouts: 4.71 us -> 9.8 us
    reduce_sum x1 -> x0, other arithmetic: 2.22 us -> none  [absorb(): denominator = denominator * rescale + jnp.sum(weights, axis=2)]
  transfers between devices with their start and end apart: 6 -> 16, of which waited for: 5 -> 4; matrix products, arithmetic and copies ran while one was open for 5% -> 0% of each run, Pallas kernels for 0% -> 14%
where the time goes in v3:
time: 72.2 us; the launch traced here: 71.7 us
  starting transfers between devices  32.3 us (45%)
  waiting for transfers between devices  15.7 us (22%)
  Pallas kernels  13.7 us (19%)
  local copies, waits for them, and re-layouts  9.8 us (14%)
    ppermute x10, starting transfers between devices, swapped(): lax.ppermute(block, 'seq', [(i, i ^ distance) for i in range(lax.axis_siz...  19.4 us
    ppermute x10, waiting for transfers between devices, swapped(): lax.ppermute(block, 'seq', [(i, i ^ distance) for i in range(lax.axis_siz...  12.3 us
    unnamed x16, local copies, waits for them, and re-layouts  9.8 us
    ppermute x4, starting transfers between devices, crossed(): return lax.ppermute(block, ('seq', 'win'), route)  7.29 us
    ppermute x2, starting transfers between devices, shifted(): lax.ppermute(block, axis, [(i, (i + distance) % count) for i in range(cou...  5.68 us
    pallas_call x2, Pallas kernels, attend(): pl.pallas_call(functools.partial(attend_kernel, group, image_rows, text_r...  5.22 us
    pallas_call x2, Pallas kernels, pack(): pl.pallas_call(functools.partial(pack_kernel, heads, group, distances, le...  3.98 us
    ppermute x4, waiting for transfers between devices, crossed(): return lax.ppermute(block, ('seq', 'win'), route)  2.96 us
  transfers between devices with their start and end apart: 16, of which 4 were waited for; matrix products, arithmetic and copies ran while one was open for 0% of the time, Pallas kernels for 14%

profile of v3, /device:TPU:1, one launch (start us, length us, event | category | flops | bytes accessed | tf_op | source)
XLA Modules:
  0.0 71.7 jit_solution(7276364801021946430)
XLA Ops:
  0.0 2.1 %pack.2 = (bf16[624,256]{1,0:T(8,128)(2,1)}, bf16[624,256]{1,0:T(8,128)(2,1)}) custom-call(bf16[192,1536]{1,0:T(8,128)(2,1)} %bitcast.6, bf16[192,1536]{1,0:T(8,128)(2,1)} %bitcast.9, bf16[16,1536]{1,0:T(8,128)(2,1)} %bitcast.15, bf16[192,1536]{1,0:T(8,128)(2,1)} %bitcast.12, bf16[16,1536]{1,0:T(8,128)(2,1)} %bitcast.18, s32[1,192]{1,0:T(1,128)} %refs_5_.5), custom_call_target="tpu_custom_call" | custom-call | tf_op jit(solution)/shard_map/pack/pallas_call | solution.py:112
  2.2 3.2 %collective-permute-start = (bf16[624,256]{1,0:T(8,128)(2,1)}, bf16[624,256]{1,0:T(8,128)(2,1)S(1)}, u32[]{:S(2)}, u32[]{:S(2)}) collective-permute-start(bf16[624,256]{1,0:T(8,128)(2,1)} %get-tuple-element.27), channel_id=1, source_target_pairs={{0,8},{4,12},{8,0},{12,4},{1,9},{5,13},{9,1},{13,5},{2,10},{6,14},... | collective-permute-start | bytes 958472 | tf_op jit(solution)/shard_map/ppermute | solution.py:33
  5.4 1.8 %pack.3 = bf16[624,256]{1,0:T(8,128)(2,1)} custom-call(bf16[192,1536]{1,0:T(8,128)(2,1)} %bitcast.7, bf16[192,1536]{1,0:T(8,128)(2,1)} %bitcast.10, bf16[16,1536]{1,0:T(8,128)(2,1)} %bitcast.16, bf16[192,1536]{1,0:T(8,128)(2,1)} %bitcast.13, bf16[16,1536]{1,0:T(8,128)(2,1)} %bitcast.19, s32[1,192]{1,0:T(1,128)} %refs_5_.5), custom_call_target="tpu_custom_call" | custom-call | tf_op jit(solution)/shard_map/pack/pallas_call | solution.py:112
  7.2 1.4 %collective-permute-start.4 = (bf16[624,256]{1,0:T(8,128)(2,1)}, bf16[624,256]{1,0:T(8,128)(2,1)S(1)}, u32[]{:S(2)}, u32[]{:S(2)}) collective-permute-start(bf16[624,256]{1,0:T(8,128)(2,1)} %pack.3), channel_id=1, source_target_pairs={{0,4},{4,0},{8,12},{12,8},{1,5},{5,1},{9,13},{13,9},{2,6},{6,2},{1... | collective-permute-start | bytes 958472 | tf_op jit(solution)/shard_map/ppermute | solution.py:33
  8.6 0.0 collective-permute-start.5
  8.6 11.2 %collective-permute-done.refs_7_.refs_2_.refs_0_ = bf16[624,256]{1,0:T(8,128)(2,1)S(1)} collective-permute-done((bf16[624,256]{1,0:T(8,128)(2,1)}, bf16[624,256]{1,0:T(8,128)(2,1)S(1)}, u32[]{:S(2)}, u32[]{:S(2)}) %collective-permute-start) | collective-permute-done | bytes 319520 | tf_op jit(solution)/shard_map/ppermute | solution.py:33
  19.7 1.1 %copy-done.1 = bf16[1,192,1536]{2,1,0:T(8,128)(2,1)S(1)} copy-done((bf16[1,192,1536]{2,1,0:T(8,128)(2,1)S(1)}, bf16[1,192,1536]{2,1,0:T(8,128)(2,1)}, u32[]{:S(2)}) %copy-start.1) | copy-done | bytes 589848
  20.8 1.1 %copy-done.2 = bf16[1,192,1536]{2,1,0:T(8,128)(2,1)S(1)} copy-done((bf16[1,192,1536]{2,1,0:T(8,128)(2,1)S(1)}, bf16[1,192,1536]{2,1,0:T(8,128)(2,1)}, u32[]{:S(2)}) %copy-start.2) | copy-done | bytes 589848
  21.9 1.1 %copy-done.3 = bf16[1,192,1536]{2,1,0:T(8,128)(2,1)S(1)} copy-done((bf16[1,192,1536]{2,1,0:T(8,128)(2,1)S(1)}, bf16[1,192,1536]{2,1,0:T(8,128)(2,1)}, u32[]{:S(2)}) %copy-start.3) | copy-done | bytes 589848
  22.9 0.8 %copy-done.4 = bf16[1,16,1536]{2,1,0:T(8,128)(2,1)S(1)} copy-done((bf16[1,16,1536]{2,1,0:T(8,128)(2,1)S(1)}, bf16[1,16,1536]{2,1,0:T(8,128)(2,1)}, u32[]{:S(2)}) %copy-start.4) | copy-done | bytes 49176
  23.7 0.8 %copy-done.5 = bf16[1,16,1536]{2,1,0:T(8,128)(2,1)S(1)} copy-done((bf16[1,16,1536]{2,1,0:T(8,128)(2,1)S(1)}, bf16[1,16,1536]{2,1,0:T(8,128)(2,1)}, u32[]{:S(2)}) %copy-start.5) | copy-done | bytes 49176
  24.5 0.7 copy-done.6
  25.2 0.7 copy-done.7
  25.8 0.5 prepare.1
  26.4 1.9 %collective-permute-start.1 = (bf16[608,256]{1,0:T(8,128)(2,1)S(1)}, bf16[608,256]{1,0:T(8,128)(2,1)S(1)}, u32[]{:S(2)}, u32[]{:S(2)}) collective-permute-start(bf16[608,256]{1,0:T(8,128)(2,1)S(1)} %get-tuple-element.30), channel_id=1, source_target_pairs={{0,4},{4,0},{8,12},{12,8},{1,5},{5,1},{9,13},{13,9},{2,6},{6,2},{1... | collective-permute-start | bytes 933896 | tf_op jit(solution)/shard_map/ppermute | solution.py:33
  28.3 3.5 %collective-permute-start.2 = (bf16[416,256]{1,0:T(8,128)(2,1)S(1)}, bf16[416,256]{1,0:T(8,128)(2,1)S(1)}, u32[]{:S(2)}, u32[]{:S(2)}) collective-permute-start(bf16[416,256]{1,0:T(8,128)(2,1)S(1)} %get-tuple-element.31), channel_id=1, source_target_pairs={{0,8},{4,12},{8,0},{12,4},{1,9},{5,13},{9,1},{13,5},{2,10},{6,14},... | collective-permute-start | bytes 638984 | tf_op jit(solution)/shard_map/ppermute | solution.py:33
  31.7 0.0 collective-permute-done.4.refs_1_
  31.7 0.0 collective-permute-done.5.refs_3_
  31.8 3.4 %attend.2 = (bf16[384,256]{1,0:T(8,128)(2,1)S(1)}, bf16[384,256]{1,0:T(8,128)(2,1)S(1)}) custom-call(f32[1,64]{1,0:T(1,128)S(1)} %get-tuple-element.28.bias, bf16[624,256]{1,0:T(8,128)(2,1)S(1)} %get-tuple-element.33.refs_0_, bf16[624,256]{1,0:T(8,128)(2,1)S(1)} %collective-permute-done.4.refs_1_, ...), custom_call_target="tpu_custom_call" | custom-call | tf_op jit(solution)/shard_map/attend/pallas_call | solution.py:232
  35.2 5.2 %collective-permute-start.6 = (bf16[384,256]{1,0:T(8,128)(2,1)S(1)}, bf16[384,256]{1,0:T(8,128)(2,1)S(1)}, u32[]{:S(2)}, u32[]{:S(2)}) collective-permute-start(bf16[384,256]{1,0:T(8,128)(2,1)S(1)} %get-tuple-element.36), channel_id=1, source_target_pairs={{0,1},{1,2},{2,3},{3,0},{4,5},{5,6},{6,7},{7,4},{8,9},{9,10},{10,1... | collective-permute-start | bytes 589832 | tf_op jit(solution)/shard_map/ppermute | solution.py:29
  40.4 4.0 %collective-permute-start.3 = (bf16[416,256]{1,0:T(8,128)(2,1)S(1)}, bf16[416,256]{1,0:T(8,128)(2,1)S(1)}, u32[]{:S(2)}, u32[]{:S(2)}) collective-permute-start(bf16[416,256]{1,0:T(8,128)(2,1)S(1)} %get-tuple-element.32), channel_id=1, source_target_pairs={{0,12},{4,8},{8,4},{12,0},{1,13},{5,9},{9,5},{13,1},{2,14},{6,10},... | collective-permute-start | bytes 638984 | tf_op jit(solution)/shard_map/ppermute | solution.py:33
  44.4 0.2 weigh.1
  44.6 0.0 collective-permute-done.6.other
  44.6 0.1 blend.1
  44.7 0.2 collective-permute-start.12
  44.9 2.5 %collective-permute-start.13 = (bf16[96,256]{1,0:T(8,128)(2,1)S(1)}, bf16[96,256]{1,0:T(8,128)(2,1)S(1)}, u32[]{:S(2)}, u32[]{:S(2)}) collective-permute-start(bf16[96,256]{1,0:T(8,128)(2,1)S(1)} %get-tuple-element.47), channel_id=1, source_target_pairs={{0,8},{4,12},{8,0},{12,4},{1,9},{5,13},{9,1},{13,5},{2,10},{6,14},... | collective-permute-start | bytes 147464 | tf_op jit(solution)/shard_map/ppermute | solution.py:33
  47.5 0.0 collective-permute-done.2.refs_2_
  47.5 1.3 %collective-permute-start.14 = (bf16[96,256]{1,0:T(8,128)(2,1)S(1)}, bf16[96,256]{1,0:T(8,128)(2,1)S(1)}, u32[]{:S(2)}, u32[]{:S(2)}) collective-permute-start(bf16[96,256]{1,0:T(8,128)(2,1)S(1)} %get-tuple-element.48), channel_id=1, source_target_pairs={{0,12},{4,8},{8,4},{12,0},{1,13},{5,9},{9,5},{13,1},{2,14},{6,10},... | collective-permute-start | bytes 147464 | tf_op jit(solution)/shard_map/ppermute | solution.py:33
  48.8 3.7 %copy-done = bf16[1536,3072]{1,0:T(8,128)(2,1)S(1)} copy-done((bf16[1536,3072]{1,0:T(8,128)(2,1)S(1)}, bf16[1536,3072]{1,0:T(8,128)(2,1)}, u32[]{:S(2)}) %copy-start) | copy-done | bytes 9437208
  52.5 0.6 load_weights.1.refs_5_.weights.refs_8_
  53.1 0.0 collective-permute-done.3.refs_3_
  53.2 0.0 collective-permute-done.1.refs_1_
  53.2 1.8 %attend.3 = (bf16[192,256]{1,0:T(8,128)(2,1)S(1)}, bf16[96,256]{1,0:T(8,128)(2,1)S(1)}, bf16[96,256]{1,0:T(8,128)(2,1)S(1)}, bf16[192,256]{1,0:T(8,128)(2,1)S(1)...) custom-call(f32[1,64]{1,0:T(1,128)S(1)} %get-tuple-element.28.bias, ...), custom_call_target="tpu_custom_call" | custom-call | tf_op jit(solution)/shard_map/attend/pallas_call | solution.py:232
  55.0 0.0 collective-permute-done.12.refs_1_
  55.0 1.2 %collective-permute-done.13.refs_2_ = bf16[96,256]{1,0:T(8,128)(2,1)S(1)} collective-permute-done((bf16[96,256]{1,0:T(8,128)(2,1)S(1)}, bf16[96,256]{1,0:T(8,128)(2,1)S(1)}, u32[]{:S(2)}, u32[]{:S(2)}) %collective-permute-start.13) | collective-permute-done | bytes 49184 | tf_op jit(solution)/shard_map/ppermute | solution.py:33
  56.1 0.0 collective-permute-done.14.refs_3_
  56.2 0.4 collective-permute-start.15
  56.6 1.3 %collective-permute-start.9 = (bf16[192,256]{1,0:T(8,128)(2,1)S(1)}, bf16[192,256]{1,0:T(8,128)(2,1)S(1)}, u32[]{:S(2)}, u32[]{:S(2)}) collective-permute-start(bf16[192,256]{1,0:T(8,128)(2,1)S(1)} %get-tuple-element.42), channel_id=1, source_target_pairs={{0,4},{4,0},{8,12},{12,8},{1,5},{5,1},{9,13},{13,9},{2,6},{6,2},{1... | collective-permute-start | bytes 294920 | tf_op jit(solution)/shard_map/ppermute | solution.py:33
  58.0 4.2 %collective-permute-start.7 = (bf16[96,256]{1,0:T(8,128)(2,1)S(1)}, bf16[96,256]{1,0:T(8,128)(2,1)S(1)}, u32[]{:S(2)}, u32[]{:S(2)}) collective-permute-start(bf16[96,256]{1,0:T(8,128)(2,1)S(1)} %get-tuple-element.40), channel_id=1, source_target_pairs={{0,1},{1,2},{2,3},{3,0},{4,5},{5,6},{6,7},{7,4},{8,9},{9,10},{10,1... | collective-permute-start | bytes 147464 | tf_op jit(solution)/shard_map/ppermute | solution.py:43
  62.2 0.0 collective-permute-start.8
  62.2 3.1 %collective-permute-start.10 = (bf16[96,256]{1,0:T(8,128)(2,1)S(1)}, bf16[96,256]{1,0:T(8,128)(2,1)S(1)}, u32[]{:S(2)}, u32[]{:S(2)}) collective-permute-start(bf16[96,256]{1,0:T(8,128)(2,1)S(1)} %get-tuple-element.43), channel_id=1, source_target_pairs={{0,5},{1,6},{2,7},{3,4},{4,1},{5,2},{6,3},{7,0},{8,13},{9,14},{10,... | collective-permute-start | bytes 147464 | tf_op jit(solution)/shard_map/ppermute | solution.py:43
  65.3 0.4 collective-permute-done.15.right
  65.7 1.4 %project_begin.1.refs_9_ = f32[192,3072]{1,0:T(8,128)S(1)} custom-call(bf16[96,1024]{1,0:T(8,128)(2,1)S(1)} %collect.1.left, bf16[96,1024]{1,0:T(8,128)(2,1)S(1)} %collective-permute-done.15.right, bf16[1536,3072]{1,0:T(8,128)(2,1)S(1)} %load_weights.1.refs_5_.weights.refs_8_), custom_call_target="tpu_custom_call" | custom-call | tf_op jit(solution)/shard_map/project_begin/pallas_call | solution.py:364
  67.1 0.0 collective-permute-done.7.refs_1_
  67.1 0.0 collective-permute-done.8.refs_2_
  67.1 3.0 %collective-permute-done.11.refs_5_ = bf16[96,256]{1,0:T(8,128)(2,1)S(1)} collective-permute-done((bf16[96,256]{1,0:T(8,128)(2,1)S(1)}, bf16[96,256]{1,0:T(8,128)(2,1)S(1)}, u32[]{:S(2)}, u32[]{:S(2)}) %collective-permute-start.11) | collective-permute-done | bytes 49184 | tf_op jit(solution)/shard_map/ppermute | solution.py:43
  70.1 0.0 collective-permute-done.9.refs_3_
  70.1 1.6 %project_end.1 = bf16[192,3072]{1,0:T(8,128)(2,1)} custom-call(bf16[192,256]{1,0:T(8,128)(2,1)S(1)} %get-tuple-element.39.refs_4_.refs_0_, bf16[96,256]{1,0:T(8,128)(2,1)S(1)} %collective-permute-done.7.refs_1_, bf16[96,256]{1,0:T(8,128)(2,1)S(1)} %collective-permute-done.8.refs_2_, bf16[192,256]{1,0:T(8,128)(2,1)S(1)} %collective-permute-done.9.refs_3_, ...), custom_call_target="tpu_custom_call" | custom-call | tf_op jit(solution)/shard_map/project_end/pallas_call | solution.py:417
  (11 shorter events, 0.1 us)
Async XLA Ops:
  2.2 17.6 %collective-permute-start = (bf16[624,256]{1,0:T(8,128)(2,1)}, bf16[624,256]{1,0:T(8,128)(2,1)S(1)}, u32[]{:S(2)}, u32[]{:S(2)}) collective-permute-start(bf16[624,256]{1,0:T(8,128)(2,1)} %get-tuple-element.27), channel_id=1, source_target_pairs={{0,8},{4,12},{8,0},{12,4},{1,9},{5,13},{9,1},{13,5},{2,10},{6,14},... | collective-permute-start | bytes 958472 | tf_op jit(solution)/shard_map/ppermute | solution.py:33
  7.2 24.6 %collective-permute-start.4 = (bf16[624,256]{1,0:T(8,128)(2,1)}, bf16[624,256]{1,0:T(8,128)(2,1)S(1)}, u32[]{:S(2)}, u32[]{:S(2)}) collective-permute-start(bf16[624,256]{1,0:T(8,128)(2,1)} %pack.3), channel_id=1, source_target_pairs={{0,4},{4,0},{8,12},{12,8},{1,5},{5,1},{9,13},{13,9},{2,6},{6,2},{1... | collective-permute-start | bytes 958472 | tf_op jit(solution)/shard_map/ppermute | solution.py:33
  8.6 23.2 %collective-permute-start.5 = (bf16[624,256]{1,0:T(8,128)(2,1)}, bf16[624,256]{1,0:T(8,128)(2,1)S(1)}, u32[]{:S(2)}, u32[]{:S(2)}) collective-permute-start(bf16[624,256]{1,0:T(8,128)(2,1)} %get-tuple-element.34), channel_id=1, source_target_pairs={{0,12},{4,8},{8,4},{12,0},{1,13},{5,9},{9,5},{13,1},{2,14},{6,10},... | collective-permute-start | bytes 958472 | tf_op jit(solution)/shard_map/ppermute | solution.py:33
  19.7 1.1 %copy-start.1 = (bf16[1,192,1536]{2,1,0:T(8,128)(2,1)S(1)}, bf16[1,192,1536]{2,1,0:T(8,128)(2,1)}, u32[]{:S(2)}) copy-start(bf16[1,192,1536]{2,1,0:T(8,128)(2,1)} %param.8) | copy-start | bytes 1769476
  20.8 1.1 %copy-start.2 = (bf16[1,192,1536]{2,1,0:T(8,128)(2,1)S(1)}, bf16[1,192,1536]{2,1,0:T(8,128)(2,1)}, u32[]{:S(2)}) copy-start(bf16[1,192,1536]{2,1,0:T(8,128)(2,1)} %param.9) | copy-start | bytes 1769476
  21.9 1.1 %copy-start.3 = (bf16[1,192,1536]{2,1,0:T(8,128)(2,1)S(1)}, bf16[1,192,1536]{2,1,0:T(8,128)(2,1)}, u32[]{:S(2)}) copy-start(bf16[1,192,1536]{2,1,0:T(8,128)(2,1)} %param.10) | copy-start | bytes 1769476
  22.9 0.8 %copy-start.4 = (bf16[1,16,1536]{2,1,0:T(8,128)(2,1)S(1)}, bf16[1,16,1536]{2,1,0:T(8,128)(2,1)}, u32[]{:S(2)}) copy-start(bf16[1,16,1536]{2,1,0:T(8,128)(2,1)} %param.11) | copy-start | bytes 147460
  23.7 0.8 %copy-start.5 = (bf16[1,16,1536]{2,1,0:T(8,128)(2,1)S(1)}, bf16[1,16,1536]{2,1,0:T(8,128)(2,1)}, u32[]{:S(2)}) copy-start(bf16[1,16,1536]{2,1,0:T(8,128)(2,1)} %param.12) | copy-start | bytes 147460
  24.5 0.7 copy-start.6
  25.2 0.7 copy-start.7
  26.4 26.8 %collective-permute-start.1 = (bf16[608,256]{1,0:T(8,128)(2,1)S(1)}, bf16[608,256]{1,0:T(8,128)(2,1)S(1)}, u32[]{:S(2)}, u32[]{:S(2)}) collective-permute-start(bf16[608,256]{1,0:T(8,128)(2,1)S(1)} %get-tuple-element.30), channel_id=1, source_target_pairs={{0,4},{4,0},{8,12},{12,8},{1,5},{5,1},{9,13},{13,9},{2,6},{6,2},{1... | collective-permute-start | bytes 933896 | tf_op jit(solution)/shard_map/ppermute | solution.py:33
  28.3 19.2 %collective-permute-start.2 = (bf16[416,256]{1,0:T(8,128)(2,1)S(1)}, bf16[416,256]{1,0:T(8,128)(2,1)S(1)}, u32[]{:S(2)}, u32[]{:S(2)}) collective-permute-start(bf16[416,256]{1,0:T(8,128)(2,1)S(1)} %get-tuple-element.31), channel_id=1, source_target_pairs={{0,8},{4,12},{8,0},{12,4},{1,9},{5,13},{9,1},{13,5},{2,10},{6,14},... | collective-permute-start | bytes 638984 | tf_op jit(solution)/shard_map/ppermute | solution.py:33
  35.2 9.5 %collective-permute-start.6 = (bf16[384,256]{1,0:T(8,128)(2,1)S(1)}, bf16[384,256]{1,0:T(8,128)(2,1)S(1)}, u32[]{:S(2)}, u32[]{:S(2)}) collective-permute-start(bf16[384,256]{1,0:T(8,128)(2,1)S(1)} %get-tuple-element.36), channel_id=1, source_target_pairs={{0,1},{1,2},{2,3},{3,0},{4,5},{5,6},{6,7},{7,4},{8,9},{9,10},{10,1... | collective-permute-start | bytes 589832 | tf_op jit(solution)/shard_map/ppermute | solution.py:29
  40.4 12.7 %collective-permute-start.3 = (bf16[416,256]{1,0:T(8,128)(2,1)S(1)}, bf16[416,256]{1,0:T(8,128)(2,1)S(1)}, u32[]{:S(2)}, u32[]{:S(2)}) collective-permute-start(bf16[416,256]{1,0:T(8,128)(2,1)S(1)} %get-tuple-element.32), channel_id=1, source_target_pairs={{0,12},{4,8},{8,4},{12,0},{1,13},{5,9},{9,5},{13,1},{2,14},{6,10},... | collective-permute-start | bytes 638984 | tf_op jit(solution)/shard_map/ppermute | solution.py:33
  44.7 10.2 %collective-permute-start.12 = (bf16[96,256]{1,0:T(8,128)(2,1)S(1)}, bf16[96,256]{1,0:T(8,128)(2,1)S(1)}, u32[]{:S(2)}, u32[]{:S(2)}) collective-permute-start(bf16[96,256]{1,0:T(8,128)(2,1)S(1)} %get-tuple-element.46), channel_id=1, source_target_pairs={{0,4},{4,0},{8,12},{12,8},{1,5},{5,1},{9,13},{13,9},{2,6},{6,2},{1... | collective-permute-start | bytes 147464 | tf_op jit(solution)/shard_map/ppermute | solution.py:33
  44.9 11.2 %collective-permute-start.13 = (bf16[96,256]{1,0:T(8,128)(2,1)S(1)}, bf16[96,256]{1,0:T(8,128)(2,1)S(1)}, u32[]{:S(2)}, u32[]{:S(2)}) collective-permute-start(bf16[96,256]{1,0:T(8,128)(2,1)S(1)} %get-tuple-element.47), channel_id=1, source_target_pairs={{0,8},{4,12},{8,0},{12,4},{1,9},{5,13},{9,1},{13,5},{2,10},{6,14},... | collective-permute-start | bytes 147464 | tf_op jit(solution)/shard_map/ppermute | solution.py:33
  47.5 8.7 %collective-permute-start.14 = (bf16[96,256]{1,0:T(8,128)(2,1)S(1)}, bf16[96,256]{1,0:T(8,128)(2,1)S(1)}, u32[]{:S(2)}, u32[]{:S(2)}) collective-permute-start(bf16[96,256]{1,0:T(8,128)(2,1)S(1)} %get-tuple-element.48), channel_id=1, source_target_pairs={{0,12},{4,8},{8,4},{12,0},{1,13},{5,9},{9,5},{13,1},{2,14},{6,10},... | collective-permute-start | bytes 147464 | tf_op jit(solution)/shard_map/ppermute | solution.py:33
  48.8 3.7 %copy-start = (bf16[1536,3072]{1,0:T(8,128)(2,1)S(1)}, bf16[1536,3072]{1,0:T(8,128)(2,1)}, u32[]{:S(2)}) copy-start(bf16[1536,3072]{1,0:T(8,128)(2,1)} %w_out.1) | copy-start | bytes 28311556
  56.2 9.5 %collective-permute-start.15 = (bf16[96,1024]{1,0:T(8,128)(2,1)S(1)}, bf16[96,1024]{1,0:T(8,128)(2,1)S(1)}, u32[]{:S(2)}, u32[]{:S(2)}) collective-permute-start(bf16[96,1024]{1,0:T(8,128)(2,1)S(1)} %collect.1.left), channel_id=1, source_target_pairs={{0,3},{1,0},{2,1},{3,2},{4,7},{5,4},{6,5},{7,6},{8,11},{9,8},{10,9... | collective-permute-start | bytes 589832 | tf_op jit(solution)/shard_map/ppermute | solution.py:29
  56.6 13.5 %collective-permute-start.9 = (bf16[192,256]{1,0:T(8,128)(2,1)S(1)}, bf16[192,256]{1,0:T(8,128)(2,1)S(1)}, u32[]{:S(2)}, u32[]{:S(2)}) collective-permute-start(bf16[192,256]{1,0:T(8,128)(2,1)S(1)} %get-tuple-element.42), channel_id=1, source_target_pairs={{0,4},{4,0},{8,12},{12,8},{1,5},{5,1},{9,13},{13,9},{2,6},{6,2},{1... | collective-permute-start | bytes 294920 | tf_op jit(solution)/shard_map/ppermute | solution.py:33
  58.0 9.1 %collective-permute-start.7 = (bf16[96,256]{1,0:T(8,128)(2,1)S(1)}, bf16[96,256]{1,0:T(8,128)(2,1)S(1)}, u32[]{:S(2)}, u32[]{:S(2)}) collective-permute-start(bf16[96,256]{1,0:T(8,128)(2,1)S(1)} %get-tuple-element.40), channel_id=1, source_target_pairs={{0,1},{1,2},{2,3},{3,0},{4,5},{5,6},{6,7},{7,4},{8,9},{9,10},{10,1... | collective-permute-start | bytes 147464 | tf_op jit(solution)/shard_map/ppermute | solution.py:43
  62.2 5.0 %collective-permute-start.8 = (bf16[96,256]{1,0:T(8,128)(2,1)S(1)}, bf16[96,256]{1,0:T(8,128)(2,1)S(1)}, u32[]{:S(2)}, u32[]{:S(2)}) collective-permute-start(bf16[96,256]{1,0:T(8,128)(2,1)S(1)} %get-tuple-element.41), channel_id=1, source_target_pairs={{0,3},{1,0},{2,1},{3,2},{4,7},{5,4},{6,5},{7,6},{8,11},{9,8},{10,9... | collective-permute-start | bytes 147464 | tf_op jit(solution)/shard_map/ppermute | solution.py:43
  62.2 5.0 %collective-permute-start.10 = (bf16[96,256]{1,0:T(8,128)(2,1)S(1)}, bf16[96,256]{1,0:T(8,128)(2,1)S(1)}, u32[]{:S(2)}, u32[]{:S(2)}) collective-permute-start(bf16[96,256]{1,0:T(8,128)(2,1)S(1)} %get-tuple-element.43), channel_id=1, source_target_pairs={{0,5},{1,6},{2,7},{3,4},{4,1},{5,2},{6,3},{7,0},{8,13},{9,14},{10,... | collective-permute-start | bytes 147464 | tf_op jit(solution)/shard_map/ppermute | solution.py:43
  65.7 4.4 %collective-permute-start.11 = (bf16[96,256]{1,0:T(8,128)(2,1)S(1)}, bf16[96,256]{1,0:T(8,128)(2,1)S(1)}, u32[]{:S(2)}, u32[]{:S(2)}) collective-permute-start(bf16[96,256]{1,0:T(8,128)(2,1)S(1)} %get-tuple-element.44), channel_id=1, source_target_pairs={{0,7},{1,4},{2,5},{3,6},{4,3},{5,0},{6,1},{7,2},{8,15},{9,12},{10,... | collective-permute-start | bytes 147464 | tf_op jit(solution)/shard_map/ppermute | solution.py:43

commit v4 on v3

--- a/solution.py
+++ b/solution.py
@@ -31,16 +31,6 @@
 
 def swapped(block, distance):
     return lax.ppermute(block, "seq", [(i, i ^ distance) for i in range(lax.axis_size("seq"))])
-
-
-def crossed(block, step, distance):
-    wins, seqs = lax.axis_size("win"), lax.axis_size("seq")
-    route = [
-        (s * wins + w, (s ^ distance) * wins + (w + step) % wins)
-        for s in range(seqs)
-        for w in range(wins)
-    ]
-    return lax.ppermute(block, ("seq", "win"), route)
 
 
 def partner(distance, group):
@@ -163,95 +153,127 @@
     )(*sources, blend, ids, *after)
 
 
-def attend_kernel(group, image_rows, text_rows, query_blocks, outputs, store, bias, *refs):
-    blocks, outs, (keys, values) = refs[:group], refs[-2 - outputs : -2], refs[-2:]
+def soften(query, key, value, bias):
+    scores = lax.dot_general(
+        query, key, (((1,), (1,)), ((), ())), preferred_element_type=jnp.float32
+    )
+    image_keys = scores.shape[1] - bias.shape[1]
+    scores = jnp.concatenate([scores[:, :image_keys], scores[:, image_keys:] + bias], axis=1)
+    peak = jnp.max(scores, axis=1, keepdims=True)
+    weights = jnp.exp2((scores - peak) * EXP2_SCALE)
+    total = jnp.sum(weights, axis=1, keepdims=True)
+    result = jnp.dot(weights.astype(jnp.bfloat16), value, preferred_element_type=jnp.float32)
+    return (result / total).astype(jnp.bfloat16)
+
+
+def half_kernel(group, image_rows, text_rows, bias, *refs):
+    blocks, outs, (keys, values) = refs[:group], refs[-2 - group // 2 : -2], refs[-2:]
     key_rows = image_rows + text_rows
-    for distance in range(group):
-        block = blocks[distance]
+    for distance, block in enumerate(blocks):
         source = partner(distance, group)
         image = pl.ds(distance * image_rows, image_rows)
         text = pl.ds(pl.multiple_of(group * image_rows + source * text_rows, text_rows), text_rows)
-        key_at = image_rows if distance < query_blocks else 0
-        value_at = key_at + key_rows
-        keys[image] = block[key_at : key_at + image_rows]
-        keys[text] = block[key_at + image_rows : key_at + key_rows]
-        values[image] = block[value_at : value_at + image_rows]
-        values[text] = block[value_at + image_rows : value_at + key_rows]
-    image_keys = group * image_rows
+        key_at = image_rows if distance < group // 2 else 0
+        for ref, at in ((keys, key_at), (values, key_at + key_rows)):
+            ref[image] = block[at : at + image_rows]
+            ref[text] = block[at + image_rows : at + key_rows]
+    for at in range(0, keys.shape[1], HEAD_DIM):
+        head = slice(at, at + HEAD_DIM)
+        for block, out in zip(blocks, outs):
+            out[:, head] = soften(block[:image_rows, head], keys[:, head], values[:, head], bias[...])
+
+
+def attend_half(blocks, bias, image_rows, text_rows, after):
+    group, width = len(blocks), blocks[0].shape[1]
+    keys = pltpu.VMEM((group * (image_rows + text_rows), width), jnp.bfloat16)
+    return pl.pallas_call(
+        functools.partial(half_kernel, group, image_rows, text_rows),
+        out_shape=[jax.ShapeDtypeStruct((image_rows, width), jnp.bfloat16)] * (group // 2),
+        in_specs=[VMEM] * (1 + group) + [ANY] * len(after),
+        out_specs=[VMEM] * (group // 2),
+        scratch_shapes=[keys, keys],
+        compiler_params=SMALL,
+        cost_estimate=NO_COST,
+        name="attend_half",
+    )(bias, *blocks, *after)
+
+
+def merge_kernel(group, *refs):
+    blocks, (left, right) = refs[: group // 2], refs[-2:]
+    width = blocks[0].shape[1]
+    for distance, block in enumerate(blocks):
+        start = lax.rem(partner(distance, group), group // 2) * width
+        columns = pl.ds(pl.multiple_of(start, HEAD_DIM), width)
+        for row in range(block.shape[0] // WCOLS):
+            for side, out in enumerate((left, right)):
+                at = row * WCOLS + side * STRIDE
+                out[pl.ds(row * STRIDE, STRIDE), columns] = block[at : at + STRIDE]
+
+
+def merge(blocks, group, after):
+    rows, width = blocks[0].shape
+    strip = jax.ShapeDtypeStruct((rows // 2, len(blocks) * width), jnp.bfloat16)
+    return pl.pallas_call(
+        functools.partial(merge_kernel, group),
+        out_shape=[strip, strip],
+        in_specs=[VMEM] * len(blocks) + [ANY] * len(after),
+        out_specs=[VMEM] * 2,
+        compiler_params=SMALL,
+        cost_estimate=NO_COST,
+        name="merge",
+    )(*blocks, *after)
+
+
+def attend_kernel(group, image_rows, text_rows, bias, *refs):
+    blocks, lefts, rights, (keys, values) = refs[:group], refs[-6:-4], refs[-4:-2], refs[-2:]
+    key_rows = image_rows + text_rows
+    for distance, block in enumerate(blocks):
+        source = partner(distance, group)
+        image = pl.ds(distance * image_rows, image_rows)
+        text = pl.ds(pl.multiple_of(group * image_rows + source * text_rows, text_rows), text_rows)
+        for ref, at in ((keys, image_rows), (values, image_rows + key_rows)):
+            ref[image] = block[at : at + image_rows]
+            ref[text] = block[at + image_rows : at + key_rows]
+    half = image_rows // 2
     for at_head in range(0, keys.shape[1], HEAD_DIM):
         head = slice(at_head, at_head + HEAD_DIM)
-        for distance in range(query_blocks):
-            scores = lax.dot_general(
-                blocks[distance][:image_rows, head],
-                keys[:, head],
-                (((1,), (1,)), ((), ())),
-                preferred_element_type=jnp.float32,
-            )
-            scores = jnp.concatenate(
-                [scores[:, :image_keys], scores[:, image_keys:] + bias[...]], axis=1
-            )
-            peak = jnp.max(scores, axis=1, keepdims=True)
-            weights = jnp.exp2((scores - peak) * EXP2_SCALE)
-            total = jnp.sum(weights, axis=1, keepdims=True)
-            result = jnp.dot(
-                weights.astype(jnp.bfloat16), values[:, head], preferred_element_type=jnp.float32
-            )
-            result = (result / total).astype(jnp.bfloat16)
-            store(outs, result, distance, head)
-
-
-def store_strips(outs, result, distance, head):
-    rows = result.shape[0]
-    for row in range(rows // WCOLS):
-        at = distance * rows // 2 + row * STRIDE
-        for side, out in enumerate(outs):
-            start = row * WCOLS + side * STRIDE
-            out[at : at + STRIDE, head] = result[start : start + STRIDE]
-
-
-def store_blocks(outs, result, distance, head):
-    rows = result.shape[0]
-    both = outs[3 * distance]
-    for row in range(rows // WCOLS):
-        at = row * STRIDE
-        for side, out in enumerate(outs[3 * distance + 1 : 3 * distance + 3]):
-            start = row * WCOLS + side * STRIDE
-            out[at : at + STRIDE, head] = result[start : start + STRIDE]
-            at_both = at + side * rows // 2
-            both[at_both : at_both + STRIDE, head] = result[start : start + STRIDE]
-
-
-def attend(blocks, query_blocks, bias, image_rows, text_rows, store, after):
+        for distance, block in enumerate(blocks):
+            result = soften(block[:image_rows, head], keys[:, head], values[:, head], bias[...])
+            piece, place = divmod(distance, group // 2)
+            left, right = lefts[piece], rights[piece]
+            for row in range(image_rows // WCOLS):
+                at = place * half + row * STRIDE
+                left[at : at + STRIDE, head] = result[row * WCOLS : row * WCOLS + STRIDE]
+                right[at : at + STRIDE, head] = result[row * WCOLS + STRIDE : (row + 1) * WCOLS]
+
+
+def attend(blocks, bias, image_rows, text_rows):
     group, width = len(blocks), blocks[0].shape[1]
-    half = image_rows // 2
-    if store is store_strips:
-        rows = [query_blocks * half] * 2
-    else:
-        rows = [image_rows, half, half] * query_blocks
+    strip = jax.ShapeDtypeStruct((group // 2 * image_rows // 2, width), jnp.bfloat16)
     keys = pltpu.VMEM((group * (image_rows + text_rows), width), jnp.bfloat16)
-    return pl.pallas_call(
-        functools.partial(
-            attend_kernel, group, image_rows, text_rows, query_blocks, len(rows), store
-        ),
-        out_shape=[jax.ShapeDtypeStruct((count, width), jnp.bfloat16) for count in rows],
-        in_specs=[VMEM] * (1 + group) + [ANY] * len(after),
-        out_specs=[VMEM] * len(rows),
+    strips = pl.pallas_call(
+        functools.partial(attend_kernel, group, image_rows, text_rows),
+        out_shape=[strip] * 4,
+        in_specs=[VMEM] * (1 + group),
+        out_specs=[VMEM] * 4,
         scratch_shapes=[keys, keys],
         compiler_params=SMALL,
         cost_estimate=NO_COST,
         name="attend",
-    )(bias, *blocks, *after)
+    )(bias, *blocks)
+    return strips[:2], strips[2:]
 
 
 def weigh_kernel(group, weight_row, image_rows, *refs):
-    blocks, (weight_left, weight_right) = refs[:group], refs[group:]
+    blocks, outs = refs[:group], refs[group:]
     half = image_rows // 2
     for distance in range(group):
         columns = blocks[distance][weight_row : weight_row + 16, :128].astype(jnp.float32).T
         for row in range(image_rows // WCOLS):
             column, start = row * WCOLS // 128, row * WCOLS % 128
-            at = distance * half + row * STRIDE
-            for side, out in ((0, weight_left), (1, weight_right)):
+            piece, place = divmod(distance, group // 2)
+            at = place * half + row * STRIDE
+            for side, out in enumerate(outs[2 * piece : 2 * piece + 2]):
                 first = start + side * STRIDE
                 out[at : at + STRIDE] = jnp.broadcast_to(
                     columns[first : first + STRIDE, column : column + 1], (STRIDE, HEAD_DIM)
@@ -260,44 +282,44 @@
 
 def weigh(blocks, weight_row, image_rows):
     group = len(blocks)
-    out = jax.ShapeDtypeStruct((group * image_rows // 2, HEAD_DIM), jnp.float32)
+    out = jax.ShapeDtypeStruct((group // 2 * image_rows // 2, HEAD_DIM), jnp.float32)
     return pl.pallas_call(
         functools.partial(weigh_kernel, group, weight_row, image_rows),
-        out_shape=[out, out],
+        out_shape=[out] * 4,
         in_specs=[VMEM] * group,
-        out_specs=[VMEM, VMEM],
+        out_specs=[VMEM] * 4,
         compiler_params=SMALL,
         cost_estimate=NO_COST,
         name="weigh",
     )(*blocks)
 
 
-def mix(weight, own, other):
-    mixed = weight * own.astype(jnp.float32) + (BLEND_TOTAL - weight) * other.astype(jnp.float32)
-    return (mixed * (1.0 / BLEND_TOTAL)).astype(jnp.bfloat16)
-
-
-def blend_kernel(own, other, weight, *outs):
-    half = outs[0].shape[0]
-    for distance, out in enumerate(outs):
-        rows = pl.ds(distance * half, half)
+def blend_kernel(count, *refs):
+    sides, outs = refs[: 3 * count], refs[3 * count :]
+    half, blocks = outs[0].shape[0], len(outs) // count
+    for index, out in enumerate(outs):
+        own, other, weight_ref = sides[index // blocks * 3 : index // blocks * 3 + 3]
+        rows = pl.ds(index % blocks * half, half)
         for at_head in range(0, own.shape[1], HEAD_DIM):
             head = pl.ds(at_head, HEAD_DIM)
-            out[:, head] = mix(weight[rows], own[rows, head], other[rows, head])
-
-
-def blend_strips(own, other, weight, blocks):
-    rows, width = own.shape
-    out = jax.ShapeDtypeStruct((rows // blocks, width), jnp.bfloat16)
-    return pl.pallas_call(
-        blend_kernel,
+            weight = weight_ref[rows]
+            mixed = weight * own[rows, head].astype(jnp.float32)
+            mixed += (BLEND_TOTAL - weight) * other[rows, head].astype(jnp.float32)
+            out[:, head] = (mixed * (1.0 / BLEND_TOTAL)).astype(jnp.bfloat16)
+
+
+def blend_strips(sides, blocks):
+    rows, width = sides[0][0].shape
+    out = jax.ShapeDtypeStruct((len(sides) * rows // blocks, width), jnp.bfloat16)
+    return pl.pallas_call(
+        functools.partial(blend_kernel, len(sides)),
         out_shape=[out] * blocks,
-        in_specs=[VMEM] * 3,
+        in_specs=[VMEM] * (3 * len(sides)),
         out_specs=[VMEM] * blocks,
         compiler_params=SMALL,
         cost_estimate=NO_COST,
         name="blend",
-    )(own, other, weight)
+    )(*sum(sides, ()))
 
 
 def load_kernel(w_out, *refs):
@@ -318,6 +340,22 @@
         cost_estimate=NO_COST,
         name="load_weights",
     )(w_out, *after)
+
+
+def hold_kernel(source, *refs):
+    refs[-1][...] = source[...]
+
+
+def hold(array, after):
+    return pl.pallas_call(
+        hold_kernel,
+        out_shape=jax.ShapeDtypeStruct(array.shape, array.dtype),
+        in_specs=[VMEM] + [ANY] * len(after),
+        out_specs=VMEM,
+        compiler_params=SMALL,
+        cost_estimate=NO_COST,
+        name="hold",
+    )(array, *after)
 
 
 def collect_kernel(group, *refs):
@@ -328,18 +366,18 @@
         out[:, pl.ds(start, width)] = blocks[distance][...]
 
 
-def collect(blocks, after):
+def collect(blocks):
     group = len(blocks)
     rows, width = blocks[0].shape
     return pl.pallas_call(
         functools.partial(collect_kernel, group),
         out_shape=jax.ShapeDtypeStruct((rows, group * width), blocks[0].dtype),
-        in_specs=[VMEM] * group + [ANY] * len(after),
+        in_specs=[VMEM] * group,
         out_specs=VMEM,
         compiler_params=SMALL,
         cost_estimate=NO_COST,
         name="collect",
-    )(*blocks, *after)
+    )(*blocks)
 
 
 TILES = 6
@@ -373,26 +411,21 @@
     )(left, right, weights)
 
 
-def end_kernel(group, *refs):
-    blocks, refs = refs[:-8], refs[-8:]
+def end_kernel(left, right, from_prev, from_next, *refs):
     weight_left, weight_right, weights, total, out, features, result, sems = refs
-    width, half = blocks[0].shape[1], features.shape[0] // 2
-    for distance in range(len(blocks) // 3):
-        own, from_prev, from_next = blocks[3 * distance : 3 * distance + 3]
-        place = lax.rem(partner(distance, group), len(blocks) // 3)
-        for at_head in range(0, width, HEAD_DIM):
-            columns = pl.ds(pl.multiple_of(place * width + at_head, HEAD_DIM), HEAD_DIM)
-            head = pl.ds(at_head, HEAD_DIM)
-            for row in range(features.shape[0] // WCOLS):
-                strip = pl.ds(row * STRIDE, STRIDE)
-                for side, other, weight in (
-                    (0, from_prev, weight_left),
-                    (1, from_next, weight_right),
-                ):
-                    mine = own[pl.ds(side * half + row * STRIDE, STRIDE), head]
-                    features[pl.ds(row * WCOLS + side * STRIDE, STRIDE), columns] = mix(
-                        weight[strip], mine, other[strip, head]
-                    )
+    rows = left.shape[0]
+    for side, (own, other, weight_ref) in enumerate(
+        ((left, from_prev, weight_left), (right, from_next, weight_right))
+    ):
+        weight = weight_ref[:rows]
+        for at in range(0, own.shape[1], HEAD_DIM):
+            head = pl.ds(at, HEAD_DIM)
+            mixed = weight * own[:, head].astype(jnp.float32)
+            mixed += (BLEND_TOTAL - weight) * other[:, head].astype(jnp.float32)
+            mixed = (mixed * (1.0 / BLEND_TOTAL)).astype(jnp.bfloat16)
+            for row in range(rows // STRIDE):
+                start = row * WCOLS + side * STRIDE
+                features[pl.ds(start, STRIDE), head] = mixed[row * STRIDE : (row + 1) * STRIDE]
     tile = result.shape[1] // TILES
     first = weights.shape[0] - features.shape[1]
     copies = []
@@ -411,23 +444,22 @@
         copy.wait()
 
 
-def project_end(blocks, weight_left, weight_right, weights, total, group):
+def project_end(strips, blend_weights, weights, total):
     rows, width = total.shape
-    depth = len(blocks) // 3 * blocks[0].shape[1]
-    return pl.pallas_call(
-        functools.partial(end_kernel, group),
+    return pl.pallas_call(
+        end_kernel,
         out_shape=jax.ShapeDtypeStruct((rows, width), jnp.bfloat16),
-        in_specs=[VMEM] * (len(blocks) + 4),
+        in_specs=[VMEM] * 8,
         out_specs=ANY,
         scratch_shapes=[
-            pltpu.VMEM((rows, depth), jnp.bfloat16),
+            pltpu.VMEM((rows, strips[0].shape[1]), jnp.bfloat16),
             pltpu.VMEM((rows, width), jnp.bfloat16),
             pltpu.SemaphoreType.DMA((TILES,)),
         ],
         compiler_params=SMALL,
         cost_estimate=NO_COST,
         name="project_end",
-    )(*blocks, weight_left, weight_right, weights, total)
+    )(*strips, *blend_weights, weights, total)
 
 
 def absorb(carried, keys, values, valid_keys, queries):
@@ -445,7 +477,7 @@
     return (updated, denominator, numerator)
 
 
-def attend_ring(blocks, query_blocks, prompt_ids, image_rows, text_rows, store):
+def attend_ring(blocks, query_blocks, prompt_ids, image_rows, text_rows):
     group, width = len(blocks), blocks[0].shape[1]
     head_count = width // HEAD_DIM
     key_rows = image_rows + text_rows
@@ -485,14 +517,18 @@
     carried, _, _ = lax.fori_loop(1, group_count, one_turn, (carried, keys, values))
     _, denominator, numerator = carried
     attended = (numerator / denominator[:, :, None]).astype(jnp.bfloat16)
-    strips = [attended.reshape(-1, 2, STRIDE, width)[:, side] for side in range(2)]
-    if store is store_strips:
-        return [strip.reshape(-1, width) for strip in strips]
-    sides = [strip.reshape(query_blocks, -1, width) for strip in strips]
-    blocks = []
-    for left, right in zip(*sides):
-        blocks += [jnp.concatenate([left, right], axis=0), left, right]
-    return blocks
+    return attended.reshape(query_blocks, image_rows, width)
+
+
+def ring_strips(blocks, prompt_ids, image_rows, text_rows):
+    group = len(blocks)
+    attended = attend_ring(blocks, group, prompt_ids, image_rows, text_rows)
+    sides = attended.reshape(2, -1, 2, STRIDE, attended.shape[2])
+    return [[sides[p, :, s].reshape(-1, attended.shape[2]) for p in range(2)] for s in range(2)]
+
+
+def ring_half(blocks, prompt_ids, image_rows, text_rows):
+    return list(attend_ring(blocks, len(blocks) // 2, prompt_ids, image_rows, text_rows))
 
 
 def on_device(query, key_image, value_image, key_text, value_text, prompt_ids, blend, w_out):
@@ -505,42 +541,48 @@
     sources = [query[0], key_image[0], key_text[0], value_image[0], value_text[0]]
 
     far, near = tuple(range(halfway, group)), tuple(range(1, halfway))
-    first = [None] * group
+    received = [None] * group
     for distances in (far, near):
         packed = pack(sources, blend, heads, group, distances)
         for distance, message in zip(distances, packed):
-            first[distance] = swapped(message, distance)
-    prepared = prepare(sources, blend, prompt_ids, heads, group, [first[halfway]])
-    first[0], second, bias = prepared[0], prepared[1:-1], prepared[-1]
-    second = [second[0]] + [swapped(second[d], d) for d in range(1, group)]
-    weights = load_weights(w_out, [first[halfway]])
-    weight_left, weight_right = weigh(first, message_rows, image_rows)
-
-    if seq_count == group:
-        def attended(blocks, query_blocks, store, after):
-            return attend(blocks, query_blocks, bias, image_rows, text_rows, store, after)
-    else:
-        def attended(blocks, query_blocks, store, after):
-            return attend_ring(
-                blocks, query_blocks, prompt_ids[0], image_rows, text_rows, store
-            )
-
-    left, right = attended(first, group, store_strips, [])
-    mixed = blend_strips(left, shifted(right, "win", 1), weight_left, group)
-    begins = [mixed[0]] + [swapped(mixed[d], d) for d in range(1, group)]
-
-    results = attended(second, halfway, store_blocks, [mixed[0], weights])
-    blocks = []
-    for distance in range(halfway):
-        both, left, right = results[3 * distance : 3 * distance + 3]
-        blocks += [
-            swapped(both, distance) if distance else both,
-            crossed(right, 1, distance),
-            crossed(left, -1, distance),
-        ]
-    begins = collect(begins, [results[0]])
+            received[distance] = swapped(message, distance)
+    weights = load_weights(w_out, [])
+    prepared = prepare(sources, blend, prompt_ids, heads, group, [weights])
+    received[0], packed, bias = prepared[0], prepared[1:-1], prepared[-1]
+    first = received
+    second = [packed[0]] + [swapped(packed[d], d) for d in near]
+    for distance in far:
+        second.append(swapped(hold(packed[distance], first[halfway:]), distance))
+    blend_weights = weigh(first, message_rows, image_rows)
+
+    def strips_of(blocks):
+        if seq_count == group:
+            return attend(blocks, bias, image_rows, text_rows)
+        return ring_strips(blocks, prompt_ids[0], image_rows, text_rows)
+
+    def results_of(blocks, after):
+        if seq_count == group:
+            return attend_half(blocks, bias, image_rows, text_rows, after)
+        return ring_half(blocks, prompt_ids[0], image_rows, text_rows)
+
+    def returned(mixed):
+        return [mixed[0]] + [swapped(mixed[d], d) for d in range(1, len(mixed))]
+
+    lefts, rights = strips_of(first)
+    sides = [
+        (left, shifted(right, "win", 1), weight)
+        for left, right, weight in zip(lefts, rights, blend_weights[::2])
+    ]
+    mixed = blend_strips(sides, group)
+    begun = returned(mixed)
+
+    results = returned(results_of(second, [mixed[0], weights]))
+    left, right = merge(results, group, begun[1:])
+    from_prev, from_next = shifted(right, "win", 1), shifted(left, "win", -1)
+    begins = collect(begun)
     total = project_begin(begins, shifted(begins, "win", -1), weights)
-    return project_end(blocks, weight_left, weight_right, weights, total, group)[None]
+    strips = [left, right, from_prev, from_next]
+    return project_end(strips, blend_weights[:2], weights, total)[None]
 
 
 def solution(mesh):

time: 72.2 us -> 68.9 us (0.954)
  local copies, waits for them, and re-layouts: 9.8 us -> 4.43 us
  waiting for transfers between devices: 15.7 us -> 17.4 us
  Pallas kernels: 13.7 us -> 14.5 us
    ppermute x4 -> x0, starting transfers between devices: 7.29 us -> none  [crossed(): return lax.ppermute(block, ('seq', 'win'), route)]
    ppermute x2 -> x5, starting transfers between devices: 5.68 us -> 11.2 us  [shifted(): lax.ppermute(block, axis, [(i, (i + distance) % count) for i in range(cou...]
    unnamed x16, local copies, waits for them, and re-layouts: 9.8 us -> 4.43 us
    ppermute x2 -> x5, waiting for transfers between devices: 0.42 us -> 4.11 us  [shifted(): lax.ppermute(block, axis, [(i, (i + distance) % count) for i in range(cou...]
    ppermute x4 -> x0, waiting for transfers between devices: 2.96 us -> none  [crossed(): return lax.ppermute(block, ('seq', 'win'), route)]
    pallas_call x2 -> x6, Pallas kernels: 1.72 us -> 3.57 us  [the longest x1 1.8 us: attend_half(): pl.pallas_call(functools.partial(half_kernel, group, image_rows, text_row...]
    pallas_call x2 -> x1, Pallas kernels: 5.22 us -> 3.43 us  [attend(): pl.pallas_call(functools.partial(attend_kernel, group, image_rows, text_r...]
    ppermute x10, starting transfers between devices: 19.4 us -> 20.8 us  [swapped(): lax.ppermute(block, 'seq', [(i, i ^ distance) for i in range(lax.axis_siz...]
  transfers between devices with their start and end apart: 16 -> 15, of which waited for: 4 -> 6; matrix products, arithmetic and copies ran while one was open for 0% -> 0% of each run, Pallas kernels for 14% -> 16%
where the time goes in v4:
time: 68.9 us; the launch traced here: 68.5 us
  starting transfers between devices  32 us (46%)
  waiting for transfers between devices  17.4 us (25%)
  Pallas kernels  14.5 us (21%)
  local copies, waits for them, and re-layouts  4.43 us (6%)
    ppermute x10, starting transfers between devices, swapped(): lax.ppermute(block, 'seq', [(i, i ^ distance) for i in range(lax.axis_siz...  20.8 us
    ppermute x10, waiting for transfers between devices, swapped(): lax.ppermute(block, 'seq', [(i, i ^ distance) for i in range(lax.axis_siz...  13.3 us
    ppermute x5, starting transfers between devices, shifted(): lax.ppermute(block, axis, [(i, (i + distance) % count) for i in range(cou...  11.2 us
    unnamed x16, local copies, waits for them, and re-layouts  4.43 us
    ppermute x5, waiting for transfers between devices, shifted(): lax.ppermute(block, axis, [(i, (i + distance) % count) for i in range(cou...  4.11 us
    pallas_call x2, Pallas kernels, pack(): pl.pallas_call(functools.partial(pack_kernel, heads, group, distances, le...  3.98 us
    pallas_call x1, Pallas kernels, attend(): pl.pallas_call(functools.partial(attend_kernel, group, image_rows, text_r...  3.43 us
    pallas_call x1, Pallas kernels, attend_half(): pl.pallas_call(functools.partial(half_kernel, group, image_rows, text_row...  1.8 us
  transfers between devices with their start and end apart: 15, of which 6 were waited for; matrix products, arithmetic and copies ran while one was open for 0% of the time, Pallas kernels for 16%

profile of v4, /device:TPU:1, one launch (start us, length us, event | category | flops | bytes accessed | tf_op | source)
XLA Modules:
  0.0 68.5 jit_solution(3340965839093432066)
XLA Ops:
  0.0 2.1 %pack.2 = (bf16[624,256]{1,0:T(8,128)(2,1)}, bf16[624,256]{1,0:T(8,128)(2,1)}) custom-call(bf16[192,1536]{1,0:T(8,128)(2,1)} %bitcast.6, bf16[192,1536]{1,0:T(8,128)(2,1)} %bitcast.9, bf16[16,1536]{1,0:T(8,128)(2,1)} %bitcast.15, bf16[192,1536]{1,0:T(8,128)(2,1)} %bitcast.12, bf16[16,1536]{1,0:T(8,128)(2,1)} %bitcast.18, s32[1,192]{1,0:T(1,128)} %refs_5_.5), custom_call_target="tpu_custom_call" | custom-call | tf_op jit(solution)/shard_map/pack/pallas_call | solution.py:102
  2.2 3.2 %collective-permute-start.1 = (bf16[624,256]{1,0:T(8,128)(2,1)}, bf16[624,256]{1,0:T(8,128)(2,1)S(1)}, u32[]{:S(2)}, u32[]{:S(2)}) collective-permute-start(bf16[624,256]{1,0:T(8,128)(2,1)} %get-tuple-element.32), channel_id=1, source_target_pairs={{0,8},{4,12},{8,0},{12,4},{1,9},{5,13},{9,1},{13,5},{2,10},{6,14},... | collective-permute-start | bytes 958472 | tf_op jit(solution)/shard_map/ppermute | solution.py:33
  5.4 1.1 %collective-permute-start.2 = (bf16[624,256]{1,0:T(8,128)(2,1)}, bf16[624,256]{1,0:T(8,128)(2,1)S(1)}, u32[]{:S(2)}, u32[]{:S(2)}) collective-permute-start(bf16[624,256]{1,0:T(8,128)(2,1)} %get-tuple-element.33), channel_id=1, source_target_pairs={{0,12},{4,8},{8,4},{12,0},{1,13},{5,9},{9,5},{13,1},{2,14},{6,10},... | collective-permute-start | bytes 958472 | tf_op jit(solution)/shard_map/ppermute | solution.py:33
  6.4 1.8 %pack.3 = bf16[624,256]{1,0:T(8,128)(2,1)} custom-call(bf16[192,1536]{1,0:T(8,128)(2,1)} %bitcast.7, bf16[192,1536]{1,0:T(8,128)(2,1)} %bitcast.10, bf16[16,1536]{1,0:T(8,128)(2,1)} %bitcast.16, bf16[192,1536]{1,0:T(8,128)(2,1)} %bitcast.13, bf16[16,1536]{1,0:T(8,128)(2,1)} %bitcast.19, s32[1,192]{1,0:T(1,128)} %refs_5_.5), custom_call_target="tpu_custom_call" | custom-call | tf_op jit(solution)/shard_map/pack/pallas_call | solution.py:102
  8.3 0.3 collective-permute-start.5
  8.6 3.7 %copy-done = bf16[1536,3072]{1,0:T(8,128)(2,1)S(1)} copy-done((bf16[1536,3072]{1,0:T(8,128)(2,1)S(1)}, bf16[1536,3072]{1,0:T(8,128)(2,1)}, u32[]{:S(2)}) %copy-start) | copy-done | bytes 9437208
  12.3 0.0 copy-start.5
  12.3 0.0 copy-start.6
  12.3 0.0 copy-start.7
  12.3 0.6 load_weights.1.refs_7_.refs_5_.weights.refs_2_
  12.9 0.4 copy-done.1
  13.3 0.2 copy-done.2
  13.5 0.2 copy-done.3
  13.7 0.0 copy-done.6
  13.7 0.5 prepare.1
  14.2 1.3 %collective-permute-start = (bf16[608,256]{1,0:T(8,128)(2,1)S(1)}, bf16[608,256]{1,0:T(8,128)(2,1)S(1)}, u32[]{:S(2)}, u32[]{:S(2)}) collective-permute-start(bf16[608,256]{1,0:T(8,128)(2,1)S(1)} %get-tuple-element.30), channel_id=1, source_target_pairs={{0,4},{4,0},{8,12},{12,8},{1,5},{5,1},{9,13},{13,9},{2,6},{6,2},{1... | collective-permute-start | bytes 933896 | tf_op jit(solution)/shard_map/ppermute | solution.py:33
  15.5 11.0 %collective-permute-done.1.refs_0_.refs_2_ = bf16[624,256]{1,0:T(8,128)(2,1)S(1)} collective-permute-done((bf16[624,256]{1,0:T(8,128)(2,1)}, bf16[624,256]{1,0:T(8,128)(2,1)S(1)}, u32[]{:S(2)}, u32[]{:S(2)}) %collective-permute-start.1) | collective-permute-done | bytes 319520 | tf_op jit(solution)/shard_map/ppermute | solution.py:33
  26.6 0.0 collective-permute-done.2.refs_1_.refs_3_
  26.6 4.1 %collective-permute-start.4 = (bf16[416,256]{1,0:T(8,128)(2,1)S(1)}, bf16[416,256]{1,0:T(8,128)(2,1)S(1)}, u32[]{:S(2)}, u32[]{:S(2)}) collective-permute-start(bf16[416,256]{1,0:T(8,128)(2,1)S(1)} %hold.3), channel_id=1, source_target_pairs={{0,12},{4,8},{8,4},{12,0},{1,13},{5,9},{9,5},{13,1},{2,14},{6,10},... | collective-permute-start | bytes 638984 | tf_op jit(solution)/shard_map/ppermute | solution.py:33
  30.7 7.2 %collective-permute-start.3 = (bf16[416,256]{1,0:T(8,128)(2,1)S(1)}, bf16[416,256]{1,0:T(8,128)(2,1)S(1)}, u32[]{:S(2)}, u32[]{:S(2)}) collective-permute-start(bf16[416,256]{1,0:T(8,128)(2,1)S(1)} %hold.2), channel_id=1, source_target_pairs={{0,8},{4,12},{8,0},{12,4},{1,9},{5,13},{9,1},{13,5},{2,10},{6,14},... | collective-permute-start | bytes 638984 | tf_op jit(solution)/shard_map/ppermute | solution.py:33
  37.9 0.0 collective-permute-done.5.refs_1_
  37.9 3.4 %attend.1 = (bf16[192,256]{1,0:T(8,128)(2,1)S(1)}, bf16[192,256]{1,0:T(8,128)(2,1)S(1)}, bf16[192,256]{1,0:T(8,128)(2,1)S(1)}, bf16[192,256]{1,0:T(8,128)(2,1)S(1)}) custom-call(f32[1,64]{1,0:T(1,128)S(1)} %get-tuple-element.28.bias, bf16[624,256]{1,0:T(8,128)(2,1)S(1)} %get-tuple-element.35.refs_0_, bf16[624,256]{1,0:T(8,128)(2,1)S(1)} %collective-permute-done.5.refs_1_, ...), custom_call_target="tpu_custom_call" | custom-call | tf_op jit(solution)/shard_map/attend/pallas_call | solution.py:254
  41.3 5.3 %collective-permute-start.6 = (bf16[192,256]{1,0:T(8,128)(2,1)S(1)}, bf16[192,256]{1,0:T(8,128)(2,1)S(1)}, u32[]{:S(2)}, u32[]{:S(2)}) collective-permute-start(bf16[192,256]{1,0:T(8,128)(2,1)S(1)} %get-tuple-element.37), channel_id=1, source_target_pairs={{0,1},{1,2},{2,3},{3,0},{4,5},{5,6},{6,7},{7,4},{8,9},{9,10},{10,1... | collective-permute-start | bytes 294920 | tf_op jit(solution)/shard_map/ppermute | solution.py:29
  46.6 0.1 collective-permute-start.7
  46.7 0.8 %weigh.1 = (f32[192,128]{1,0:T(8,128)S(1)}, f32[192,128]{1,0:T(8,128)S(1)}, f32[192,128]{1,0:T(8,128)S(1)}, f32[192,128]{1,0:T(8,128)}) custom-call(bf16[624,256]{1,0:T(8,128)(2,1)S(1)} %get-tuple-element.35.refs_0_, bf16[624,256]{1,0:T(8,128)(2,1)S(1)} %collective-permute-done.5.refs_1_, bf16[624,256]{1,0:T(8,128)(2,1)S(1)} %collective-permute-done.1.refs_0_.refs_2_, ...), custom_call_target="tpu_custom_call" | custom-call | tf_op jit(solution)/shard_map/weigh/pallas_call | solution.py:286
  47.5 0.7 %collective-permute-done.6.refs_1_ = bf16[192,256]{1,0:T(8,128)(2,1)S(1)} collective-permute-done((bf16[192,256]{1,0:T(8,128)(2,1)S(1)}, bf16[192,256]{1,0:T(8,128)(2,1)S(1)}, u32[]{:S(2)}, u32[]{:S(2)}) %collective-permute-start.6) | collective-permute-done | bytes 98336 | tf_op jit(solution)/shard_map/ppermute | solution.py:29
  48.3 1.0 %collective-permute-done.7.refs_4_ = bf16[192,256]{1,0:T(8,128)(2,1)S(1)} collective-permute-done((bf16[192,256]{1,0:T(8,128)(2,1)S(1)}, bf16[192,256]{1,0:T(8,128)(2,1)S(1)}, u32[]{:S(2)}, u32[]{:S(2)}) %collective-permute-start.7) | collective-permute-done | bytes 98336 | tf_op jit(solution)/shard_map/ppermute | solution.py:29
  49.2 0.1 blend.1
  49.3 0.4 collective-permute-start.9
  49.7 2.6 %collective-permute-start.10 = (bf16[96,256]{1,0:T(8,128)(2,1)S(1)}, bf16[96,256]{1,0:T(8,128)(2,1)S(1)}, u32[]{:S(2)}, u32[]{:S(2)}) collective-permute-start(bf16[96,256]{1,0:T(8,128)(2,1)S(1)} %get-tuple-element.46), channel_id=1, source_target_pairs={{0,8},{4,12},{8,0},{12,4},{1,9},{5,13},{9,1},{13,5},{2,10},{6,14},... | collective-permute-start | bytes 147464 | tf_op jit(solution)/shard_map/ppermute | solution.py:33
  52.3 0.0 collective-permute-done.refs_1_
  52.3 0.6 collective-permute-start.11
  53.0 0.0 collective-permute-done.4.refs_3_
  53.0 0.0 collective-permute-done.3.refs_2_
  53.0 1.8 %attend_half.1 = (bf16[192,256]{1,0:T(8,128)(2,1)S(1)}, bf16[192,256]{1,0:T(8,128)(2,1)S(1)}) custom-call(f32[1,64]{1,0:T(1,128)S(1)} %get-tuple-element.28.bias, bf16[608,256]{1,0:T(8,128)(2,1)S(1)} %get-tuple-element.29.refs_0_, bf16[608,256]{1,0:T(8,128)(2,1)S(1)} %collective-permute-done.refs_1_, bf16[416,256]{1,0:T(8,128)(2,1)S(1)} %collective-permute-done.3.refs_2_, ...), custom_call_target="tpu_custom_call" | custom-call | tf_op jit(solution)/shard_map/attend_half/pallas_call | solution.py:189
  54.8 0.1 collective-permute-start.8
  54.8 0.1 collective-permute-done.9.refs_2_.refs_1_
  54.9 0.0 collective-permute-done.10.refs_3_.refs_2_
  54.9 2.2 %collective-permute-done.11.refs_4_.refs_3_ = bf16[96,256]{1,0:T(8,128)(2,1)S(1)} collective-permute-done((bf16[96,256]{1,0:T(8,128)(2,1)S(1)}, bf16[96,256]{1,0:T(8,128)(2,1)S(1)}, u32[]{:S(2)}, u32[]{:S(2)}) %collective-permute-start.11) | collective-permute-done | bytes 49184 | tf_op jit(solution)/shard_map/ppermute | solution.py:33
  57.2 3.5 %collective-permute-start.14 = (bf16[96,1024]{1,0:T(8,128)(2,1)S(1)}, bf16[96,1024]{1,0:T(8,128)(2,1)S(1)}, u32[]{:S(2)}, u32[]{:S(2)}) collective-permute-start(bf16[96,1024]{1,0:T(8,128)(2,1)S(1)} %collect.1.left), channel_id=1, source_target_pairs={{0,3},{1,0},{2,1},{3,2},{4,7},{5,4},{6,5},{7,6},{8,11},{9,8},{10,9... | collective-permute-start | bytes 589832 | tf_op jit(solution)/shard_map/ppermute | solution.py:29
  60.7 0.0 collective-permute-done.8.refs_1_
  60.7 1.0 %collective-permute-start.13 = (bf16[96,512]{1,0:T(8,128)(2,1)S(1)}, bf16[96,512]{1,0:T(8,128)(2,1)S(1)}, u32[]{:S(2)}, u32[]{:S(2)}) collective-permute-start(bf16[96,512]{1,0:T(8,128)(2,1)S(1)} %get-tuple-element.48.left), channel_id=1, source_target_pairs={{0,3},{1,0},{2,1},{3,2},{4,7},{5,4},{6,5},{7,6},{8,11},{9,8},{10,9... | collective-permute-start | bytes 294920 | tf_op jit(solution)/shard_map/ppermute | solution.py:29
  61.8 1.2 %collective-permute-start.12 = (bf16[96,512]{1,0:T(8,128)(2,1)S(1)}, bf16[96,512]{1,0:T(8,128)(2,1)S(1)}, u32[]{:S(2)}, u32[]{:S(2)}) collective-permute-start(bf16[96,512]{1,0:T(8,128)(2,1)S(1)} %get-tuple-element.49.right), channel_id=1, source_target_pairs={{0,1},{1,2},{2,3},{3,0},{4,5},{5,6},{6,7},{7,4},{8,9},{9,10},{10,1... | collective-permute-start | bytes 294920 | tf_op jit(solution)/shard_map/ppermute | solution.py:29
  63.0 2.4 %collective-permute-done.14.right = bf16[96,1024]{1,0:T(8,128)(2,1)S(1)} collective-permute-done((bf16[96,1024]{1,0:T(8,128)(2,1)S(1)}, bf16[96,1024]{1,0:T(8,128)(2,1)S(1)}, u32[]{:S(2)}, u32[]{:S(2)}) %collective-permute-start.14) | collective-permute-done | bytes 196640 | tf_op jit(solution)/shard_map/ppermute | solution.py:29
  65.4 1.4 %project_begin.1.refs_3_ = f32[192,3072]{1,0:T(8,128)S(1)} custom-call(bf16[96,1024]{1,0:T(8,128)(2,1)S(1)} %collect.1.left, bf16[96,1024]{1,0:T(8,128)(2,1)S(1)} %collective-permute-done.14.right, bf16[1536,3072]{1,0:T(8,128)(2,1)S(1)} %load_weights.1.refs_7_.refs_5_.weights.refs_2_), custom_call_target="tpu_custom_call" | custom-call | tf_op jit(solution)/shard_map/project_begin/pallas_call | solution.py:402
  66.8 0.0 collective-permute-done.13.from_next
  66.8 0.0 collective-permute-done.12.from_prev
  66.8 1.6 %project_end.1 = bf16[192,3072]{1,0:T(8,128)(2,1)} custom-call(bf16[96,512]{1,0:T(8,128)(2,1)S(1)} %get-tuple-element.48.left, bf16[96,512]{1,0:T(8,128)(2,1)S(1)} %get-tuple-element.49.right, bf16[96,512]{1,0:T(8,128)(2,1)S(1)} %collective-permute-done.12.from_prev, bf16[96,512]{1,0:T(8,128)(2,1)S(1)} %collective-permute-done.13.from_next, ...), custom_call_target="tpu_custom_call" | custom-call | tf_op jit(solution)/shard_map/project_end/pallas_call | solution.py:449
  (12 shorter events, 0.1 us)
Async XLA Ops:
  2.2 24.4 %collective-permute-start.1 = (bf16[624,256]{1,0:T(8,128)(2,1)}, bf16[624,256]{1,0:T(8,128)(2,1)S(1)}, u32[]{:S(2)}, u32[]{:S(2)}) collective-permute-start(bf16[624,256]{1,0:T(8,128)(2,1)} %get-tuple-element.32), channel_id=1, source_target_pairs={{0,8},{4,12},{8,0},{12,4},{1,9},{5,13},{9,1},{13,5},{2,10},{6,14},... | collective-permute-start | bytes 958472 | tf_op jit(solution)/shard_map/ppermute | solution.py:33
  5.4 21.2 %collective-permute-start.2 = (bf16[624,256]{1,0:T(8,128)(2,1)}, bf16[624,256]{1,0:T(8,128)(2,1)S(1)}, u32[]{:S(2)}, u32[]{:S(2)}) collective-permute-start(bf16[624,256]{1,0:T(8,128)(2,1)} %get-tuple-element.33), channel_id=1, source_target_pairs={{0,12},{4,8},{8,4},{12,0},{1,13},{5,9},{9,5},{13,1},{2,14},{6,10},... | collective-permute-start | bytes 958472 | tf_op jit(solution)/shard_map/ppermute | solution.py:33
  8.3 29.6 %collective-permute-start.5 = (bf16[624,256]{1,0:T(8,128)(2,1)}, bf16[624,256]{1,0:T(8,128)(2,1)S(1)}, u32[]{:S(2)}, u32[]{:S(2)}) collective-permute-start(bf16[624,256]{1,0:T(8,128)(2,1)} %pack.3), channel_id=1, source_target_pairs={{0,4},{4,0},{8,12},{12,8},{1,5},{5,1},{9,13},{13,9},{2,6},{6,2},{1... | collective-permute-start | bytes 958472 | tf_op jit(solution)/shard_map/ppermute | solution.py:33
  8.6 3.7 %copy-start = (bf16[1536,3072]{1,0:T(8,128)(2,1)S(1)}, bf16[1536,3072]{1,0:T(8,128)(2,1)}, u32[]{:S(2)}) copy-start(bf16[1536,3072]{1,0:T(8,128)(2,1)} %w_out.1) | copy-start | bytes 28311556
  12.2 1.1 %copy-start.1 = (bf16[1,192,1536]{2,1,0:T(8,128)(2,1)S(1)}, bf16[1,192,1536]{2,1,0:T(8,128)(2,1)}, u32[]{:S(2)}) copy-start(bf16[1,192,1536]{2,1,0:T(8,128)(2,1)} %param.8) | copy-start | bytes 1769476
  12.2 1.2 %copy-start.2 = (bf16[1,192,1536]{2,1,0:T(8,128)(2,1)S(1)}, bf16[1,192,1536]{2,1,0:T(8,128)(2,1)}, u32[]{:S(2)}) copy-start(bf16[1,192,1536]{2,1,0:T(8,128)(2,1)} %param.9) | copy-start | bytes 1769476
  12.2 1.4 %copy-start.3 = (bf16[1,192,1536]{2,1,0:T(8,128)(2,1)S(1)}, bf16[1,192,1536]{2,1,0:T(8,128)(2,1)}, u32[]{:S(2)}) copy-start(bf16[1,192,1536]{2,1,0:T(8,128)(2,1)} %param.10) | copy-start | bytes 1769476
  12.2 1.4 %copy-start.4 = (bf16[1,16,1536]{2,1,0:T(8,128)(2,1)S(1)}, bf16[1,16,1536]{2,1,0:T(8,128)(2,1)}, u32[]{:S(2)}) copy-start(bf16[1,16,1536]{2,1,0:T(8,128)(2,1)} %param.11) | copy-start | bytes 147460
  12.3 1.4 %copy-start.5 = (bf16[1,16,1536]{2,1,0:T(8,128)(2,1)S(1)}, bf16[1,16,1536]{2,1,0:T(8,128)(2,1)}, u32[]{:S(2)}) copy-start(bf16[1,16,1536]{2,1,0:T(8,128)(2,1)} %param.12) | copy-start | bytes 147460
  12.3 1.4 %copy-start.6 = (s32[1,192]{1,0:T(1,128)S(1)}, s32[1,192]{1,0:T(1,128)}, u32[]{:S(2)}) copy-start(s32[1,192]{1,0:T(1,128)} %refs_5_.5) | copy-start | bytes 2308
  12.3 1.4 %copy-start.7 = (s32[1,64]{1,0:T(1,128)S(1)}, s32[1,64]{1,0:T(1,128)}, u32[]{:S(2)}) copy-start(s32[1,64]{1,0:T(1,128)} %refs_6_.1) | copy-start | bytes 772
  14.2 38.1 %collective-permute-start = (bf16[608,256]{1,0:T(8,128)(2,1)S(1)}, bf16[608,256]{1,0:T(8,128)(2,1)S(1)}, u32[]{:S(2)}, u32[]{:S(2)}) collective-permute-start(bf16[608,256]{1,0:T(8,128)(2,1)S(1)} %get-tuple-element.30), channel_id=1, source_target_pairs={{0,4},{4,0},{8,12},{12,8},{1,5},{5,1},{9,13},{13,9},{2,6},{6,2},{1... | collective-permute-start | bytes 933896 | tf_op jit(solution)/shard_map/ppermute | solution.py:33
  26.6 26.4 %collective-permute-start.4 = (bf16[416,256]{1,0:T(8,128)(2,1)S(1)}, bf16[416,256]{1,0:T(8,128)(2,1)S(1)}, u32[]{:S(2)}, u32[]{:S(2)}) collective-permute-start(bf16[416,256]{1,0:T(8,128)(2,1)S(1)} %hold.3), channel_id=1, source_target_pairs={{0,12},{4,8},{8,4},{12,0},{1,13},{5,9},{9,5},{13,1},{2,14},{6,10},... | collective-permute-start | bytes 638984 | tf_op jit(solution)/shard_map/ppermute | solution.py:33
  30.7 22.3 %collective-permute-start.3 = (bf16[416,256]{1,0:T(8,128)(2,1)S(1)}, bf16[416,256]{1,0:T(8,128)(2,1)S(1)}, u32[]{:S(2)}, u32[]{:S(2)}) collective-permute-start(bf16[416,256]{1,0:T(8,128)(2,1)S(1)} %hold.2), channel_id=1, source_target_pairs={{0,8},{4,12},{8,0},{12,4},{1,9},{5,13},{9,1},{13,5},{2,10},{6,14},... | collective-permute-start | bytes 638984 | tf_op jit(solution)/shard_map/ppermute | solution.py:33
  41.3 7.0 %collective-permute-start.6 = (bf16[192,256]{1,0:T(8,128)(2,1)S(1)}, bf16[192,256]{1,0:T(8,128)(2,1)S(1)}, u32[]{:S(2)}, u32[]{:S(2)}) collective-permute-start(bf16[192,256]{1,0:T(8,128)(2,1)S(1)} %get-tuple-element.37), channel_id=1, source_target_pairs={{0,1},{1,2},{2,3},{3,0},{4,5},{5,6},{6,7},{7,4},{8,9},{9,10},{10,1... | collective-permute-start | bytes 294920 | tf_op jit(solution)/shard_map/ppermute | solution.py:29
  46.6 2.6 %collective-permute-start.7 = (bf16[192,256]{1,0:T(8,128)(2,1)S(1)}, bf16[192,256]{1,0:T(8,128)(2,1)S(1)}, u32[]{:S(2)}, u32[]{:S(2)}) collective-permute-start(bf16[192,256]{1,0:T(8,128)(2,1)S(1)} %get-tuple-element.40), channel_id=1, source_target_pairs={{0,1},{1,2},{2,3},{3,0},{4,5},{5,6},{6,7},{7,4},{8,9},{9,10},{10,1... | collective-permute-start | bytes 294920 | tf_op jit(solution)/shard_map/ppermute | solution.py:29
  49.3 5.6 %collective-permute-start.9 = (bf16[96,256]{1,0:T(8,128)(2,1)S(1)}, bf16[96,256]{1,0:T(8,128)(2,1)S(1)}, u32[]{:S(2)}, u32[]{:S(2)}) collective-permute-start(bf16[96,256]{1,0:T(8,128)(2,1)S(1)} %get-tuple-element.45), channel_id=1, source_target_pairs={{0,4},{4,0},{8,12},{12,8},{1,5},{5,1},{9,13},{13,9},{2,6},{6,2},{1... | collective-permute-start | bytes 147464 | tf_op jit(solution)/shard_map/ppermute | solution.py:33
  49.7 5.2 %collective-permute-start.10 = (bf16[96,256]{1,0:T(8,128)(2,1)S(1)}, bf16[96,256]{1,0:T(8,128)(2,1)S(1)}, u32[]{:S(2)}, u32[]{:S(2)}) collective-permute-start(bf16[96,256]{1,0:T(8,128)(2,1)S(1)} %get-tuple-element.46), channel_id=1, source_target_pairs={{0,8},{4,12},{8,0},{12,4},{1,9},{5,13},{9,1},{13,5},{2,10},{6,14},... | collective-permute-start | bytes 147464 | tf_op jit(solution)/shard_map/ppermute | solution.py:33
  52.3 4.8 %collective-permute-start.11 = (bf16[96,256]{1,0:T(8,128)(2,1)S(1)}, bf16[96,256]{1,0:T(8,128)(2,1)S(1)}, u32[]{:S(2)}, u32[]{:S(2)}) collective-permute-start(bf16[96,256]{1,0:T(8,128)(2,1)S(1)} %get-tuple-element.47), channel_id=1, source_target_pairs={{0,12},{4,8},{8,4},{12,0},{1,13},{5,9},{9,5},{13,1},{2,14},{6,10},... | collective-permute-start | bytes 147464 | tf_op jit(solution)/shard_map/ppermute | solution.py:33
  54.8 5.9 %collective-permute-start.8 = (bf16[192,256]{1,0:T(8,128)(2,1)S(1)}, bf16[192,256]{1,0:T(8,128)(2,1)S(1)}, u32[]{:S(2)}, u32[]{:S(2)}) collective-permute-start(bf16[192,256]{1,0:T(8,128)(2,1)S(1)} %get-tuple-element.44), channel_id=1, source_target_pairs={{0,4},{4,0},{8,12},{12,8},{1,5},{5,1},{9,13},{13,9},{2,6},{6,2},{1... | collective-permute-start | bytes 294920 | tf_op jit(solution)/shard_map/ppermute | solution.py:33
  57.2 8.2 %collective-permute-start.14 = (bf16[96,1024]{1,0:T(8,128)(2,1)S(1)}, bf16[96,1024]{1,0:T(8,128)(2,1)S(1)}, u32[]{:S(2)}, u32[]{:S(2)}) collective-permute-start(bf16[96,1024]{1,0:T(8,128)(2,1)S(1)} %collect.1.left), channel_id=1, source_target_pairs={{0,3},{1,0},{2,1},{3,2},{4,7},{5,4},{6,5},{7,6},{8,11},{9,8},{10,9... | collective-permute-start | bytes 589832 | tf_op jit(solution)/shard_map/ppermute | solution.py:29
  60.7 6.1 %collective-permute-start.13 = (bf16[96,512]{1,0:T(8,128)(2,1)S(1)}, bf16[96,512]{1,0:T(8,128)(2,1)S(1)}, u32[]{:S(2)}, u32[]{:S(2)}) collective-permute-start(bf16[96,512]{1,0:T(8,128)(2,1)S(1)} %get-tuple-element.48.left), channel_id=1, source_target_pairs={{0,3},{1,0},{2,1},{3,2},{4,7},{5,4},{6,5},{7,6},{8,11},{9,8},{10,9... | collective-permute-start | bytes 294920 | tf_op jit(solution)/shard_map/ppermute | solution.py:29
  61.8 5.1 %collective-permute-start.12 = (bf16[96,512]{1,0:T(8,128)(2,1)S(1)}, bf16[96,512]{1,0:T(8,128)(2,1)S(1)}, u32[]{:S(2)}, u32[]{:S(2)}) collective-permute-start(bf16[96,512]{1,0:T(8,128)(2,1)S(1)} %get-tuple-element.49.right), channel_id=1, source_target_pairs={{0,1},{1,2},{2,3},{3,0},{4,5},{5,6},{6,7},{7,4},{8,9},{9,10},{10,1... | collective-permute-start | bytes 294920 | tf_op jit(solution)/shard_map/ppermute | solution.py:29

commit v5 on v4

--- a/solution.py
+++ b/solution.py
@@ -109,7 +109,7 @@
             pltpu.VMEM(blend.shape, blend.dtype),
             pltpu.VMEM(wide_shape(blend), jnp.float32),
         ],
-        compiler_params=LARGE,
+        compiler_params=SMALL,
         cost_estimate=NO_COST,
         name="pack",
     )(*sources, blend)
@@ -166,36 +166,119 @@
     return (result / total).astype(jnp.bfloat16)
 
 
-def half_kernel(group, image_rows, text_rows, bias, *refs):
-    blocks, outs, (keys, values) = refs[:group], refs[-2 - group // 2 : -2], refs[-2:]
-    key_rows = image_rows + text_rows
-    for distance, block in enumerate(blocks):
-        source = partner(distance, group)
-        image = pl.ds(distance * image_rows, image_rows)
-        text = pl.ds(pl.multiple_of(group * image_rows + source * text_rows, text_rows), text_rows)
-        key_at = image_rows if distance < group // 2 else 0
-        for ref, at in ((keys, key_at), (values, key_at + key_rows)):
-            ref[image] = block[at : at + image_rows]
+def fill(keys, values, mask, bias, blocks, sources, starts, group, image_rows, text_rows):
+    key_rows, texts = image_rows + text_rows, group * text_rows
+    for ref, offset in ((keys, 0), (values, key_rows)):
+        ref[:texts] = jnp.zeros((texts, ref.shape[1]), ref.dtype)
+        for index, (block, source, start) in enumerate(zip(blocks, sources, starts)):
+            at, image = start + offset, texts + index * image_rows
+            ref[image : image + image_rows] = block[at : at + image_rows]
+            text = pl.ds(pl.multiple_of(source * text_rows, text_rows), text_rows)
             ref[text] = block[at + image_rows : at + key_rows]
+    lane = lax.broadcasted_iota(jnp.int32, bias.shape, 1)
+    here = jnp.zeros(bias.shape, jnp.int32)
+    for source in sources:
+        inside = (lane >= source * text_rows) & (lane < (source + 1) * text_rows)
+        here = jnp.where(inside, 1, here)
+    mask[...] = jnp.zeros_like(mask)
+    mask[:, :texts] = jnp.where(here == 1, bias[...], -jnp.inf)
+
+
+def sum_up(query, key, value, mask, peak=None):
+    scores = lax.dot_general(
+        query, key, (((1,), (1,)), ((), ())), preferred_element_type=jnp.float32
+    )
+    scores = scores + mask
+    highest = jnp.max(scores, axis=1, keepdims=True)
+    highest = jnp.broadcast_to(highest, (scores.shape[0], HEAD_DIM))
+    if peak is not None:
+        highest = jnp.maximum(highest, peak)
+    tiles = -(-scores.shape[1] // HEAD_DIM)
+    wide = jnp.concatenate([highest] * tiles, axis=1)[:, : scores.shape[1]]
+    weights = jnp.exp2((scores - wide) * EXP2_SCALE)
+    total = jnp.broadcast_to(jnp.sum(weights, axis=1, keepdims=True), highest.shape)
+    product = jnp.dot(weights.astype(jnp.bfloat16), value, preferred_element_type=jnp.float32)
+    return product, total, highest
+
+
+def early_kernel(group, image_rows, text_rows, bias, *refs):
+    halfway = group // 2
+    blocks = refs[: group - 1]
+    products, totals, peaks, keys, values, mask = refs[-6:]
+    distances = [d for d in range(group) if d != halfway]
+    sources = [partner(d, group) for d in distances]
+    starts = [image_rows if d < halfway else 0 for d in distances]
+    fill(keys, values, mask, bias, blocks, sources, starts, group, image_rows, text_rows)
     for at in range(0, keys.shape[1], HEAD_DIM):
         head = slice(at, at + HEAD_DIM)
-        for block, out in zip(blocks, outs):
-            out[:, head] = soften(block[:image_rows, head], keys[:, head], values[:, head], bias[...])
+        for index in range(halfway):
+            rows = slice(index * image_rows, (index + 1) * image_rows)
+            product, total, peak = sum_up(
+                blocks[index][:image_rows, head],
+                keys[:, head],
+                values[:, head],
+                mask[...],
+            )
+            products[rows, head] = product
+            totals[rows, head] = total
+            peaks[rows, head] = peak
+
+
+def late_kernel(group, image_rows, text_rows, bias, products, totals, peaks, *refs):
+    halfway = group // 2
+    near, block = refs[:halfway], refs[halfway]
+    outs, (keys, values, mask) = refs[-3 - halfway : -3], refs[-3:]
+    sources = [partner(halfway, group)]
+    fill(keys, values, mask, bias, [block], sources, [0], group, image_rows, text_rows)
+    for at in range(0, keys.shape[1], HEAD_DIM):
+        head = slice(at, at + HEAD_DIM)
+        for index, out in enumerate(outs):
+            rows = slice(index * image_rows, (index + 1) * image_rows)
+            before = peaks[rows, head]
+            product, total, peak = sum_up(
+                near[index][:image_rows, head],
+                keys[:, head],
+                values[:, head],
+                mask[...],
+                before,
+            )
+            scale = jnp.exp2((before - peak) * EXP2_SCALE)
+            total += totals[rows, head] * scale
+            product += products[rows, head] * scale
+            out[:, head] = (product / total).astype(jnp.bfloat16)
 
 
 def attend_half(blocks, bias, image_rows, text_rows, after):
     group, width = len(blocks), blocks[0].shape[1]
-    keys = pltpu.VMEM((group * (image_rows + text_rows), width), jnp.bfloat16)
-    return pl.pallas_call(
-        functools.partial(half_kernel, group, image_rows, text_rows),
-        out_shape=[jax.ShapeDtypeStruct((image_rows, width), jnp.bfloat16)] * (group // 2),
-        in_specs=[VMEM] * (1 + group) + [ANY] * len(after),
-        out_specs=[VMEM] * (group // 2),
-        scratch_shapes=[keys, keys],
-        compiler_params=SMALL,
-        cost_estimate=NO_COST,
-        name="attend_half",
-    )(bias, *blocks, *after)
+    halfway = group // 2
+    near, last = list(blocks[:halfway]), blocks[halfway]
+    others = near + list(blocks[halfway + 1 :])
+    texts = group * text_rows
+    total = jax.ShapeDtypeStruct((halfway * image_rows, width), jnp.float32)
+    count = len(others) * image_rows + texts
+    keys, mask = pltpu.VMEM((count, width), jnp.bfloat16), pltpu.VMEM((1, count), jnp.float32)
+    sums = pl.pallas_call(
+        functools.partial(early_kernel, group, image_rows, text_rows),
+        out_shape=[total] * 3,
+        in_specs=[VMEM] * group + [ANY] * len(after),
+        out_specs=[VMEM] * 3,
+        scratch_shapes=[keys, keys, mask],
+        compiler_params=SMALL,
+        cost_estimate=NO_COST,
+        name="attend_early",
+    )(bias, *others, *after)
+    count = image_rows + texts
+    keys, mask = pltpu.VMEM((count, width), jnp.bfloat16), pltpu.VMEM((1, count), jnp.float32)
+    return pl.pallas_call(
+        functools.partial(late_kernel, group, image_rows, text_rows),
+        out_shape=[jax.ShapeDtypeStruct((image_rows, width), jnp.bfloat16)] * halfway,
+        in_specs=[VMEM] * (5 + halfway),
+        out_specs=[VMEM] * halfway,
+        scratch_shapes=[keys, keys, mask],
+        compiler_params=SMALL,
+        cost_estimate=NO_COST,
+        name="attend_late",
+    )(bias, *sums, *near, last)
 
 
 def merge_kernel(group, *refs):
@@ -539,20 +622,22 @@
     image_rows, text_rows = query.shape[1], key_text.shape[1]
     message_rows = 3 * image_rows + 2 * text_rows
     sources = [query[0], key_image[0], key_text[0], value_image[0], value_text[0]]
-
+    sources = [pltpu.with_memory_space_constraint(source, pltpu.HBM) for source in sources]
+
+    blend_there = pltpu.with_memory_space_constraint(blend, pltpu.HBM)
     far, near = tuple(range(halfway, group)), tuple(range(1, halfway))
     received = [None] * group
     for distances in (far, near):
-        packed = pack(sources, blend, heads, group, distances)
+        packed = pack(sources, blend_there, heads, group, distances)
         for distance, message in zip(distances, packed):
             received[distance] = swapped(message, distance)
     weights = load_weights(w_out, [])
     prepared = prepare(sources, blend, prompt_ids, heads, group, [weights])
     received[0], packed, bias = prepared[0], prepared[1:-1], prepared[-1]
     first = received
-    second = [packed[0]] + [swapped(packed[d], d) for d in near]
+    second = [packed[0]] + [swapped(hold(packed[d], [first[halfway]]), d) for d in near]
     for distance in far:
-        second.append(swapped(hold(packed[distance], first[halfway:]), distance))
+        second.append(swapped(hold(packed[distance], first[halfway:] if distance == halfway else first[halfway : halfway + 1]), distance))
     blend_weights = weigh(first, message_rows, image_rows)
 
     def strips_of(blocks):
@@ -577,7 +662,7 @@
     begun = returned(mixed)
 
     results = returned(results_of(second, [mixed[0], weights]))
-    left, right = merge(results, group, begun[1:])
+    left, right = merge(results, group, [])
     from_prev, from_next = shifted(right, "win", 1), shifted(left, "win", -1)
     begins = collect(begun)
     total = project_begin(begins, shifted(begins, "win", -1), weights)

time: 68.9 us -> 67.2 us (0.975)
  starting transfers between devices: 32 us -> 27.1 us
  waiting for transfers between devices: 17.4 us -> 21 us
  local copies, waits for them, and re-layouts: 4.43 us -> 3.72 us
    ppermute x10, waiting for transfers between devices: 13.3 us -> 17.4 us  [swapped(): lax.ppermute(block, 'seq', [(i, i ^ distance) for i in range(lax.axis_siz...]
    ppermute x5, starting transfers between devices: 11.2 us -> 7.73 us  [shifted(): lax.ppermute(block, axis, [(i, (i + distance) % count) for i in range(cou...]
    pallas_call x2, Pallas kernels: 3.98 us -> 2.43 us  [pack(): pl.pallas_call(functools.partial(pack_kernel, heads, group, distances, le...]
    ppermute x10, starting transfers between devices: 20.8 us -> 19.4 us  [swapped(): lax.ppermute(block, 'seq', [(i, i ^ distance) for i in range(lax.axis_siz...]
    pallas_call x1, Pallas kernels: 0.53 us -> 1.74 us  [prepare(): pl.pallas_call(functools.partial(prepare_kernel, heads, group, len(source...]
    unnamed x16 -> x6, local copies, waits for them, and re-layouts: 4.43 us -> 3.72 us
    pallas_call x1 -> x2, Pallas kernels: 1.8 us -> 2.4 us  [the longest x1 1.59 us: attend_half(): pl.pallas_call(functools.partial(early_kernel, group, image_rows, text_ro...]
  transfers between devices with their start and end apart: 15 -> 15, of which waited for: 6 -> 6; matrix products, arithmetic and copies ran while one was open for 0% -> 0% of each run, Pallas kernels for 16% -> 18%
where the time goes in v5:
time: 67.2 us; the launch traced here: 66.5 us
  starting transfers between devices  27.1 us (40%)
  waiting for transfers between devices  21 us (31%)
  Pallas kernels  14.6 us (22%)
  local copies, waits for them, and re-layouts  3.72 us (6%)
    ppermute x10, starting transfers between devices, swapped(): lax.ppermute(block, 'seq', [(i, i ^ distance) for i in range(lax.axis_siz...  19.4 us
    ppermute x10, waiting for transfers between devices, swapped(): lax.ppermute(block, 'seq', [(i, i ^ distance) for i in range(lax.axis_siz...  17.4 us
    ppermute x5, starting transfers between devices, shifted(): lax.ppermute(block, axis, [(i, (i + distance) % count) for i in range(cou...  7.73 us
    unnamed x6, local copies, waits for them, and re-layouts  3.72 us
    ppermute x5, waiting for transfers between devices, shifted(): lax.ppermute(block, axis, [(i, (i + distance) % count) for i in range(cou...  3.53 us
    pallas_call x1, Pallas kernels, attend(): pl.pallas_call(functools.partial(attend_kernel, group, image_rows, text_r...  3.42 us
    pallas_call x2, Pallas kernels, pack(): pl.pallas_call(functools.partial(pack_kernel, heads, group, distances, le...  2.43 us
    pallas_call x1, Pallas kernels, prepare(): pl.pallas_call(functools.partial(prepare_kernel, heads, group, len(source...  1.74 us
  transfers between devices with their start and end apart: 15, of which 6 were waited for; matrix products, arithmetic and copies ran while one was open for 0% of the time, Pallas kernels for 18%

profile of v5, /device:TPU:1, one launch (start us, length us, event | category | flops | bytes accessed | tf_op | source)
XLA Modules:
  0.0 66.5 jit_solution(10928428249322970043)
XLA Ops:
  0.0 1.3 %pack.2 = (bf16[624,256]{1,0:T(8,128)(2,1)S(1)}, bf16[624,256]{1,0:T(8,128)(2,1)S(1)}) custom-call(bf16[192,1536]{1,0:T(8,128)(2,1)} %bitcast.6, bf16[192,1536]{1,0:T(8,128)(2,1)} %bitcast.9, bf16[16,1536]{1,0:T(8,128)(2,1)} %bitcast.15, bf16[192,1536]{1,0:T(8,128)(2,1)} %bitcast.12, bf16[16,1536]{1,0:T(8,128)(2,1)} %bitcast.18, s32[1,192]{1,0:T(1,128)} %refs_5_.5), custom_call_target="tpu_custom_call" | custom-call | tf_op jit(solution)/shard_map/pack/pallas_call | solution.py:102
  1.3 3.2 %collective-permute-start = (bf16[624,256]{1,0:T(8,128)(2,1)S(1)}, bf16[624,256]{1,0:T(8,128)(2,1)S(1)}, u32[]{:S(2)}, u32[]{:S(2)}) collective-permute-start(bf16[624,256]{1,0:T(8,128)(2,1)S(1)} %get-tuple-element.34), channel_id=1, source_target_pairs={{0,8},{4,12},{8,0},{12,4},{1,9},{5,13},{9,1},{13,5},{2,10},{6,14},... | collective-permute-start | bytes 958472 | tf_op jit(solution)/shard_map/ppermute | solution.py:33
  4.5 1.1 %collective-permute-start.4 = (bf16[624,256]{1,0:T(8,128)(2,1)S(1)}, bf16[624,256]{1,0:T(8,128)(2,1)S(1)}, u32[]{:S(2)}, u32[]{:S(2)}) collective-permute-start(bf16[624,256]{1,0:T(8,128)(2,1)S(1)} %get-tuple-element.37), channel_id=1, source_target_pairs={{0,12},{4,8},{8,4},{12,0},{1,13},{5,9},{9,5},{13,1},{2,14},{6,10},... | collective-permute-start | bytes 958472 | tf_op jit(solution)/shard_map/ppermute | solution.py:33
  5.6 1.1 %pack.3 = bf16[624,256]{1,0:T(8,128)(2,1)S(1)} custom-call(bf16[192,1536]{1,0:T(8,128)(2,1)} %bitcast.7, bf16[192,1536]{1,0:T(8,128)(2,1)} %bitcast.10, bf16[16,1536]{1,0:T(8,128)(2,1)} %bitcast.16, bf16[192,1536]{1,0:T(8,128)(2,1)} %bitcast.13, bf16[16,1536]{1,0:T(8,128)(2,1)} %bitcast.19, s32[1,192]{1,0:T(1,128)} %refs_5_.5), custom_call_target="tpu_custom_call" | custom-call | tf_op jit(solution)/shard_map/pack/pallas_call | solution.py:102
  6.7 0.3 collective-permute-start.3
  7.0 0.0 copy-start
  7.0 3.7 %copy-done = bf16[1536,3072]{1,0:T(8,128)(2,1)S(1)} copy-done((bf16[1536,3072]{1,0:T(8,128)(2,1)S(1)}, bf16[1536,3072]{1,0:T(8,128)(2,1)}, u32[]{:S(2)}) %copy-start) | copy-done | bytes 9437208
  10.7 0.0 copy-start.1
  10.7 0.0 copy-start.2
  10.7 0.6 load_weights.1.refs_7_.refs_4_.weights.refs_2_
  11.3 0.0 copy-done.1
  11.4 0.0 copy-done.2
  11.4 1.7 %prepare.1 = (bf16[624,256]{1,0:T(8,128)(2,1)S(1)}, bf16[608,256]{1,0:T(8,128)(2,1)S(1)}, bf16[608,256]{1,0:T(8,128)(2,1)S(1)}, bf16[416,256]{1,0:T(8,128)(2,1)S...) custom-call(bf16[192,1536]{1,0:T(8,128)(2,1)} %bitcast.8, bf16[192,1536]{1,0:T(8,128)(2,1)} %bitcast.11, ...), custom_call_target="tpu_custom_call" | custom-call | tf_op jit(solution)/shard_map/prepare/pallas_call | solution.py:141
  13.1 12.4 %collective-permute-done.refs_0_.refs_2_ = bf16[624,256]{1,0:T(8,128)(2,1)S(1)} collective-permute-done((bf16[624,256]{1,0:T(8,128)(2,1)S(1)}, bf16[624,256]{1,0:T(8,128)(2,1)S(1)}, u32[]{:S(2)}, u32[]{:S(2)}) %collective-permute-start) | collective-permute-done | bytes 319520 | tf_op jit(solution)/shard_map/ppermute | solution.py:33
  25.6 1.2 %collective-permute-start.1 = (bf16[608,256]{1,0:T(8,128)(2,1)S(1)}, bf16[608,256]{1,0:T(8,128)(2,1)S(1)}, u32[]{:S(2)}, u32[]{:S(2)}) collective-permute-start(bf16[608,256]{1,0:T(8,128)(2,1)S(1)} %hold.3), channel_id=1, source_target_pairs={{0,4},{4,0},{8,12},{12,8},{1,5},{5,1},{9,13},{13,9},{2,6},{6,2},{1... | collective-permute-start | bytes 933896 | tf_op jit(solution)/shard_map/ppermute | solution.py:33
  26.8 2.9 %collective-permute-start.2 = (bf16[416,256]{1,0:T(8,128)(2,1)S(1)}, bf16[416,256]{1,0:T(8,128)(2,1)S(1)}, u32[]{:S(2)}, u32[]{:S(2)}) collective-permute-start(bf16[416,256]{1,0:T(8,128)(2,1)S(1)} %hold.4), channel_id=1, source_target_pairs={{0,12},{4,8},{8,4},{12,0},{1,13},{5,9},{9,5},{13,1},{2,14},{6,10},... | collective-permute-start | bytes 638984 | tf_op jit(solution)/shard_map/ppermute | solution.py:33
  29.7 0.0 collective-permute-done.4.refs_3_.refs_1_
  29.7 5.8 %collective-permute-start.7 = (bf16[416,256]{1,0:T(8,128)(2,1)S(1)}, bf16[416,256]{1,0:T(8,128)(2,1)S(1)}, u32[]{:S(2)}, u32[]{:S(2)}) collective-permute-start(bf16[416,256]{1,0:T(8,128)(2,1)S(1)} %hold.5), channel_id=1, source_target_pairs={{0,8},{4,12},{8,0},{12,4},{1,9},{5,13},{9,1},{13,5},{2,10},{6,14},... | collective-permute-start | bytes 638984 | tf_op jit(solution)/shard_map/ppermute | solution.py:33
  35.6 0.0 collective-permute-done.3.refs_1_
  35.6 3.4 %attend.1 = (bf16[192,256]{1,0:T(8,128)(2,1)S(1)}, bf16[192,256]{1,0:T(8,128)(2,1)S(1)}, bf16[192,256]{1,0:T(8,128)(2,1)S(1)}, bf16[192,256]{1,0:T(8,128)(2,1)S(1)}) custom-call(f32[1,64]{1,0:T(1,128)S(1)} %get-tuple-element.31.bias, bf16[624,256]{1,0:T(8,128)(2,1)S(1)} %get-tuple-element.36.refs_0_, bf16[624,256]{1,0:T(8,128)(2,1)S(1)} %collective-permute-done.3.refs_1_, ...), custom_call_target="tpu_custom_call" | custom-call | tf_op jit(solution)/shard_map/attend/pallas_call | solution.py:337
  39.0 2.1 %collective-permute-start.5 = (bf16[192,256]{1,0:T(8,128)(2,1)S(1)}, bf16[192,256]{1,0:T(8,128)(2,1)S(1)}, u32[]{:S(2)}, u32[]{:S(2)}) collective-permute-start(bf16[192,256]{1,0:T(8,128)(2,1)S(1)} %get-tuple-element.39), channel_id=1, source_target_pairs={{0,1},{1,2},{2,3},{3,0},{4,5},{5,6},{6,7},{7,4},{8,9},{9,10},{10,1... | collective-permute-start | bytes 294920 | tf_op jit(solution)/shard_map/ppermute | solution.py:29
  41.0 0.1 collective-permute-start.6
  41.1 0.8 %weigh.1 = (f32[192,128]{1,0:T(8,128)S(1)}, f32[192,128]{1,0:T(8,128)S(1)}, f32[192,128]{1,0:T(8,128)S(1)}, f32[192,128]{1,0:T(8,128)}) custom-call(bf16[624,256]{1,0:T(8,128)(2,1)S(1)} %get-tuple-element.36.refs_0_, bf16[624,256]{1,0:T(8,128)(2,1)S(1)} %collective-permute-done.3.refs_1_, bf16[624,256]{1,0:T(8,128)(2,1)S(1)} %collective-permute-done.refs_0_.refs_2_, ...), custom_call_target="tpu_custom_call" | custom-call | tf_op jit(solution)/shard_map/weigh/pallas_call | solution.py:369
  42.0 0.7 %collective-permute-done.5.refs_1_ = bf16[192,256]{1,0:T(8,128)(2,1)S(1)} collective-permute-done((bf16[192,256]{1,0:T(8,128)(2,1)S(1)}, bf16[192,256]{1,0:T(8,128)(2,1)S(1)}, u32[]{:S(2)}, u32[]{:S(2)}) %collective-permute-start.5) | collective-permute-done | bytes 98336 | tf_op jit(solution)/shard_map/ppermute | solution.py:29
  42.7 1.0 %collective-permute-done.6.refs_4_ = bf16[192,256]{1,0:T(8,128)(2,1)S(1)} collective-permute-done((bf16[192,256]{1,0:T(8,128)(2,1)S(1)}, bf16[192,256]{1,0:T(8,128)(2,1)S(1)}, u32[]{:S(2)}, u32[]{:S(2)}) %collective-permute-start.6) | collective-permute-done | bytes 98336 | tf_op jit(solution)/shard_map/ppermute | solution.py:29
  43.7 0.1 blend.1
  43.8 0.1 collective-permute-start.11
  43.8 1.3 %collective-permute-start.12 = (bf16[96,256]{1,0:T(8,128)(2,1)S(1)}, bf16[96,256]{1,0:T(8,128)(2,1)S(1)}, u32[]{:S(2)}, u32[]{:S(2)}) collective-permute-start(bf16[96,256]{1,0:T(8,128)(2,1)S(1)} %get-tuple-element.55), channel_id=1, source_target_pairs={{0,8},{4,12},{8,0},{12,4},{1,9},{5,13},{9,1},{13,5},{2,10},{6,14},... | collective-permute-start | bytes 147464 | tf_op jit(solution)/shard_map/ppermute | solution.py:33
  45.2 0.0 collective-permute-done.2.refs_2_
  45.2 2.2 %collective-permute-start.13 = (bf16[96,256]{1,0:T(8,128)(2,1)S(1)}, bf16[96,256]{1,0:T(8,128)(2,1)S(1)}, u32[]{:S(2)}, u32[]{:S(2)}) collective-permute-start(bf16[96,256]{1,0:T(8,128)(2,1)S(1)} %get-tuple-element.56), channel_id=1, source_target_pairs={{0,12},{4,8},{8,4},{12,0},{1,13},{5,9},{9,5},{13,1},{2,14},{6,10},... | collective-permute-start | bytes 147464 | tf_op jit(solution)/shard_map/ppermute | solution.py:33
  47.4 0.0 collective-permute-done.1.refs_1_
  47.4 1.6 %attend_early.1 = (f32[384,256]{1,0:T(8,128)S(1)}, f32[384,256]{1,0:T(8,128)S(1)}, f32[384,256]{1,0:T(8,128)S(1)}) custom-call(f32[1,64]{1,0:T(1,128)S(1)} %get-tuple-element.31.bias, bf16[608,256]{1,0:T(8,128)(2,1)S(1)} %get-tuple-element.32.refs_0_, bf16[608,256]{1,0:T(8,128)(2,1)S(1)} %collective-permute-done.1.refs_1_, ...), custom_call_target="tpu_custom_call" | custom-call | tf_op jit(solution)/shard_map/attend_early/pallas_call | solution.py:260
  49.0 3.8 %collective-permute-done.7.refs_2_ = bf16[416,256]{1,0:T(8,128)(2,1)S(1)} collective-permute-done((bf16[416,256]{1,0:T(8,128)(2,1)S(1)}, bf16[416,256]{1,0:T(8,128)(2,1)S(1)}, u32[]{:S(2)}, u32[]{:S(2)}) %collective-permute-start.7) | collective-permute-done | bytes 213024 | tf_op jit(solution)/shard_map/ppermute | solution.py:33
  52.7 0.8 %attend_late.1 = (bf16[192,256]{1,0:T(8,128)(2,1)S(1)}, bf16[192,256]{1,0:T(8,128)(2,1)S(1)}) custom-call(f32[1,64]{1,0:T(1,128)S(1)} %get-tuple-element.31.bias, f32[384,256]{1,0:T(8,128)S(1)} %get-tuple-element.45.products, f32[384,256]{1,0:T(8,128)S(1)} %get-tuple-element.46.totals, f32[384,256]{1,0:T(8,128)S(1)} %get-tuple-element.47.peaks, ...), custom_call_target="tpu_custom_call" | custom-call | tf_op jit(solution)/shard_map/attend_late/pallas_call | solution.py:272
  53.6 1.2 %collective-permute-start.8 = (bf16[192,256]{1,0:T(8,128)(2,1)S(1)}, bf16[192,256]{1,0:T(8,128)(2,1)S(1)}, u32[]{:S(2)}, u32[]{:S(2)}) collective-permute-start(bf16[192,256]{1,0:T(8,128)(2,1)S(1)} %get-tuple-element.50), channel_id=1, source_target_pairs={{0,4},{4,0},{8,12},{12,8},{1,5},{5,1},{9,13},{13,9},{2,6},{6,2},{1... | collective-permute-start | bytes 294920 | tf_op jit(solution)/shard_map/ppermute | solution.py:33
  54.8 0.0 collective-permute-done.11.refs_1_
  54.8 0.0 collective-permute-done.12.refs_2_
  54.8 0.0 collective-permute-done.13.refs_3_
  54.9 1.0 %collective-permute-start.14 = (bf16[96,1024]{1,0:T(8,128)(2,1)S(1)}, bf16[96,1024]{1,0:T(8,128)(2,1)S(1)}, u32[]{:S(2)}, u32[]{:S(2)}) collective-permute-start(bf16[96,1024]{1,0:T(8,128)(2,1)S(1)} %collect.1.left), channel_id=1, source_target_pairs={{0,3},{1,0},{2,1},{3,2},{4,7},{5,4},{6,5},{7,6},{8,11},{9,8},{10,9... | collective-permute-start | bytes 589832 | tf_op jit(solution)/shard_map/ppermute | solution.py:29
  55.8 1.3 %collective-permute-done.8.refs_1_ = bf16[192,256]{1,0:T(8,128)(2,1)S(1)} collective-permute-done((bf16[192,256]{1,0:T(8,128)(2,1)S(1)}, bf16[192,256]{1,0:T(8,128)(2,1)S(1)}, u32[]{:S(2)}, u32[]{:S(2)}) %collective-permute-start.8) | collective-permute-done | bytes 98336 | tf_op jit(solution)/shard_map/ppermute | solution.py:33
  57.1 3.3 %collective-permute-start.10 = (bf16[96,512]{1,0:T(8,128)(2,1)S(1)}, bf16[96,512]{1,0:T(8,128)(2,1)S(1)}, u32[]{:S(2)}, u32[]{:S(2)}) collective-permute-start(bf16[96,512]{1,0:T(8,128)(2,1)S(1)} %get-tuple-element.51.left), channel_id=1, source_target_pairs={{0,3},{1,0},{2,1},{3,2},{4,7},{5,4},{6,5},{7,6},{8,11},{9,8},{10,9... | collective-permute-start | bytes 294920 | tf_op jit(solution)/shard_map/ppermute | solution.py:29
  60.4 1.4 %collective-permute-start.9 = (bf16[96,512]{1,0:T(8,128)(2,1)S(1)}, bf16[96,512]{1,0:T(8,128)(2,1)S(1)}, u32[]{:S(2)}, u32[]{:S(2)}) collective-permute-start(bf16[96,512]{1,0:T(8,128)(2,1)S(1)} %get-tuple-element.52.right), channel_id=1, source_target_pairs={{0,1},{1,2},{2,3},{3,0},{4,5},{5,6},{6,7},{7,4},{8,9},{9,10},{10,1... | collective-permute-start | bytes 294920 | tf_op jit(solution)/shard_map/ppermute | solution.py:29
  61.8 0.0 collective-permute-done.14.right
  61.8 1.4 %project_begin.1.refs_3_ = f32[192,3072]{1,0:T(8,128)S(1)} custom-call(bf16[96,1024]{1,0:T(8,128)(2,1)S(1)} %collect.1.left, bf16[96,1024]{1,0:T(8,128)(2,1)S(1)} %collective-permute-done.14.right, bf16[1536,3072]{1,0:T(8,128)(2,1)S(1)} %load_weights.1.refs_7_.refs_4_.weights.refs_2_), custom_call_target="tpu_custom_call" | custom-call | tf_op jit(solution)/shard_map/project_begin/pallas_call | solution.py:485
  63.2 1.8 %collective-permute-done.10.from_next = bf16[96,512]{1,0:T(8,128)(2,1)S(1)} collective-permute-done((bf16[96,512]{1,0:T(8,128)(2,1)S(1)}, bf16[96,512]{1,0:T(8,128)(2,1)S(1)}, u32[]{:S(2)}, u32[]{:S(2)}) %collective-permute-start.10) | collective-permute-done | bytes 98336 | tf_op jit(solution)/shard_map/ppermute | solution.py:29
  65.0 0.0 collective-permute-done.9.from_prev
  65.0 1.5 %project_end.1 = bf16[192,3072]{1,0:T(8,128)(2,1)} custom-call(bf16[96,512]{1,0:T(8,128)(2,1)S(1)} %get-tuple-element.51.left, bf16[96,512]{1,0:T(8,128)(2,1)S(1)} %get-tuple-element.52.right, bf16[96,512]{1,0:T(8,128)(2,1)S(1)} %collective-permute-done.9.from_prev, bf16[96,512]{1,0:T(8,128)(2,1)S(1)} %collective-permute-done.10.from_next, ...), custom_call_target="tpu_custom_call" | custom-call | tf_op jit(solution)/shard_map/project_end/pallas_call | solution.py:532
  (5 shorter events, 0.1 us)
Async XLA Ops:
  1.3 24.2 %collective-permute-start = (bf16[624,256]{1,0:T(8,128)(2,1)S(1)}, bf16[624,256]{1,0:T(8,128)(2,1)S(1)}, u32[]{:S(2)}, u32[]{:S(2)}) collective-permute-start(bf16[624,256]{1,0:T(8,128)(2,1)S(1)} %get-tuple-element.34), channel_id=1, source_target_pairs={{0,8},{4,12},{8,0},{12,4},{1,9},{5,13},{9,1},{13,5},{2,10},{6,14},... | collective-permute-start | bytes 958472 | tf_op jit(solution)/shard_map/ppermute | solution.py:33
  4.5 25.2 %collective-permute-start.4 = (bf16[624,256]{1,0:T(8,128)(2,1)S(1)}, bf16[624,256]{1,0:T(8,128)(2,1)S(1)}, u32[]{:S(2)}, u32[]{:S(2)}) collective-permute-start(bf16[624,256]{1,0:T(8,128)(2,1)S(1)} %get-tuple-element.37), channel_id=1, source_target_pairs={{0,12},{4,8},{8,4},{12,0},{1,13},{5,9},{9,5},{13,1},{2,14},{6,10},... | collective-permute-start | bytes 958472 | tf_op jit(solution)/shard_map/ppermute | solution.py:33
  6.7 28.8 %collective-permute-start.3 = (bf16[624,256]{1,0:T(8,128)(2,1)S(1)}, bf16[624,256]{1,0:T(8,128)(2,1)S(1)}, u32[]{:S(2)}, u32[]{:S(2)}) collective-permute-start(bf16[624,256]{1,0:T(8,128)(2,1)S(1)} %pack.3), channel_id=1, source_target_pairs={{0,4},{4,0},{8,12},{12,8},{1,5},{5,1},{9,13},{13,9},{2,6},{6,2},{1... | collective-permute-start | bytes 958472 | tf_op jit(solution)/shard_map/ppermute | solution.py:33
  7.0 3.7 %copy-start = (bf16[1536,3072]{1,0:T(8,128)(2,1)S(1)}, bf16[1536,3072]{1,0:T(8,128)(2,1)}, u32[]{:S(2)}) copy-start(bf16[1536,3072]{1,0:T(8,128)(2,1)} %w_out.1) | copy-start | bytes 28311556
  10.7 0.7 %copy-start.1 = (s32[1,192]{1,0:T(1,128)S(1)}, s32[1,192]{1,0:T(1,128)}, u32[]{:S(2)}) copy-start(s32[1,192]{1,0:T(1,128)} %refs_5_.5) | copy-start | bytes 2308
  10.7 0.7 %copy-start.2 = (s32[1,64]{1,0:T(1,128)S(1)}, s32[1,64]{1,0:T(1,128)}, u32[]{:S(2)}) copy-start(s32[1,64]{1,0:T(1,128)} %refs_6_.1) | copy-start | bytes 772
  25.6 21.8 %collective-permute-start.1 = (bf16[608,256]{1,0:T(8,128)(2,1)S(1)}, bf16[608,256]{1,0:T(8,128)(2,1)S(1)}, u32[]{:S(2)}, u32[]{:S(2)}) collective-permute-start(bf16[608,256]{1,0:T(8,128)(2,1)S(1)} %hold.3), channel_id=1, source_target_pairs={{0,4},{4,0},{8,12},{12,8},{1,5},{5,1},{9,13},{13,9},{2,6},{6,2},{1... | collective-permute-start | bytes 933896 | tf_op jit(solution)/shard_map/ppermute | solution.py:33
  26.8 18.4 %collective-permute-start.2 = (bf16[416,256]{1,0:T(8,128)(2,1)S(1)}, bf16[416,256]{1,0:T(8,128)(2,1)S(1)}, u32[]{:S(2)}, u32[]{:S(2)}) collective-permute-start(bf16[416,256]{1,0:T(8,128)(2,1)S(1)} %hold.4), channel_id=1, source_target_pairs={{0,12},{4,8},{8,4},{12,0},{1,13},{5,9},{9,5},{13,1},{2,14},{6,10},... | collective-permute-start | bytes 638984 | tf_op jit(solution)/shard_map/ppermute | solution.py:33
  29.7 23.0 %collective-permute-start.7 = (bf16[416,256]{1,0:T(8,128)(2,1)S(1)}, bf16[416,256]{1,0:T(8,128)(2,1)S(1)}, u32[]{:S(2)}, u32[]{:S(2)}) collective-permute-start(bf16[416,256]{1,0:T(8,128)(2,1)S(1)} %hold.5), channel_id=1, source_target_pairs={{0,8},{4,12},{8,0},{12,4},{1,9},{5,13},{9,1},{13,5},{2,10},{6,14},... | collective-permute-start | bytes 638984 | tf_op jit(solution)/shard_map/ppermute | solution.py:33
  39.0 3.7 %collective-permute-start.5 = (bf16[192,256]{1,0:T(8,128)(2,1)S(1)}, bf16[192,256]{1,0:T(8,128)(2,1)S(1)}, u32[]{:S(2)}, u32[]{:S(2)}) collective-permute-start(bf16[192,256]{1,0:T(8,128)(2,1)S(1)} %get-tuple-element.39), channel_id=1, source_target_pairs={{0,1},{1,2},{2,3},{3,0},{4,5},{5,6},{6,7},{7,4},{8,9},{9,10},{10,1... | collective-permute-start | bytes 294920 | tf_op jit(solution)/shard_map/ppermute | solution.py:29
  41.0 2.6 %collective-permute-start.6 = (bf16[192,256]{1,0:T(8,128)(2,1)S(1)}, bf16[192,256]{1,0:T(8,128)(2,1)S(1)}, u32[]{:S(2)}, u32[]{:S(2)}) collective-permute-start(bf16[192,256]{1,0:T(8,128)(2,1)S(1)} %get-tuple-element.42), channel_id=1, source_target_pairs={{0,1},{1,2},{2,3},{3,0},{4,5},{5,6},{6,7},{7,4},{8,9},{9,10},{10,1... | collective-permute-start | bytes 294920 | tf_op jit(solution)/shard_map/ppermute | solution.py:29
  43.8 11.0 %collective-permute-start.11 = (bf16[96,256]{1,0:T(8,128)(2,1)S(1)}, bf16[96,256]{1,0:T(8,128)(2,1)S(1)}, u32[]{:S(2)}, u32[]{:S(2)}) collective-permute-start(bf16[96,256]{1,0:T(8,128)(2,1)S(1)} %get-tuple-element.54), channel_id=1, source_target_pairs={{0,4},{4,0},{8,12},{12,8},{1,5},{5,1},{9,13},{13,9},{2,6},{6,2},{1... | collective-permute-start | bytes 147464 | tf_op jit(solution)/shard_map/ppermute | solution.py:33
  43.8 11.0 %collective-permute-start.12 = (bf16[96,256]{1,0:T(8,128)(2,1)S(1)}, bf16[96,256]{1,0:T(8,128)(2,1)S(1)}, u32[]{:S(2)}, u32[]{:S(2)}) collective-permute-start(bf16[96,256]{1,0:T(8,128)(2,1)S(1)} %get-tuple-element.55), channel_id=1, source_target_pairs={{0,8},{4,12},{8,0},{12,4},{1,9},{5,13},{9,1},{13,5},{2,10},{6,14},... | collective-permute-start | bytes 147464 | tf_op jit(solution)/shard_map/ppermute | solution.py:33
  45.2 9.6 %collective-permute-start.13 = (bf16[96,256]{1,0:T(8,128)(2,1)S(1)}, bf16[96,256]{1,0:T(8,128)(2,1)S(1)}, u32[]{:S(2)}, u32[]{:S(2)}) collective-permute-start(bf16[96,256]{1,0:T(8,128)(2,1)S(1)} %get-tuple-element.56), channel_id=1, source_target_pairs={{0,12},{4,8},{8,4},{12,0},{1,13},{5,9},{9,5},{13,1},{2,14},{6,10},... | collective-permute-start | bytes 147464 | tf_op jit(solution)/shard_map/ppermute | solution.py:33
  53.6 3.5 %collective-permute-start.8 = (bf16[192,256]{1,0:T(8,128)(2,1)S(1)}, bf16[192,256]{1,0:T(8,128)(2,1)S(1)}, u32[]{:S(2)}, u32[]{:S(2)}) collective-permute-start(bf16[192,256]{1,0:T(8,128)(2,1)S(1)} %get-tuple-element.50), channel_id=1, source_target_pairs={{0,4},{4,0},{8,12},{12,8},{1,5},{5,1},{9,13},{13,9},{2,6},{6,2},{1... | collective-permute-start | bytes 294920 | tf_op jit(solution)/shard_map/ppermute | solution.py:33
  54.9 6.9 %collective-permute-start.14 = (bf16[96,1024]{1,0:T(8,128)(2,1)S(1)}, bf16[96,1024]{1,0:T(8,128)(2,1)S(1)}, u32[]{:S(2)}, u32[]{:S(2)}) collective-permute-start(bf16[96,1024]{1,0:T(8,128)(2,1)S(1)} %collect.1.left), channel_id=1, source_target_pairs={{0,3},{1,0},{2,1},{3,2},{4,7},{5,4},{6,5},{7,6},{8,11},{9,8},{10,9... | collective-permute-start | bytes 589832 | tf_op jit(solution)/shard_map/ppermute | solution.py:29
  57.1 7.9 %collective-permute-start.10 = (bf16[96,512]{1,0:T(8,128)(2,1)S(1)}, bf16[96,512]{1,0:T(8,128)(2,1)S(1)}, u32[]{:S(2)}, u32[]{:S(2)}) collective-permute-start(bf16[96,512]{1,0:T(8,128)(2,1)S(1)} %get-tuple-element.51.left), channel_id=1, source_target_pairs={{0,3},{1,0},{2,1},{3,2},{4,7},{5,4},{6,5},{7,6},{8,11},{9,8},{10,9... | collective-permute-start | bytes 294920 | tf_op jit(solution)/shard_map/ppermute | solution.py:29
  60.4 4.6 %collective-permute-start.9 = (bf16[96,512]{1,0:T(8,128)(2,1)S(1)}, bf16[96,512]{1,0:T(8,128)(2,1)S(1)}, u32[]{:S(2)}, u32[]{:S(2)}) collective-permute-start(bf16[96,512]{1,0:T(8,128)(2,1)S(1)} %get-tuple-element.52.right), channel_id=1, source_target_pairs={{0,1},{1,2},{2,3},{3,0},{4,5},{5,6},{6,7},{7,4},{8,9},{9,10},{10,1... | collective-permute-start | bytes 294920 | tf_op jit(solution)/shard_map/ppermute | solution.py:29

commit v6 on v5

--- a/solution.py
+++ b/solution.py
@@ -27,6 +27,12 @@
 def shifted(block, axis, distance):
     count = lax.axis_size(axis)
     return lax.ppermute(block, axis, [(i, (i + distance) % count) for i in range(count)])
+
+
+def paired(block, odd):
+    count = lax.axis_size("win")
+    step = [-1, 1] if odd else [1, -1]
+    return lax.ppermute(block, "win", [(i, (i + step[i % 2]) % count) for i in range(count)])
 
 
 def swapped(block, distance):
@@ -224,28 +230,26 @@
             peaks[rows, head] = peak
 
 
-def late_kernel(group, image_rows, text_rows, bias, products, totals, peaks, *refs):
+def late_kernel(group, image_rows, text_rows, index, bias, products, totals, peaks, *refs):
     halfway = group // 2
-    near, block = refs[:halfway], refs[halfway]
-    outs, (keys, values, mask) = refs[-3 - halfway : -3], refs[-3:]
+    near, block, out, keys, values, mask = refs
     sources = [partner(halfway, group)]
     fill(keys, values, mask, bias, [block], sources, [0], group, image_rows, text_rows)
     for at in range(0, keys.shape[1], HEAD_DIM):
         head = slice(at, at + HEAD_DIM)
-        for index, out in enumerate(outs):
-            rows = slice(index * image_rows, (index + 1) * image_rows)
-            before = peaks[rows, head]
-            product, total, peak = sum_up(
-                near[index][:image_rows, head],
-                keys[:, head],
-                values[:, head],
-                mask[...],
-                before,
-            )
-            scale = jnp.exp2((before - peak) * EXP2_SCALE)
-            total += totals[rows, head] * scale
-            product += products[rows, head] * scale
-            out[:, head] = (product / total).astype(jnp.bfloat16)
+        rows = slice(index * image_rows, (index + 1) * image_rows)
+        before = peaks[rows, head]
+        product, total, peak = sum_up(
+            near[:image_rows, head],
+            keys[:, head],
+            values[:, head],
+            mask[...],
+            before,
+        )
+        scale = jnp.exp2((before - peak) * EXP2_SCALE)
+        total += totals[rows, head] * scale
+        product += products[rows, head] * scale
+        out[:, head] = (product / total).astype(jnp.bfloat16)
 
 
 def attend_half(blocks, bias, image_rows, text_rows, after):
@@ -269,21 +273,25 @@
     )(bias, *others, *after)
     count = image_rows + texts
     keys, mask = pltpu.VMEM((count, width), jnp.bfloat16), pltpu.VMEM((1, count), jnp.float32)
-    return pl.pallas_call(
-        functools.partial(late_kernel, group, image_rows, text_rows),
-        out_shape=[jax.ShapeDtypeStruct((image_rows, width), jnp.bfloat16)] * halfway,
-        in_specs=[VMEM] * (5 + halfway),
-        out_specs=[VMEM] * halfway,
-        scratch_shapes=[keys, keys, mask],
-        compiler_params=SMALL,
-        cost_estimate=NO_COST,
-        name="attend_late",
-    )(bias, *sums, *near, last)
+    results = [None] * halfway
+    for index in reversed(range(halfway)):
+        results[index] = pl.pallas_call(
+            functools.partial(late_kernel, group, image_rows, text_rows, index),
+            out_shape=jax.ShapeDtypeStruct((image_rows, width), jnp.bfloat16),
+            in_specs=[VMEM] * 6,
+            out_specs=VMEM,
+            scratch_shapes=[keys, keys, mask],
+            compiler_params=SMALL,
+            cost_estimate=NO_COST,
+            name="attend_late",
+        )(bias, *sums, near[index], last)
+    return results
 
 
 def merge_kernel(group, *refs):
-    blocks, (left, right) = refs[: group // 2], refs[-2:]
+    blocks, (left, right, first, second) = refs[: group // 2], refs[-4:]
     width = blocks[0].shape[1]
+    even = lax.rem(lax.axis_index("win"), 2) == 0
     for distance, block in enumerate(blocks):
         start = lax.rem(partner(distance, group), group // 2) * width
         columns = pl.ds(pl.multiple_of(start, HEAD_DIM), width)
@@ -292,19 +300,27 @@
                 at = row * WCOLS + side * STRIDE
                 out[pl.ds(row * STRIDE, STRIDE), columns] = block[at : at + STRIDE]
 
-
-def merge(blocks, group, after):
+    @pl.when(even)
+    def _():
+        first[...], second[...] = right[...], left[...]
+
+    @pl.when(jnp.logical_not(even))
+    def _():
+        first[...], second[...] = left[...], right[...]
+
+
+def merge(blocks, group):
     rows, width = blocks[0].shape
     strip = jax.ShapeDtypeStruct((rows // 2, len(blocks) * width), jnp.bfloat16)
     return pl.pallas_call(
         functools.partial(merge_kernel, group),
-        out_shape=[strip, strip],
-        in_specs=[VMEM] * len(blocks) + [ANY] * len(after),
-        out_specs=[VMEM] * 2,
+        out_shape=[strip] * 4,
+        in_specs=[VMEM] * len(blocks),
+        out_specs=[VMEM] * 4,
         compiler_params=SMALL,
         cost_estimate=NO_COST,
         name="merge",
-    )(*blocks, *after)
+    )(*blocks)
 
 
 def attend_kernel(group, image_rows, text_rows, bias, *refs):
@@ -494,17 +510,19 @@
     )(left, right, weights)
 
 
-def end_kernel(left, right, from_prev, from_next, *refs):
+def end_kernel(left, right, first_in, second_in, *refs):
     weight_left, weight_right, weights, total, out, features, result, sems = refs
     rows = left.shape[0]
+    even = lax.rem(lax.axis_index("win"), 2) == 0
     for side, (own, other, weight_ref) in enumerate(
-        ((left, from_prev, weight_left), (right, from_next, weight_right))
+        ((left, (second_in, first_in), weight_left), (right, (first_in, second_in), weight_right))
     ):
         weight = weight_ref[:rows]
         for at in range(0, own.shape[1], HEAD_DIM):
             head = pl.ds(at, HEAD_DIM)
             mixed = weight * own[:, head].astype(jnp.float32)
-            mixed += (BLEND_TOTAL - weight) * other[:, head].astype(jnp.float32)
+            theirs = [ref[:, head].astype(jnp.float32) for ref in other]
+            mixed += (BLEND_TOTAL - weight) * jnp.where(even, *theirs)
             mixed = (mixed * (1.0 / BLEND_TOTAL)).astype(jnp.bfloat16)
             for row in range(rows // STRIDE):
                 start = row * WCOLS + side * STRIDE
@@ -662,11 +680,11 @@
     begun = returned(mixed)
 
     results = returned(results_of(second, [mixed[0], weights]))
-    left, right = merge(results, group, [])
-    from_prev, from_next = shifted(right, "win", 1), shifted(left, "win", -1)
+    left, right, to_first, to_second = merge(results, group)
+    second_in, first_in = paired(to_second, True), paired(to_first, False)
     begins = collect(begun)
     total = project_begin(begins, shifted(begins, "win", -1), weights)
-    strips = [left, right, from_prev, from_next]
+    strips = [left, right, first_in, second_in]
     return project_end(strips, blend_weights[:2], weights, total)[None]
 
 

time: 67.2 us -> 66.7 us (level)
  waiting for transfers between devices: 21 us -> 20.1 us
    ppermute x0 -> x2, starting transfers between devices: none -> 4.67 us  [paired(): lax.ppermute(block, 'win', [(i, (i + step[i % 2]) % count) for i in range...]
    ppermute x5 -> x3, starting transfers between devices: 7.73 us -> 3.09 us  [shifted(): lax.ppermute(block, axis, [(i, (i + distance) % count) for i in range(cou...]
    ppermute x5 -> x3, waiting for transfers between devices: 3.53 us -> 1.71 us  [shifted(): lax.ppermute(block, axis, [(i, (i + distance) % count) for i in range(cou...]
    ppermute x0 -> x2, waiting for transfers between devices: none -> 1.68 us  [paired(): lax.ppermute(block, 'win', [(i, (i + step[i % 2]) % count) for i in range...]
    ppermute x10, waiting for transfers between devices: 17.4 us -> 16.7 us  [swapped(): lax.ppermute(block, 'seq', [(i, i ^ distance) for i in range(lax.axis_siz...]
    pallas_call x1 -> x2, Pallas kernels: 0.82 us -> 1.37 us  [attend_half(): pl.pallas_call(functools.partial(late_kernel, group, image_rows, text_row...]
  transfers between devices with their start and end apart: 15 -> 15, of which waited for: 6 -> 6; matrix products, arithmetic and copies ran while one was open for 0% -> 0% of each run, Pallas kernels for 18% -> 19%
where the time goes in v6:
time: 66.7 us; the launch traced here: 66.4 us
  starting transfers between devices  27.1 us (41%)
  waiting for transfers between devices  20.1 us (30%)
  Pallas kernels  15.2 us (23%)
  local copies, waits for them, and re-layouts  3.72 us (6%)
    ppermute x10, starting transfers between devices, swapped(): lax.ppermute(block, 'seq', [(i, i ^ distance) for i in range(lax.axis_siz...  19.4 us
    ppermute x10, waiting for transfers between devices, swapped(): lax.ppermute(block, 'seq', [(i, i ^ distance) for i in range(lax.axis_siz...  16.7 us
    ppermute x2, starting transfers between devices, paired(): lax.ppermute(block, 'win', [(i, (i + step[i % 2]) % count) for i in range...  4.67 us
    unnamed x6, local copies, waits for them, and re-layouts  3.72 us
    pallas_call x1, Pallas kernels, attend(): pl.pallas_call(functools.partial(attend_kernel, group, image_rows, text_r...  3.42 us
    ppermute x3, starting transfers between devices, shifted(): lax.ppermute(block, axis, [(i, (i + distance) % count) for i in range(cou...  3.09 us
    pallas_call x2, Pallas kernels, pack(): pl.pallas_call(functools.partial(pack_kernel, heads, group, distances, le...  2.43 us
    pallas_call x1, Pallas kernels, prepare(): pl.pallas_call(functools.partial(prepare_kernel, heads, group, len(source...  1.74 us
  transfers between devices with their start and end apart: 15, of which 6 were waited for; matrix products, arithmetic and copies ran while one was open for 0% of the time, Pallas kernels for 19%

profile of v6, /device:TPU:1, one launch (start us, length us, event | category | flops | bytes accessed | tf_op | source)
XLA Modules:
  0.0 66.4 jit_solution(18371520691074507241)
XLA Ops:
  0.0 1.3 %pack.2 = (bf16[624,256]{1,0:T(8,128)(2,1)S(1)}, bf16[624,256]{1,0:T(8,128)(2,1)S(1)}) custom-call(bf16[192,1536]{1,0:T(8,128)(2,1)} %bitcast.6, bf16[192,1536]{1,0:T(8,128)(2,1)} %bitcast.9, bf16[16,1536]{1,0:T(8,128)(2,1)} %bitcast.15, bf16[192,1536]{1,0:T(8,128)(2,1)} %bitcast.12, bf16[16,1536]{1,0:T(8,128)(2,1)} %bitcast.18, s32[1,192]{1,0:T(1,128)} %refs_5_.5), custom_call_target="tpu_custom_call" | custom-call | tf_op jit(solution)/shard_map/pack/pallas_call | solution.py:108
  1.3 3.2 %collective-permute-start = (bf16[624,256]{1,0:T(8,128)(2,1)S(1)}, bf16[624,256]{1,0:T(8,128)(2,1)S(1)}, u32[]{:S(2)}, u32[]{:S(2)}) collective-permute-start(bf16[624,256]{1,0:T(8,128)(2,1)S(1)} %get-tuple-element.34), channel_id=1, source_target_pairs={{0,8},{4,12},{8,0},{12,4},{1,9},{5,13},{9,1},{13,5},{2,10},{6,14},... | collective-permute-start | bytes 958472 | tf_op jit(solution)/shard_map/ppermute | solution.py:39
  4.5 1.1 %collective-permute-start.4 = (bf16[624,256]{1,0:T(8,128)(2,1)S(1)}, bf16[624,256]{1,0:T(8,128)(2,1)S(1)}, u32[]{:S(2)}, u32[]{:S(2)}) collective-permute-start(bf16[624,256]{1,0:T(8,128)(2,1)S(1)} %get-tuple-element.37), channel_id=1, source_target_pairs={{0,12},{4,8},{8,4},{12,0},{1,13},{5,9},{9,5},{13,1},{2,14},{6,10},... | collective-permute-start | bytes 958472 | tf_op jit(solution)/shard_map/ppermute | solution.py:39
  5.6 1.1 %pack.3 = bf16[624,256]{1,0:T(8,128)(2,1)S(1)} custom-call(bf16[192,1536]{1,0:T(8,128)(2,1)} %bitcast.7, bf16[192,1536]{1,0:T(8,128)(2,1)} %bitcast.10, bf16[16,1536]{1,0:T(8,128)(2,1)} %bitcast.16, bf16[192,1536]{1,0:T(8,128)(2,1)} %bitcast.13, bf16[16,1536]{1,0:T(8,128)(2,1)} %bitcast.19, s32[1,192]{1,0:T(1,128)} %refs_5_.5), custom_call_target="tpu_custom_call" | custom-call | tf_op jit(solution)/shard_map/pack/pallas_call | solution.py:108
  6.7 0.3 collective-permute-start.3
  7.0 0.0 copy-start
  7.0 3.7 %copy-done = bf16[1536,3072]{1,0:T(8,128)(2,1)S(1)} copy-done((bf16[1536,3072]{1,0:T(8,128)(2,1)S(1)}, bf16[1536,3072]{1,0:T(8,128)(2,1)}, u32[]{:S(2)}) %copy-start) | copy-done | bytes 9437208
  10.7 0.0 copy-start.1
  10.7 0.0 copy-start.2
  10.7 0.6 load_weights.1.refs_7_.refs_4_.weights.refs_2_
  11.3 0.0 copy-done.1
  11.4 0.0 copy-done.2
  11.4 1.7 %prepare.1 = (bf16[624,256]{1,0:T(8,128)(2,1)S(1)}, bf16[608,256]{1,0:T(8,128)(2,1)S(1)}, bf16[608,256]{1,0:T(8,128)(2,1)S(1)}, bf16[416,256]{1,0:T(8,128)(2,1)S...) custom-call(bf16[192,1536]{1,0:T(8,128)(2,1)} %bitcast.8, bf16[192,1536]{1,0:T(8,128)(2,1)} %bitcast.11, ...), custom_call_target="tpu_custom_call" | custom-call | tf_op jit(solution)/shard_map/prepare/pallas_call | solution.py:147
  13.1 12.4 %collective-permute-done.refs_0_.refs_2_ = bf16[624,256]{1,0:T(8,128)(2,1)S(1)} collective-permute-done((bf16[624,256]{1,0:T(8,128)(2,1)S(1)}, bf16[624,256]{1,0:T(8,128)(2,1)S(1)}, u32[]{:S(2)}, u32[]{:S(2)}) %collective-permute-start) | collective-permute-done | bytes 319520 | tf_op jit(solution)/shard_map/ppermute | solution.py:39
  25.6 1.2 %collective-permute-start.1 = (bf16[608,256]{1,0:T(8,128)(2,1)S(1)}, bf16[608,256]{1,0:T(8,128)(2,1)S(1)}, u32[]{:S(2)}, u32[]{:S(2)}) collective-permute-start(bf16[608,256]{1,0:T(8,128)(2,1)S(1)} %hold.3), channel_id=1, source_target_pairs={{0,4},{4,0},{8,12},{12,8},{1,5},{5,1},{9,13},{13,9},{2,6},{6,2},{1... | collective-permute-start | bytes 933896 | tf_op jit(solution)/shard_map/ppermute | solution.py:39
  26.8 2.9 %collective-permute-start.2 = (bf16[416,256]{1,0:T(8,128)(2,1)S(1)}, bf16[416,256]{1,0:T(8,128)(2,1)S(1)}, u32[]{:S(2)}, u32[]{:S(2)}) collective-permute-start(bf16[416,256]{1,0:T(8,128)(2,1)S(1)} %hold.4), channel_id=1, source_target_pairs={{0,12},{4,8},{8,4},{12,0},{1,13},{5,9},{9,5},{13,1},{2,14},{6,10},... | collective-permute-start | bytes 638984 | tf_op jit(solution)/shard_map/ppermute | solution.py:39
  29.7 0.0 collective-permute-done.4.refs_3_.refs_1_
  29.7 5.8 %collective-permute-start.7 = (bf16[416,256]{1,0:T(8,128)(2,1)S(1)}, bf16[416,256]{1,0:T(8,128)(2,1)S(1)}, u32[]{:S(2)}, u32[]{:S(2)}) collective-permute-start(bf16[416,256]{1,0:T(8,128)(2,1)S(1)} %hold.5), channel_id=1, source_target_pairs={{0,8},{4,12},{8,0},{12,4},{1,9},{5,13},{9,1},{13,5},{2,10},{6,14},... | collective-permute-start | bytes 638984 | tf_op jit(solution)/shard_map/ppermute | solution.py:39
  35.6 0.0 collective-permute-done.3.refs_1_
  35.6 3.4 %attend.1 = (bf16[192,256]{1,0:T(8,128)(2,1)S(1)}, bf16[192,256]{1,0:T(8,128)(2,1)S(1)}, bf16[192,256]{1,0:T(8,128)(2,1)S(1)}, bf16[192,256]{1,0:T(8,128)(2,1)S(1)}) custom-call(f32[1,64]{1,0:T(1,128)S(1)} %get-tuple-element.31.bias, bf16[624,256]{1,0:T(8,128)(2,1)S(1)} %get-tuple-element.36.refs_0_, bf16[624,256]{1,0:T(8,128)(2,1)S(1)} %collective-permute-done.3.refs_1_, ...), custom_call_target="tpu_custom_call" | custom-call | tf_op jit(solution)/shard_map/attend/pallas_call | solution.py:353
  39.0 2.1 %collective-permute-start.5 = (bf16[192,256]{1,0:T(8,128)(2,1)S(1)}, bf16[192,256]{1,0:T(8,128)(2,1)S(1)}, u32[]{:S(2)}, u32[]{:S(2)}) collective-permute-start(bf16[192,256]{1,0:T(8,128)(2,1)S(1)} %get-tuple-element.39), channel_id=1, source_target_pairs={{0,1},{1,2},{2,3},{3,0},{4,5},{5,6},{6,7},{7,4},{8,9},{9,10},{10,1... | collective-permute-start | bytes 294920 | tf_op jit(solution)/shard_map/ppermute | solution.py:29
  41.0 0.1 collective-permute-start.6
  41.1 0.8 %weigh.1 = (f32[192,128]{1,0:T(8,128)S(1)}, f32[192,128]{1,0:T(8,128)S(1)}, f32[192,128]{1,0:T(8,128)S(1)}, f32[192,128]{1,0:T(8,128)}) custom-call(bf16[624,256]{1,0:T(8,128)(2,1)S(1)} %get-tuple-element.36.refs_0_, bf16[624,256]{1,0:T(8,128)(2,1)S(1)} %collective-permute-done.3.refs_1_, bf16[624,256]{1,0:T(8,128)(2,1)S(1)} %collective-permute-done.refs_0_.refs_2_, ...), custom_call_target="tpu_custom_call" | custom-call | tf_op jit(solution)/shard_map/weigh/pallas_call | solution.py:385
  42.0 0.7 %collective-permute-done.5.refs_1_ = bf16[192,256]{1,0:T(8,128)(2,1)S(1)} collective-permute-done((bf16[192,256]{1,0:T(8,128)(2,1)S(1)}, bf16[192,256]{1,0:T(8,128)(2,1)S(1)}, u32[]{:S(2)}, u32[]{:S(2)}) %collective-permute-start.5) | collective-permute-done | bytes 98336 | tf_op jit(solution)/shard_map/ppermute | solution.py:29
  42.7 1.0 %collective-permute-done.6.refs_4_ = bf16[192,256]{1,0:T(8,128)(2,1)S(1)} collective-permute-done((bf16[192,256]{1,0:T(8,128)(2,1)S(1)}, bf16[192,256]{1,0:T(8,128)(2,1)S(1)}, u32[]{:S(2)}, u32[]{:S(2)}) %collective-permute-start.6) | collective-permute-done | bytes 98336 | tf_op jit(solution)/shard_map/ppermute | solution.py:29
  43.7 0.1 blend.1
  43.8 0.1 collective-permute-start.11
  43.8 1.3 %collective-permute-start.12 = (bf16[96,256]{1,0:T(8,128)(2,1)S(1)}, bf16[96,256]{1,0:T(8,128)(2,1)S(1)}, u32[]{:S(2)}, u32[]{:S(2)}) collective-permute-start(bf16[96,256]{1,0:T(8,128)(2,1)S(1)} %get-tuple-element.55), channel_id=1, source_target_pairs={{0,8},{4,12},{8,0},{12,4},{1,9},{5,13},{9,1},{13,5},{2,10},{6,14},... | collective-permute-start | bytes 147464 | tf_op jit(solution)/shard_map/ppermute | solution.py:39
  45.2 0.0 collective-permute-done.2.refs_2_
  45.2 2.2 %collective-permute-start.13 = (bf16[96,256]{1,0:T(8,128)(2,1)S(1)}, bf16[96,256]{1,0:T(8,128)(2,1)S(1)}, u32[]{:S(2)}, u32[]{:S(2)}) collective-permute-start(bf16[96,256]{1,0:T(8,128)(2,1)S(1)} %get-tuple-element.56), channel_id=1, source_target_pairs={{0,12},{4,8},{8,4},{12,0},{1,13},{5,9},{9,5},{13,1},{2,14},{6,10},... | collective-permute-start | bytes 147464 | tf_op jit(solution)/shard_map/ppermute | solution.py:39
  47.4 0.0 collective-permute-done.1.refs_1_.refs_0_
  47.4 1.6 %attend_early.1 = (f32[384,256]{1,0:T(8,128)S(1)}, f32[384,256]{1,0:T(8,128)S(1)}, f32[384,256]{1,0:T(8,128)S(1)}) custom-call(f32[1,64]{1,0:T(1,128)S(1)} %get-tuple-element.31.bias, bf16[608,256]{1,0:T(8,128)(2,1)S(1)} %get-tuple-element.32.refs_0_, bf16[608,256]{1,0:T(8,128)(2,1)S(1)} %collective-permute-done.1.refs_1_.refs_0_, ...), custom_call_target="tpu_custom_call" | custom-call | tf_op jit(solution)/shard_map/attend_early/pallas_call | solution.py:264
  49.0 3.8 %collective-permute-done.7.refs_1_ = bf16[416,256]{1,0:T(8,128)(2,1)S(1)} collective-permute-done((bf16[416,256]{1,0:T(8,128)(2,1)S(1)}, bf16[416,256]{1,0:T(8,128)(2,1)S(1)}, u32[]{:S(2)}, u32[]{:S(2)}) %collective-permute-start.7) | collective-permute-done | bytes 213024 | tf_op jit(solution)/shard_map/ppermute | solution.py:39
  52.7 0.7 %attend_late.3 = bf16[192,256]{1,0:T(8,128)(2,1)S(1)} custom-call(f32[1,64]{1,0:T(1,128)S(1)} %get-tuple-element.31.bias, f32[384,256]{1,0:T(8,128)S(1)} %get-tuple-element.45.products, f32[384,256]{1,0:T(8,128)S(1)} %get-tuple-element.46.totals, f32[384,256]{1,0:T(8,128)S(1)} %get-tuple-element.47.peaks, ...), custom_call_target="tpu_custom_call" | custom-call | tf_op jit(solution)/shard_map/attend_late/pallas_call | solution.py:278
  53.4 1.2 %collective-permute-start.8 = (bf16[192,256]{1,0:T(8,128)(2,1)S(1)}, bf16[192,256]{1,0:T(8,128)(2,1)S(1)}, u32[]{:S(2)}, u32[]{:S(2)}) collective-permute-start(bf16[192,256]{1,0:T(8,128)(2,1)S(1)} %attend_late.3), channel_id=1, source_target_pairs={{0,4},{4,0},{8,12},{12,8},{1,5},{5,1},{9,13},{13,9},{2,6},{6,2},{1... | collective-permute-start | bytes 294920 | tf_op jit(solution)/shard_map/ppermute | solution.py:39
  54.7 0.0 collective-permute-done.11.refs_1_
  54.7 0.0 collective-permute-done.12.refs_2_
  54.7 0.0 collective-permute-done.13.refs_3_
  54.7 1.0 %collective-permute-start.14 = (bf16[96,1024]{1,0:T(8,128)(2,1)S(1)}, bf16[96,1024]{1,0:T(8,128)(2,1)S(1)}, u32[]{:S(2)}, u32[]{:S(2)}) collective-permute-start(bf16[96,1024]{1,0:T(8,128)(2,1)S(1)} %collect.1.left), channel_id=1, source_target_pairs={{0,3},{1,0},{2,1},{3,2},{4,7},{5,4},{6,5},{7,6},{8,11},{9,8},{10,9... | collective-permute-start | bytes 589832 | tf_op jit(solution)/shard_map/ppermute | solution.py:29
  55.7 0.7 %attend_late.2.refs_0_ = bf16[192,256]{1,0:T(8,128)(2,1)S(1)} custom-call(f32[1,64]{1,0:T(1,128)S(1)} %get-tuple-element.31.bias, f32[384,256]{1,0:T(8,128)S(1)} %get-tuple-element.45.products, f32[384,256]{1,0:T(8,128)S(1)} %get-tuple-element.46.totals, f32[384,256]{1,0:T(8,128)S(1)} %get-tuple-element.47.peaks, ...), custom_call_target="tpu_custom_call" | custom-call | tf_op jit(solution)/shard_map/attend_late/pallas_call | solution.py:278
  56.4 0.6 collective-permute-done.8.refs_1_
  57.0 3.3 %collective-permute-start.9 = (bf16[96,512]{1,0:T(8,128)(2,1)S(1)}, bf16[96,512]{1,0:T(8,128)(2,1)S(1)}, u32[]{:S(2)}, u32[]{:S(2)}) collective-permute-start(bf16[96,512]{1,0:T(8,128)(2,1)S(1)} %get-tuple-element.51), channel_id=1, source_target_pairs={{0,1},{1,0},{2,3},{3,2},{4,5},{5,4},{6,7},{7,6},{8,9},{9,8},{10,11... | collective-permute-start | bytes 294920 | tf_op jit(solution)/shard_map/ppermute | solution.py:35
  60.3 1.4 %collective-permute-start.10 = (bf16[96,512]{1,0:T(8,128)(2,1)S(1)}, bf16[96,512]{1,0:T(8,128)(2,1)S(1)}, u32[]{:S(2)}, u32[]{:S(2)}) collective-permute-start(bf16[96,512]{1,0:T(8,128)(2,1)S(1)} %get-tuple-element.52), channel_id=1, source_target_pairs={{0,3},{1,2},{2,1},{3,0},{4,7},{5,6},{6,5},{7,4},{8,11},{9,10},{10,... | collective-permute-start | bytes 294920 | tf_op jit(solution)/shard_map/ppermute | solution.py:35
  61.7 0.0 collective-permute-done.14.right
  61.7 1.4 %project_begin.1.refs_3_ = f32[192,3072]{1,0:T(8,128)S(1)} custom-call(bf16[96,1024]{1,0:T(8,128)(2,1)S(1)} %collect.1.left, bf16[96,1024]{1,0:T(8,128)(2,1)S(1)} %collective-permute-done.14.right, bf16[1536,3072]{1,0:T(8,128)(2,1)S(1)} %load_weights.1.refs_7_.refs_4_.weights.refs_2_), custom_call_target="tpu_custom_call" | custom-call | tf_op jit(solution)/shard_map/project_begin/pallas_call | solution.py:501
  63.1 0.0 collective-permute-done.9.first_in
  63.1 1.7 %collective-permute-done.10.second_in = bf16[96,512]{1,0:T(8,128)(2,1)S(1)} collective-permute-done((bf16[96,512]{1,0:T(8,128)(2,1)S(1)}, bf16[96,512]{1,0:T(8,128)(2,1)S(1)}, u32[]{:S(2)}, u32[]{:S(2)}) %collective-permute-start.10) | collective-permute-done | bytes 98336 | tf_op jit(solution)/shard_map/ppermute | solution.py:35
  64.8 1.6 %project_end.1 = bf16[192,3072]{1,0:T(8,128)(2,1)} custom-call(bf16[96,512]{1,0:T(8,128)(2,1)S(1)} %get-tuple-element.49.left, bf16[96,512]{1,0:T(8,128)(2,1)S(1)} %get-tuple-element.50.right, bf16[96,512]{1,0:T(8,128)(2,1)S(1)} %collective-permute-done.9.first_in, bf16[96,512]{1,0:T(8,128)(2,1)S(1)} %collective-permute-done.10.second_in, ...), custom_call_target="tpu_custom_call" | custom-call | tf_op jit(solution)/shard_map/project_end/pallas_call | solution.py:550
  (5 shorter events, 0.1 us)
Async XLA Ops:
  1.3 24.2 %collective-permute-start = (bf16[624,256]{1,0:T(8,128)(2,1)S(1)}, bf16[624,256]{1,0:T(8,128)(2,1)S(1)}, u32[]{:S(2)}, u32[]{:S(2)}) collective-permute-start(bf16[624,256]{1,0:T(8,128)(2,1)S(1)} %get-tuple-element.34), channel_id=1, source_target_pairs={{0,8},{4,12},{8,0},{12,4},{1,9},{5,13},{9,1},{13,5},{2,10},{6,14},... | collective-permute-start | bytes 958472 | tf_op jit(solution)/shard_map/ppermute | solution.py:39
  4.5 25.2 %collective-permute-start.4 = (bf16[624,256]{1,0:T(8,128)(2,1)S(1)}, bf16[624,256]{1,0:T(8,128)(2,1)S(1)}, u32[]{:S(2)}, u32[]{:S(2)}) collective-permute-start(bf16[624,256]{1,0:T(8,128)(2,1)S(1)} %get-tuple-element.37), channel_id=1, source_target_pairs={{0,12},{4,8},{8,4},{12,0},{1,13},{5,9},{9,5},{13,1},{2,14},{6,10},... | collective-permute-start | bytes 958472 | tf_op jit(solution)/shard_map/ppermute | solution.py:39
  6.7 28.8 %collective-permute-start.3 = (bf16[624,256]{1,0:T(8,128)(2,1)S(1)}, bf16[624,256]{1,0:T(8,128)(2,1)S(1)}, u32[]{:S(2)}, u32[]{:S(2)}) collective-permute-start(bf16[624,256]{1,0:T(8,128)(2,1)S(1)} %pack.3), channel_id=1, source_target_pairs={{0,4},{4,0},{8,12},{12,8},{1,5},{5,1},{9,13},{13,9},{2,6},{6,2},{1... | collective-permute-start | bytes 958472 | tf_op jit(solution)/shard_map/ppermute | solution.py:39
  7.0 3.7 %copy-start = (bf16[1536,3072]{1,0:T(8,128)(2,1)S(1)}, bf16[1536,3072]{1,0:T(8,128)(2,1)}, u32[]{:S(2)}) copy-start(bf16[1536,3072]{1,0:T(8,128)(2,1)} %w_out.1) | copy-start | bytes 28311556
  10.7 0.7 %copy-start.1 = (s32[1,192]{1,0:T(1,128)S(1)}, s32[1,192]{1,0:T(1,128)}, u32[]{:S(2)}) copy-start(s32[1,192]{1,0:T(1,128)} %refs_5_.5) | copy-start | bytes 2308
  10.7 0.7 %copy-start.2 = (s32[1,64]{1,0:T(1,128)S(1)}, s32[1,64]{1,0:T(1,128)}, u32[]{:S(2)}) copy-start(s32[1,64]{1,0:T(1,128)} %refs_6_.1) | copy-start | bytes 772
  25.6 21.8 %collective-permute-start.1 = (bf16[608,256]{1,0:T(8,128)(2,1)S(1)}, bf16[608,256]{1,0:T(8,128)(2,1)S(1)}, u32[]{:S(2)}, u32[]{:S(2)}) collective-permute-start(bf16[608,256]{1,0:T(8,128)(2,1)S(1)} %hold.3), channel_id=1, source_target_pairs={{0,4},{4,0},{8,12},{12,8},{1,5},{5,1},{9,13},{13,9},{2,6},{6,2},{1... | collective-permute-start | bytes 933896 | tf_op jit(solution)/shard_map/ppermute | solution.py:39
  26.8 18.4 %collective-permute-start.2 = (bf16[416,256]{1,0:T(8,128)(2,1)S(1)}, bf16[416,256]{1,0:T(8,128)(2,1)S(1)}, u32[]{:S(2)}, u32[]{:S(2)}) collective-permute-start(bf16[416,256]{1,0:T(8,128)(2,1)S(1)} %hold.4), channel_id=1, source_target_pairs={{0,12},{4,8},{8,4},{12,0},{1,13},{5,9},{9,5},{13,1},{2,14},{6,10},... | collective-permute-start | bytes 638984 | tf_op jit(solution)/shard_map/ppermute | solution.py:39
  29.7 23.0 %collective-permute-start.7 = (bf16[416,256]{1,0:T(8,128)(2,1)S(1)}, bf16[416,256]{1,0:T(8,128)(2,1)S(1)}, u32[]{:S(2)}, u32[]{:S(2)}) collective-permute-start(bf16[416,256]{1,0:T(8,128)(2,1)S(1)} %hold.5), channel_id=1, source_target_pairs={{0,8},{4,12},{8,0},{12,4},{1,9},{5,13},{9,1},{13,5},{2,10},{6,14},... | collective-permute-start | bytes 638984 | tf_op jit(solution)/shard_map/ppermute | solution.py:39
  39.0 3.7 %collective-permute-start.5 = (bf16[192,256]{1,0:T(8,128)(2,1)S(1)}, bf16[192,256]{1,0:T(8,128)(2,1)S(1)}, u32[]{:S(2)}, u32[]{:S(2)}) collective-permute-start(bf16[192,256]{1,0:T(8,128)(2,1)S(1)} %get-tuple-element.39), channel_id=1, source_target_pairs={{0,1},{1,2},{2,3},{3,0},{4,5},{5,6},{6,7},{7,4},{8,9},{9,10},{10,1... | collective-permute-start | bytes 294920 | tf_op jit(solution)/shard_map/ppermute | solution.py:29
  41.0 2.6 %collective-permute-start.6 = (bf16[192,256]{1,0:T(8,128)(2,1)S(1)}, bf16[192,256]{1,0:T(8,128)(2,1)S(1)}, u32[]{:S(2)}, u32[]{:S(2)}) collective-permute-start(bf16[192,256]{1,0:T(8,128)(2,1)S(1)} %get-tuple-element.42), channel_id=1, source_target_pairs={{0,1},{1,2},{2,3},{3,0},{4,5},{5,6},{6,7},{7,4},{8,9},{9,10},{10,1... | collective-permute-start | bytes 294920 | tf_op jit(solution)/shard_map/ppermute | solution.py:29
  43.8 10.9 %collective-permute-start.11 = (bf16[96,256]{1,0:T(8,128)(2,1)S(1)}, bf16[96,256]{1,0:T(8,128)(2,1)S(1)}, u32[]{:S(2)}, u32[]{:S(2)}) collective-permute-start(bf16[96,256]{1,0:T(8,128)(2,1)S(1)} %get-tuple-element.54), channel_id=1, source_target_pairs={{0,4},{4,0},{8,12},{12,8},{1,5},{5,1},{9,13},{13,9},{2,6},{6,2},{1... | collective-permute-start | bytes 147464 | tf_op jit(solution)/shard_map/ppermute | solution.py:39
  43.8 10.8 %collective-permute-start.12 = (bf16[96,256]{1,0:T(8,128)(2,1)S(1)}, bf16[96,256]{1,0:T(8,128)(2,1)S(1)}, u32[]{:S(2)}, u32[]{:S(2)}) collective-permute-start(bf16[96,256]{1,0:T(8,128)(2,1)S(1)} %get-tuple-element.55), channel_id=1, source_target_pairs={{0,8},{4,12},{8,0},{12,4},{1,9},{5,13},{9,1},{13,5},{2,10},{6,14},... | collective-permute-start | bytes 147464 | tf_op jit(solution)/shard_map/ppermute | solution.py:39
  45.2 9.5 %collective-permute-start.13 = (bf16[96,256]{1,0:T(8,128)(2,1)S(1)}, bf16[96,256]{1,0:T(8,128)(2,1)S(1)}, u32[]{:S(2)}, u32[]{:S(2)}) collective-permute-start(bf16[96,256]{1,0:T(8,128)(2,1)S(1)} %get-tuple-element.56), channel_id=1, source_target_pairs={{0,12},{4,8},{8,4},{12,0},{1,13},{5,9},{9,5},{13,1},{2,14},{6,10},... | collective-permute-start | bytes 147464 | tf_op jit(solution)/shard_map/ppermute | solution.py:39
  53.4 3.5 %collective-permute-start.8 = (bf16[192,256]{1,0:T(8,128)(2,1)S(1)}, bf16[192,256]{1,0:T(8,128)(2,1)S(1)}, u32[]{:S(2)}, u32[]{:S(2)}) collective-permute-start(bf16[192,256]{1,0:T(8,128)(2,1)S(1)} %attend_late.3), channel_id=1, source_target_pairs={{0,4},{4,0},{8,12},{12,8},{1,5},{5,1},{9,13},{13,9},{2,6},{6,2},{1... | collective-permute-start | bytes 294920 | tf_op jit(solution)/shard_map/ppermute | solution.py:39
  54.7 7.0 %collective-permute-start.14 = (bf16[96,1024]{1,0:T(8,128)(2,1)S(1)}, bf16[96,1024]{1,0:T(8,128)(2,1)S(1)}, u32[]{:S(2)}, u32[]{:S(2)}) collective-permute-start(bf16[96,1024]{1,0:T(8,128)(2,1)S(1)} %collect.1.left), channel_id=1, source_target_pairs={{0,3},{1,0},{2,1},{3,2},{4,7},{5,4},{6,5},{7,6},{8,11},{9,8},{10,9... | collective-permute-start | bytes 589832 | tf_op jit(solution)/shard_map/ppermute | solution.py:29
  57.0 6.1 %collective-permute-start.9 = (bf16[96,512]{1,0:T(8,128)(2,1)S(1)}, bf16[96,512]{1,0:T(8,128)(2,1)S(1)}, u32[]{:S(2)}, u32[]{:S(2)}) collective-permute-start(bf16[96,512]{1,0:T(8,128)(2,1)S(1)} %get-tuple-element.51), channel_id=1, source_target_pairs={{0,1},{1,0},{2,3},{3,2},{4,5},{5,4},{6,7},{7,6},{8,9},{9,8},{10,11... | collective-permute-start | bytes 294920 | tf_op jit(solution)/shard_map/ppermute | solution.py:35
  60.3 4.5 %collective-permute-start.10 = (bf16[96,512]{1,0:T(8,128)(2,1)S(1)}, bf16[96,512]{1,0:T(8,128)(2,1)S(1)}, u32[]{:S(2)}, u32[]{:S(2)}) collective-permute-start(bf16[96,512]{1,0:T(8,128)(2,1)S(1)} %get-tuple-element.52), channel_id=1, source_target_pairs={{0,3},{1,2},{2,1},{3,0},{4,7},{5,6},{6,5},{7,4},{8,11},{9,10},{10,... | collective-permute-start | bytes 294920 | tf_op jit(solution)/shard_map/ppermute | solution.py:35

commit v7 on v6

--- a/solution.py
+++ b/solution.py
@@ -655,7 +655,7 @@
     first = received
     second = [packed[0]] + [swapped(hold(packed[d], [first[halfway]]), d) for d in near]
     for distance in far:
-        second.append(swapped(hold(packed[distance], first[halfway:] if distance == halfway else first[halfway : halfway + 1]), distance))
+        second.append(swapped(hold(packed[distance], first[halfway:] if distance == halfway else []), distance))
     blend_weights = weigh(first, message_rows, image_rows)
 
     def strips_of(blocks):

time: 66.7 us -> 66.7 us (level)
  no operation moved by 1% of the time
where the time goes in v7:
time: 66.7 us; the launch traced here: 66.4 us
  starting transfers between devices  27.1 us (41%)
  waiting for transfers between devices  20.1 us (30%)
  Pallas kernels  15.2 us (23%)
  local copies, waits for them, and re-layouts  3.72 us (6%)
    ppermute x10, starting transfers between devices, swapped(): lax.ppermute(block, 'seq', [(i, i ^ distance) for i in range(lax.axis_siz...  19.4 us
    ppermute x10, waiting for transfers between devices, swapped(): lax.ppermute(block, 'seq', [(i, i ^ distance) for i in range(lax.axis_siz...  16.7 us
    ppermute x2, starting transfers between devices, paired(): lax.ppermute(block, 'win', [(i, (i + step[i % 2]) % count) for i in range...  4.67 us
    unnamed x6, local copies, waits for them, and re-layouts  3.72 us
    pallas_call x1, Pallas kernels, attend(): pl.pallas_call(functools.partial(attend_kernel, group, image_rows, text_r...  3.42 us
    ppermute x3, starting transfers between devices, shifted(): lax.ppermute(block, axis, [(i, (i + distance) % count) for i in range(cou...  3.09 us
    pallas_call x2, Pallas kernels, pack(): pl.pallas_call(functools.partial(pack_kernel, heads, group, distances, le...  2.43 us
    pallas_call x1, Pallas kernels, prepare(): pl.pallas_call(functools.partial(prepare_kernel, heads, group, len(source...  1.74 us
  transfers between devices with their start and end apart: 15, of which 6 were waited for; matrix products, arithmetic and copies ran while one was open for 0% of the time, Pallas kernels for 19%

profile of v7, /device:TPU:1, one launch (start us, length us, event | category | flops | bytes accessed | tf_op | source)
XLA Modules:
  0.0 66.4 jit_solution(9452076227279491892)
XLA Ops:
  0.0 1.3 %pack.2 = (bf16[624,256]{1,0:T(8,128)(2,1)S(1)}, bf16[624,256]{1,0:T(8,128)(2,1)S(1)}) custom-call(bf16[192,1536]{1,0:T(8,128)(2,1)} %bitcast.6, bf16[192,1536]{1,0:T(8,128)(2,1)} %bitcast.9, bf16[16,1536]{1,0:T(8,128)(2,1)} %bitcast.15, bf16[192,1536]{1,0:T(8,128)(2,1)} %bitcast.12, bf16[16,1536]{1,0:T(8,128)(2,1)} %bitcast.18, s32[1,192]{1,0:T(1,128)} %refs_5_.5), custom_call_target="tpu_custom_call" | custom-call | tf_op jit(solution)/shard_map/pack/pallas_call | solution.py:108
  1.3 3.2 %collective-permute-start = (bf16[624,256]{1,0:T(8,128)(2,1)S(1)}, bf16[624,256]{1,0:T(8,128)(2,1)S(1)}, u32[]{:S(2)}, u32[]{:S(2)}) collective-permute-start(bf16[624,256]{1,0:T(8,128)(2,1)S(1)} %get-tuple-element.34), channel_id=1, source_target_pairs={{0,8},{4,12},{8,0},{12,4},{1,9},{5,13},{9,1},{13,5},{2,10},{6,14},... | collective-permute-start | bytes 958472 | tf_op jit(solution)/shard_map/ppermute | solution.py:39
  4.5 1.1 %collective-permute-start.4 = (bf16[624,256]{1,0:T(8,128)(2,1)S(1)}, bf16[624,256]{1,0:T(8,128)(2,1)S(1)}, u32[]{:S(2)}, u32[]{:S(2)}) collective-permute-start(bf16[624,256]{1,0:T(8,128)(2,1)S(1)} %get-tuple-element.37), channel_id=1, source_target_pairs={{0,12},{4,8},{8,4},{12,0},{1,13},{5,9},{9,5},{13,1},{2,14},{6,10},... | collective-permute-start | bytes 958472 | tf_op jit(solution)/shard_map/ppermute | solution.py:39
  5.6 1.1 %pack.3 = bf16[624,256]{1,0:T(8,128)(2,1)S(1)} custom-call(bf16[192,1536]{1,0:T(8,128)(2,1)} %bitcast.7, bf16[192,1536]{1,0:T(8,128)(2,1)} %bitcast.10, bf16[16,1536]{1,0:T(8,128)(2,1)} %bitcast.16, bf16[192,1536]{1,0:T(8,128)(2,1)} %bitcast.13, bf16[16,1536]{1,0:T(8,128)(2,1)} %bitcast.19, s32[1,192]{1,0:T(1,128)} %refs_5_.5), custom_call_target="tpu_custom_call" | custom-call | tf_op jit(solution)/shard_map/pack/pallas_call | solution.py:108
  6.7 0.3 collective-permute-start.3
  7.0 0.0 copy-start
  7.0 3.7 %copy-done = bf16[1536,3072]{1,0:T(8,128)(2,1)S(1)} copy-done((bf16[1536,3072]{1,0:T(8,128)(2,1)S(1)}, bf16[1536,3072]{1,0:T(8,128)(2,1)}, u32[]{:S(2)}) %copy-start) | copy-done | bytes 9437208
  10.7 0.0 copy-start.1
  10.7 0.0 copy-start.2
  10.7 0.6 load_weights.1.refs_7_.refs_4_.weights.refs_2_
  11.3 0.0 copy-done.1
  11.4 0.0 copy-done.2
  11.4 1.7 %prepare.1 = (bf16[624,256]{1,0:T(8,128)(2,1)S(1)}, bf16[608,256]{1,0:T(8,128)(2,1)S(1)}, bf16[608,256]{1,0:T(8,128)(2,1)S(1)}, bf16[416,256]{1,0:T(8,128)(2,1)S...) custom-call(bf16[192,1536]{1,0:T(8,128)(2,1)} %bitcast.8, bf16[192,1536]{1,0:T(8,128)(2,1)} %bitcast.11, ...), custom_call_target="tpu_custom_call" | custom-call | tf_op jit(solution)/shard_map/prepare/pallas_call | solution.py:147
  13.1 12.4 %collective-permute-done.refs_0_.refs_2_ = bf16[624,256]{1,0:T(8,128)(2,1)S(1)} collective-permute-done((bf16[624,256]{1,0:T(8,128)(2,1)S(1)}, bf16[624,256]{1,0:T(8,128)(2,1)S(1)}, u32[]{:S(2)}, u32[]{:S(2)}) %collective-permute-start) | collective-permute-done | bytes 319520 | tf_op jit(solution)/shard_map/ppermute | solution.py:39
  25.6 1.2 %collective-permute-start.1 = (bf16[608,256]{1,0:T(8,128)(2,1)S(1)}, bf16[608,256]{1,0:T(8,128)(2,1)S(1)}, u32[]{:S(2)}, u32[]{:S(2)}) collective-permute-start(bf16[608,256]{1,0:T(8,128)(2,1)S(1)} %hold.3), channel_id=1, source_target_pairs={{0,4},{4,0},{8,12},{12,8},{1,5},{5,1},{9,13},{13,9},{2,6},{6,2},{1... | collective-permute-start | bytes 933896 | tf_op jit(solution)/shard_map/ppermute | solution.py:39
  26.8 2.9 %collective-permute-start.2 = (bf16[416,256]{1,0:T(8,128)(2,1)S(1)}, bf16[416,256]{1,0:T(8,128)(2,1)S(1)}, u32[]{:S(2)}, u32[]{:S(2)}) collective-permute-start(bf16[416,256]{1,0:T(8,128)(2,1)S(1)} %hold.4), channel_id=1, source_target_pairs={{0,12},{4,8},{8,4},{12,0},{1,13},{5,9},{9,5},{13,1},{2,14},{6,10},... | collective-permute-start | bytes 638984 | tf_op jit(solution)/shard_map/ppermute | solution.py:39
  29.7 0.0 collective-permute-done.4.refs_3_.refs_1_
  29.7 5.8 %collective-permute-start.7 = (bf16[416,256]{1,0:T(8,128)(2,1)S(1)}, bf16[416,256]{1,0:T(8,128)(2,1)S(1)}, u32[]{:S(2)}, u32[]{:S(2)}) collective-permute-start(bf16[416,256]{1,0:T(8,128)(2,1)S(1)} %hold.5), channel_id=1, source_target_pairs={{0,8},{4,12},{8,0},{12,4},{1,9},{5,13},{9,1},{13,5},{2,10},{6,14},... | collective-permute-start | bytes 638984 | tf_op jit(solution)/shard_map/ppermute | solution.py:39
  35.6 0.0 collective-permute-done.3.refs_1_
  35.6 3.4 %attend.1 = (bf16[192,256]{1,0:T(8,128)(2,1)S(1)}, bf16[192,256]{1,0:T(8,128)(2,1)S(1)}, bf16[192,256]{1,0:T(8,128)(2,1)S(1)}, bf16[192,256]{1,0:T(8,128)(2,1)S(1)}) custom-call(f32[1,64]{1,0:T(1,128)S(1)} %get-tuple-element.31.bias, bf16[624,256]{1,0:T(8,128)(2,1)S(1)} %get-tuple-element.36.refs_0_, bf16[624,256]{1,0:T(8,128)(2,1)S(1)} %collective-permute-done.3.refs_1_, ...), custom_call_target="tpu_custom_call" | custom-call | tf_op jit(solution)/shard_map/attend/pallas_call | solution.py:353
  39.0 2.1 %collective-permute-start.5 = (bf16[192,256]{1,0:T(8,128)(2,1)S(1)}, bf16[192,256]{1,0:T(8,128)(2,1)S(1)}, u32[]{:S(2)}, u32[]{:S(2)}) collective-permute-start(bf16[192,256]{1,0:T(8,128)(2,1)S(1)} %get-tuple-element.39), channel_id=1, source_target_pairs={{0,1},{1,2},{2,3},{3,0},{4,5},{5,6},{6,7},{7,4},{8,9},{9,10},{10,1... | collective-permute-start | bytes 294920 | tf_op jit(solution)/shard_map/ppermute | solution.py:29
  41.0 0.1 collective-permute-start.6
  41.1 0.8 %weigh.1 = (f32[192,128]{1,0:T(8,128)S(1)}, f32[192,128]{1,0:T(8,128)S(1)}, f32[192,128]{1,0:T(8,128)S(1)}, f32[192,128]{1,0:T(8,128)}) custom-call(bf16[624,256]{1,0:T(8,128)(2,1)S(1)} %get-tuple-element.36.refs_0_, bf16[624,256]{1,0:T(8,128)(2,1)S(1)} %collective-permute-done.3.refs_1_, bf16[624,256]{1,0:T(8,128)(2,1)S(1)} %collective-permute-done.refs_0_.refs_2_, ...), custom_call_target="tpu_custom_call" | custom-call | tf_op jit(solution)/shard_map/weigh/pallas_call | solution.py:385
  42.0 0.7 %collective-permute-done.5.refs_1_ = bf16[192,256]{1,0:T(8,128)(2,1)S(1)} collective-permute-done((bf16[192,256]{1,0:T(8,128)(2,1)S(1)}, bf16[192,256]{1,0:T(8,128)(2,1)S(1)}, u32[]{:S(2)}, u32[]{:S(2)}) %collective-permute-start.5) | collective-permute-done | bytes 98336 | tf_op jit(solution)/shard_map/ppermute | solution.py:29
  42.7 1.0 %collective-permute-done.6.refs_4_ = bf16[192,256]{1,0:T(8,128)(2,1)S(1)} collective-permute-done((bf16[192,256]{1,0:T(8,128)(2,1)S(1)}, bf16[192,256]{1,0:T(8,128)(2,1)S(1)}, u32[]{:S(2)}, u32[]{:S(2)}) %collective-permute-start.6) | collective-permute-done | bytes 98336 | tf_op jit(solution)/shard_map/ppermute | solution.py:29
  43.7 0.1 blend.1
  43.8 0.1 collective-permute-start.11
  43.8 1.3 %collective-permute-start.12 = (bf16[96,256]{1,0:T(8,128)(2,1)S(1)}, bf16[96,256]{1,0:T(8,128)(2,1)S(1)}, u32[]{:S(2)}, u32[]{:S(2)}) collective-permute-start(bf16[96,256]{1,0:T(8,128)(2,1)S(1)} %get-tuple-element.55), channel_id=1, source_target_pairs={{0,8},{4,12},{8,0},{12,4},{1,9},{5,13},{9,1},{13,5},{2,10},{6,14},... | collective-permute-start | bytes 147464 | tf_op jit(solution)/shard_map/ppermute | solution.py:39
  45.2 0.0 collective-permute-done.2.refs_2_
  45.2 2.2 %collective-permute-start.13 = (bf16[96,256]{1,0:T(8,128)(2,1)S(1)}, bf16[96,256]{1,0:T(8,128)(2,1)S(1)}, u32[]{:S(2)}, u32[]{:S(2)}) collective-permute-start(bf16[96,256]{1,0:T(8,128)(2,1)S(1)} %get-tuple-element.56), channel_id=1, source_target_pairs={{0,12},{4,8},{8,4},{12,0},{1,13},{5,9},{9,5},{13,1},{2,14},{6,10},... | collective-permute-start | bytes 147464 | tf_op jit(solution)/shard_map/ppermute | solution.py:39
  47.4 0.0 collective-permute-done.1.refs_1_.refs_0_
  47.4 1.6 %attend_early.1 = (f32[384,256]{1,0:T(8,128)S(1)}, f32[384,256]{1,0:T(8,128)S(1)}, f32[384,256]{1,0:T(8,128)S(1)}) custom-call(f32[1,64]{1,0:T(1,128)S(1)} %get-tuple-element.31.bias, bf16[608,256]{1,0:T(8,128)(2,1)S(1)} %get-tuple-element.32.refs_0_, bf16[608,256]{1,0:T(8,128)(2,1)S(1)} %collective-permute-done.1.refs_1_.refs_0_, ...), custom_call_target="tpu_custom_call" | custom-call | tf_op jit(solution)/shard_map/attend_early/pallas_call | solution.py:264
  49.0 3.8 %collective-permute-done.7.refs_1_ = bf16[416,256]{1,0:T(8,128)(2,1)S(1)} collective-permute-done((bf16[416,256]{1,0:T(8,128)(2,1)S(1)}, bf16[416,256]{1,0:T(8,128)(2,1)S(1)}, u32[]{:S(2)}, u32[]{:S(2)}) %collective-permute-start.7) | collective-permute-done | bytes 213024 | tf_op jit(solution)/shard_map/ppermute | solution.py:39
  52.7 0.7 %attend_late.3 = bf16[192,256]{1,0:T(8,128)(2,1)S(1)} custom-call(f32[1,64]{1,0:T(1,128)S(1)} %get-tuple-element.31.bias, f32[384,256]{1,0:T(8,128)S(1)} %get-tuple-element.45.products, f32[384,256]{1,0:T(8,128)S(1)} %get-tuple-element.46.totals, f32[384,256]{1,0:T(8,128)S(1)} %get-tuple-element.47.peaks, ...), custom_call_target="tpu_custom_call" | custom-call | tf_op jit(solution)/shard_map/attend_late/pallas_call | solution.py:278
  53.4 1.2 %collective-permute-start.8 = (bf16[192,256]{1,0:T(8,128)(2,1)S(1)}, bf16[192,256]{1,0:T(8,128)(2,1)S(1)}, u32[]{:S(2)}, u32[]{:S(2)}) collective-permute-start(bf16[192,256]{1,0:T(8,128)(2,1)S(1)} %attend_late.3), channel_id=1, source_target_pairs={{0,4},{4,0},{8,12},{12,8},{1,5},{5,1},{9,13},{13,9},{2,6},{6,2},{1... | collective-permute-start | bytes 294920 | tf_op jit(solution)/shard_map/ppermute | solution.py:39
  54.7 0.0 collective-permute-done.11.refs_1_
  54.7 0.0 collective-permute-done.12.refs_2_
  54.7 0.0 collective-permute-done.13.refs_3_
  54.7 1.0 %collective-permute-start.14 = (bf16[96,1024]{1,0:T(8,128)(2,1)S(1)}, bf16[96,1024]{1,0:T(8,128)(2,1)S(1)}, u32[]{:S(2)}, u32[]{:S(2)}) collective-permute-start(bf16[96,1024]{1,0:T(8,128)(2,1)S(1)} %collect.1.left), channel_id=1, source_target_pairs={{0,3},{1,0},{2,1},{3,2},{4,7},{5,4},{6,5},{7,6},{8,11},{9,8},{10,9... | collective-permute-start | bytes 589832 | tf_op jit(solution)/shard_map/ppermute | solution.py:29
  55.7 0.7 %attend_late.2.refs_0_ = bf16[192,256]{1,0:T(8,128)(2,1)S(1)} custom-call(f32[1,64]{1,0:T(1,128)S(1)} %get-tuple-element.31.bias, f32[384,256]{1,0:T(8,128)S(1)} %get-tuple-element.45.products, f32[384,256]{1,0:T(8,128)S(1)} %get-tuple-element.46.totals, f32[384,256]{1,0:T(8,128)S(1)} %get-tuple-element.47.peaks, ...), custom_call_target="tpu_custom_call" | custom-call | tf_op jit(solution)/shard_map/attend_late/pallas_call | solution.py:278
  56.4 0.6 collective-permute-done.8.refs_1_
  57.0 3.3 %collective-permute-start.9 = (bf16[96,512]{1,0:T(8,128)(2,1)S(1)}, bf16[96,512]{1,0:T(8,128)(2,1)S(1)}, u32[]{:S(2)}, u32[]{:S(2)}) collective-permute-start(bf16[96,512]{1,0:T(8,128)(2,1)S(1)} %get-tuple-element.51), channel_id=1, source_target_pairs={{0,1},{1,0},{2,3},{3,2},{4,5},{5,4},{6,7},{7,6},{8,9},{9,8},{10,11... | collective-permute-start | bytes 294920 | tf_op jit(solution)/shard_map/ppermute | solution.py:35
  60.3 1.4 %collective-permute-start.10 = (bf16[96,512]{1,0:T(8,128)(2,1)S(1)}, bf16[96,512]{1,0:T(8,128)(2,1)S(1)}, u32[]{:S(2)}, u32[]{:S(2)}) collective-permute-start(bf16[96,512]{1,0:T(8,128)(2,1)S(1)} %get-tuple-element.52), channel_id=1, source_target_pairs={{0,3},{1,2},{2,1},{3,0},{4,7},{5,6},{6,5},{7,4},{8,11},{9,10},{10,... | collective-permute-start | bytes 294920 | tf_op jit(solution)/shard_map/ppermute | solution.py:35
  61.7 0.0 collective-permute-done.14.right
  61.7 1.4 %project_begin.1.refs_3_ = f32[192,3072]{1,0:T(8,128)S(1)} custom-call(bf16[96,1024]{1,0:T(8,128)(2,1)S(1)} %collect.1.left, bf16[96,1024]{1,0:T(8,128)(2,1)S(1)} %collective-permute-done.14.right, bf16[1536,3072]{1,0:T(8,128)(2,1)S(1)} %load_weights.1.refs_7_.refs_4_.weights.refs_2_), custom_call_target="tpu_custom_call" | custom-call | tf_op jit(solution)/shard_map/project_begin/pallas_call | solution.py:501
  63.1 0.0 collective-permute-done.9.first_in
  63.1 1.7 %collective-permute-done.10.second_in = bf16[96,512]{1,0:T(8,128)(2,1)S(1)} collective-permute-done((bf16[96,512]{1,0:T(8,128)(2,1)S(1)}, bf16[96,512]{1,0:T(8,128)(2,1)S(1)}, u32[]{:S(2)}, u32[]{:S(2)}) %collective-permute-start.10) | collective-permute-done | bytes 98336 | tf_op jit(solution)/shard_map/ppermute | solution.py:35
  64.8 1.6 %project_end.1 = bf16[192,3072]{1,0:T(8,128)(2,1)} custom-call(bf16[96,512]{1,0:T(8,128)(2,1)S(1)} %get-tuple-element.49.left, bf16[96,512]{1,0:T(8,128)(2,1)S(1)} %get-tuple-element.50.right, bf16[96,512]{1,0:T(8,128)(2,1)S(1)} %collective-permute-done.9.first_in, bf16[96,512]{1,0:T(8,128)(2,1)S(1)} %collective-permute-done.10.second_in, ...), custom_call_target="tpu_custom_call" | custom-call | tf_op jit(solution)/shard_map/project_end/pallas_call | solution.py:550
  (5 shorter events, 0.1 us)
Async XLA Ops:
  1.3 24.2 %collective-permute-start = (bf16[624,256]{1,0:T(8,128)(2,1)S(1)}, bf16[624,256]{1,0:T(8,128)(2,1)S(1)}, u32[]{:S(2)}, u32[]{:S(2)}) collective-permute-start(bf16[624,256]{1,0:T(8,128)(2,1)S(1)} %get-tuple-element.34), channel_id=1, source_target_pairs={{0,8},{4,12},{8,0},{12,4},{1,9},{5,13},{9,1},{13,5},{2,10},{6,14},... | collective-permute-start | bytes 958472 | tf_op jit(solution)/shard_map/ppermute | solution.py:39
  4.5 25.2 %collective-permute-start.4 = (bf16[624,256]{1,0:T(8,128)(2,1)S(1)}, bf16[624,256]{1,0:T(8,128)(2,1)S(1)}, u32[]{:S(2)}, u32[]{:S(2)}) collective-permute-start(bf16[624,256]{1,0:T(8,128)(2,1)S(1)} %get-tuple-element.37), channel_id=1, source_target_pairs={{0,12},{4,8},{8,4},{12,0},{1,13},{5,9},{9,5},{13,1},{2,14},{6,10},... | collective-permute-start | bytes 958472 | tf_op jit(solution)/shard_map/ppermute | solution.py:39
  6.7 28.8 %collective-permute-start.3 = (bf16[624,256]{1,0:T(8,128)(2,1)S(1)}, bf16[624,256]{1,0:T(8,128)(2,1)S(1)}, u32[]{:S(2)}, u32[]{:S(2)}) collective-permute-start(bf16[624,256]{1,0:T(8,128)(2,1)S(1)} %pack.3), channel_id=1, source_target_pairs={{0,4},{4,0},{8,12},{12,8},{1,5},{5,1},{9,13},{13,9},{2,6},{6,2},{1... | collective-permute-start | bytes 958472 | tf_op jit(solution)/shard_map/ppermute | solution.py:39
  7.0 3.7 %copy-start = (bf16[1536,3072]{1,0:T(8,128)(2,1)S(1)}, bf16[1536,3072]{1,0:T(8,128)(2,1)}, u32[]{:S(2)}) copy-start(bf16[1536,3072]{1,0:T(8,128)(2,1)} %w_out.1) | copy-start | bytes 28311556
  10.7 0.7 %copy-start.1 = (s32[1,192]{1,0:T(1,128)S(1)}, s32[1,192]{1,0:T(1,128)}, u32[]{:S(2)}) copy-start(s32[1,192]{1,0:T(1,128)} %refs_5_.5) | copy-start | bytes 2308
  10.7 0.7 %copy-start.2 = (s32[1,64]{1,0:T(1,128)S(1)}, s32[1,64]{1,0:T(1,128)}, u32[]{:S(2)}) copy-start(s32[1,64]{1,0:T(1,128)} %refs_6_.1) | copy-start | bytes 772
  25.6 21.8 %collective-permute-start.1 = (bf16[608,256]{1,0:T(8,128)(2,1)S(1)}, bf16[608,256]{1,0:T(8,128)(2,1)S(1)}, u32[]{:S(2)}, u32[]{:S(2)}) collective-permute-start(bf16[608,256]{1,0:T(8,128)(2,1)S(1)} %hold.3), channel_id=1, source_target_pairs={{0,4},{4,0},{8,12},{12,8},{1,5},{5,1},{9,13},{13,9},{2,6},{6,2},{1... | collective-permute-start | bytes 933896 | tf_op jit(solution)/shard_map/ppermute | solution.py:39
  26.8 18.4 %collective-permute-start.2 = (bf16[416,256]{1,0:T(8,128)(2,1)S(1)}, bf16[416,256]{1,0:T(8,128)(2,1)S(1)}, u32[]{:S(2)}, u32[]{:S(2)}) collective-permute-start(bf16[416,256]{1,0:T(8,128)(2,1)S(1)} %hold.4), channel_id=1, source_target_pairs={{0,12},{4,8},{8,4},{12,0},{1,13},{5,9},{9,5},{13,1},{2,14},{6,10},... | collective-permute-start | bytes 638984 | tf_op jit(solution)/shard_map/ppermute | solution.py:39
  29.7 23.0 %collective-permute-start.7 = (bf16[416,256]{1,0:T(8,128)(2,1)S(1)}, bf16[416,256]{1,0:T(8,128)(2,1)S(1)}, u32[]{:S(2)}, u32[]{:S(2)}) collective-permute-start(bf16[416,256]{1,0:T(8,128)(2,1)S(1)} %hold.5), channel_id=1, source_target_pairs={{0,8},{4,12},{8,0},{12,4},{1,9},{5,13},{9,1},{13,5},{2,10},{6,14},... | collective-permute-start | bytes 638984 | tf_op jit(solution)/shard_map/ppermute | solution.py:39
  39.0 3.7 %collective-permute-start.5 = (bf16[192,256]{1,0:T(8,128)(2,1)S(1)}, bf16[192,256]{1,0:T(8,128)(2,1)S(1)}, u32[]{:S(2)}, u32[]{:S(2)}) collective-permute-start(bf16[192,256]{1,0:T(8,128)(2,1)S(1)} %get-tuple-element.39), channel_id=1, source_target_pairs={{0,1},{1,2},{2,3},{3,0},{4,5},{5,6},{6,7},{7,4},{8,9},{9,10},{10,1... | collective-permute-start | bytes 294920 | tf_op jit(solution)/shard_map/ppermute | solution.py:29
  41.0 2.6 %collective-permute-start.6 = (bf16[192,256]{1,0:T(8,128)(2,1)S(1)}, bf16[192,256]{1,0:T(8,128)(2,1)S(1)}, u32[]{:S(2)}, u32[]{:S(2)}) collective-permute-start(bf16[192,256]{1,0:T(8,128)(2,1)S(1)} %get-tuple-element.42), channel_id=1, source_target_pairs={{0,1},{1,2},{2,3},{3,0},{4,5},{5,6},{6,7},{7,4},{8,9},{9,10},{10,1... | collective-permute-start | bytes 294920 | tf_op jit(solution)/shard_map/ppermute | solution.py:29
  43.8 10.9 %collective-permute-start.11 = (bf16[96,256]{1,0:T(8,128)(2,1)S(1)}, bf16[96,256]{1,0:T(8,128)(2,1)S(1)}, u32[]{:S(2)}, u32[]{:S(2)}) collective-permute-start(bf16[96,256]{1,0:T(8,128)(2,1)S(1)} %get-tuple-element.54), channel_id=1, source_target_pairs={{0,4},{4,0},{8,12},{12,8},{1,5},{5,1},{9,13},{13,9},{2,6},{6,2},{1... | collective-permute-start | bytes 147464 | tf_op jit(solution)/shard_map/ppermute | solution.py:39
  43.8 10.8 %collective-permute-start.12 = (bf16[96,256]{1,0:T(8,128)(2,1)S(1)}, bf16[96,256]{1,0:T(8,128)(2,1)S(1)}, u32[]{:S(2)}, u32[]{:S(2)}) collective-permute-start(bf16[96,256]{1,0:T(8,128)(2,1)S(1)} %get-tuple-element.55), channel_id=1, source_target_pairs={{0,8},{4,12},{8,0},{12,4},{1,9},{5,13},{9,1},{13,5},{2,10},{6,14},... | collective-permute-start | bytes 147464 | tf_op jit(solution)/shard_map/ppermute | solution.py:39
  45.2 9.5 %collective-permute-start.13 = (bf16[96,256]{1,0:T(8,128)(2,1)S(1)}, bf16[96,256]{1,0:T(8,128)(2,1)S(1)}, u32[]{:S(2)}, u32[]{:S(2)}) collective-permute-start(bf16[96,256]{1,0:T(8,128)(2,1)S(1)} %get-tuple-element.56), channel_id=1, source_target_pairs={{0,12},{4,8},{8,4},{12,0},{1,13},{5,9},{9,5},{13,1},{2,14},{6,10},... | collective-permute-start | bytes 147464 | tf_op jit(solution)/shard_map/ppermute | solution.py:39
  53.4 3.5 %collective-permute-start.8 = (bf16[192,256]{1,0:T(8,128)(2,1)S(1)}, bf16[192,256]{1,0:T(8,128)(2,1)S(1)}, u32[]{:S(2)}, u32[]{:S(2)}) collective-permute-start(bf16[192,256]{1,0:T(8,128)(2,1)S(1)} %attend_late.3), channel_id=1, source_target_pairs={{0,4},{4,0},{8,12},{12,8},{1,5},{5,1},{9,13},{13,9},{2,6},{6,2},{1... | collective-permute-start | bytes 294920 | tf_op jit(solution)/shard_map/ppermute | solution.py:39
  54.7 7.0 %collective-permute-start.14 = (bf16[96,1024]{1,0:T(8,128)(2,1)S(1)}, bf16[96,1024]{1,0:T(8,128)(2,1)S(1)}, u32[]{:S(2)}, u32[]{:S(2)}) collective-permute-start(bf16[96,1024]{1,0:T(8,128)(2,1)S(1)} %collect.1.left), channel_id=1, source_target_pairs={{0,3},{1,0},{2,1},{3,2},{4,7},{5,4},{6,5},{7,6},{8,11},{9,8},{10,9... | collective-permute-start | bytes 589832 | tf_op jit(solution)/shard_map/ppermute | solution.py:29
  57.0 6.1 %collective-permute-start.9 = (bf16[96,512]{1,0:T(8,128)(2,1)S(1)}, bf16[96,512]{1,0:T(8,128)(2,1)S(1)}, u32[]{:S(2)}, u32[]{:S(2)}) collective-permute-start(bf16[96,512]{1,0:T(8,128)(2,1)S(1)} %get-tuple-element.51), channel_id=1, source_target_pairs={{0,1},{1,0},{2,3},{3,2},{4,5},{5,4},{6,7},{7,6},{8,9},{9,8},{10,11... | collective-permute-start | bytes 294920 | tf_op jit(solution)/shard_map/ppermute | solution.py:35
  60.3 4.5 %collective-permute-start.10 = (bf16[96,512]{1,0:T(8,128)(2,1)S(1)}, bf16[96,512]{1,0:T(8,128)(2,1)S(1)}, u32[]{:S(2)}, u32[]{:S(2)}) collective-permute-start(bf16[96,512]{1,0:T(8,128)(2,1)S(1)} %get-tuple-element.52), channel_id=1, source_target_pairs={{0,3},{1,2},{2,1},{3,0},{4,7},{5,6},{6,5},{7,4},{8,11},{9,10},{10,... | collective-permute-start | bytes 294920 | tf_op jit(solution)/shard_map/ppermute | solution.py:35
